TPU v7x, 256 devices: a whole 4x4x8 slice. The times are simulated.
256 devices in a mesh: span: 32 (over x_hi, z, core), seq: 8 (over y, x_lo).
Axes of the slice: x: 4 (x_hi: 2, x_lo: 2; x = x_hi * 2 + x_lo), y: 4, z: 8, core: 2. Of those that a mesh axis runs over, the one named last changes fastest.
Arguments:
- tokens: bfloat16 [65536, 1024], P(('span', 'seq')), may hold values from -48 to 48
- w_qkv: bfloat16 [1024, 3072], P('span'), may hold values from -0.1875 to 0.1875
- w_out: bfloat16 [1024, 1024], replicated, may hold values from -0.1875 to 0.1875
- w_cross: bfloat16 [1024, 2048], replicated, may hold values from -0.1875 to 0.1875
- ln_gain: float32 [1024], replicated, may hold values from 0.5 to 1.5
- ln_bias: float32 [1024], replicated, may hold values from -3 to 3
- queries: bfloat16 [1024, 1024], replicated, may hold values from -144 to 144
Outputs:
- encoded: bfloat16 [65536, 1024], P(('span', 'seq'))
- cross_out: bfloat16 [1024, 1024], P('span')
All inputs are finite; a program needn't handle non-finite values.
Results may differ from a plain program's by a relative error of at most 0.013.
The roundings to bfloat16 on the way count: a program that leaves them out, or rounds other values in their place, can miss the bound.
Values may be sent and summed in bfloat16 or wider, within the bound.
No kernel may reach another device: no remote copies, remote signals or barrier semaphores. Data moves between devices by JAX's collectives and lax.ppermute only.
A program may use at most 128 MiB of HBM per device.

v0:
```python
import jax
import jax.numpy as jnp
from jax import lax
from jax.sharding import PartitionSpec as P

H = 16
DH = 64


score_scale = 0.125


def layer_norm(residual, ln_gain, ln_bias):
    center = residual - jnp.mean(residual, -1, keepdims=True)
    spread = jnp.mean(center * center, -1, keepdims=True)
    return center * lax.rsqrt(spread + 1e-05) * ln_gain + ln_bias


def per_device(tokens, w_qkv, w_out, w_cross, ln_gain, ln_bias, queries):
    tok_rows = tokens.shape[0]
    model_width = tokens.shape[1]
    seq_count = lax.axis_size("seq")
    span_count = lax.axis_size("span")
    projected = jnp.dot(
        tokens,
        lax.all_gather(w_qkv, "span", axis=0, tiled=True),
        preferred_element_type=jnp.float32,
    )
    projected = projected.astype(jnp.bfloat16).reshape(tok_rows, 3, model_width)
    grouped = lax.all_to_all(projected, "seq", split_axis=2, concat_axis=0, tiled=True)
    span_length = tok_rows * seq_count
    heads_here = grouped.shape[2] // DH
    query_all = grouped[:, 0].reshape(span_length, heads_here, DH)
    key_all = grouped[:, 1].reshape(span_length, heads_here, DH)
    value_all = grouped[:, 2].reshape(span_length, heads_here, DH)
    block_rows = min(512, span_length)
    query_blocks = query_all.reshape(span_length // block_rows, block_rows, heads_here, DH)

    def attend(query_block):
        scores = (
            jnp.einsum("qhd,khd->hqk", query_block, key_all, preferred_element_type=jnp.float32)
            * score_scale
        )
        peaks = jnp.max(scores, -1, keepdims=True)
        powers = jnp.exp(scores - peaks)
        totals = jnp.sum(powers, -1, keepdims=True)
        mixed = jnp.einsum(
            "hqk,khd->qhd",
            powers.astype(jnp.bfloat16),
            value_all,
            preferred_element_type=jnp.float32,
        )
        mixed = mixed / jnp.transpose(totals, (1, 0, 2))
        return mixed.astype(jnp.bfloat16).reshape(block_rows, heads_here * DH)

    attn = lax.map(attend, query_blocks).reshape(span_length, heads_here * DH)
    attn_tokens = lax.all_to_all(attn, "seq", split_axis=0, concat_axis=1, tiled=True)
    residual = tokens.astype(jnp.float32) + jnp.dot(
        attn_tokens, w_out, preferred_element_type=jnp.float32
    )
    encoded = layer_norm(residual, ln_gain, ln_bias).astype(jnp.bfloat16)
    cross_kv = jnp.dot(encoded, w_cross, preferred_element_type=jnp.float32).astype(jnp.bfloat16)
    cross_keys = cross_kv[:, :model_width].reshape(tok_rows, H, DH)
    cross_values = cross_kv[:, model_width:].reshape(tok_rows, H, DH)
    query_count = queries.shape[0]
    query_heads = queries.reshape(query_count, H, DH)
    cross_scores = (
        jnp.einsum("qhd,khd->qhk", query_heads, cross_keys, preferred_element_type=jnp.float32)
        * score_scale
    )
    local_peak = jnp.max(cross_scores, -1)
    cross_peak = lax.pmax(local_peak, ("span", "seq"))
    cross_powers = jnp.exp(cross_scores - cross_peak[:, :, None])
    cross_total = jnp.sum(cross_powers, -1)
    numerator = jnp.einsum(
        "qhk,khd->qhd",
        cross_powers.astype(jnp.bfloat16),
        cross_values,
        preferred_element_type=jnp.float32,
    )
    numerator = numerator.reshape(query_count, model_width)
    own_rows = query_count // span_count
    summed, sum_total = lax.psum((numerator, cross_total), ("span", "seq"))
    row_start = lax.axis_index("span") * own_rows
    summed = lax.dynamic_slice_in_dim(summed, row_start, own_rows, 0)
    sum_total = lax.dynamic_slice_in_dim(sum_total, row_start, own_rows, 0)
    cross_out = summed.reshape(own_rows, H, DH) / sum_total[:, :, None]
    return (encoded, cross_out.reshape(own_rows, model_width).astype(jnp.bfloat16))


def solution(mesh):
    in_specs = (P(("span", "seq"), None), P("span", None), P(), P(), P(), P(), P())
    out_specs = (P(("span", "seq"), None), P("span", None))
    return jax.shard_map(
        per_device, mesh=mesh, in_specs=in_specs, out_specs=out_specs, check_vma=False
    )
```

profile of v0, /device:TPU:32, one launch (start us, length us, event | category | flops | bytes accessed | tf_op | source)
XLA Modules:
  0.0 758.2 jit_solution(8230057120306540714)
XLA Ops:
  7.2 0.7 all-gather.2.cloned.1.call-update
  7.9 99.7 %all-gather.2.cloned.1.call-done = bf16[1024,3072]{1,0:T(8,128)(2,1)} async-done(((bf16[32,3072]{1,0:T(8,128)(2,1)}), bf16[1024,3072]{1,0:T(8,128)(2,1)}) %all-gather.2.cloned.1.call-update) | async-done | bytes 6291472 | tf_op jit(solution)/shard_map/all_gather | solution.py:26
  107.6 5.9 convolution_convert_fusion
  113.5 2.6 copy.50
  116.1 4.1 copy.51
  120.2 4.3 all-to-all-start
  124.5 27.7 %all-to-all-done = bf16[256,3,1024]{0,1,2:T(4,128)(2,1)} async-done(((bf16[256,3,1024]{0,1,2:T(4,128)(2,1)}), bf16[256,3,1024]{0,1,2:T(4,128)(2,1)}, u32[]{:S(2)}, u32[]{:S(2)}) %all-to-all-start) | async-done | bytes 1572896 | tf_op jit(solution)/shard_map/all_to_all | solution.py:30
  152.2 3.0 copy.52
  155.2 2.6 copy.53
  157.8 2.6 fusion.26
  160.4 2.4 reshape.51
  162.8 1.8 copy.57
  164.6 1.2 copy.55
  165.9 1.2 copy.56
  167.1 25.5 %while.10 = (s32[]{:T(128)}, bf16[4,512,128]{2,1,0:T(8,128)(2,1)}, bf16[4,512,2,64]{1,3,2,0:T(8,128)(2,1)}, bf16[2048,2,64]{0,2,1:T(8,128)(2,1)S(1)}, bf16[2048,2,64]{0,2,1:T(8,128)(2,1)S(1)}, /*index=5*/s32[]{:T(128)}) while((s32[]{:T(128)}, bf16[4,512,128]{2,1,0:T(8,128)(2,1)}, bf16[4,512,2,64]{1,3,2,0:T(8,128)(2,1)}, ...), condition=%wide.region_3.4_spmd, body=%wide.region_0.3_spmd.sunk | while | flops 553777152 | bytes 27021396 | solution.py:56
  167.2 2.3 multiply_reduce_fusion.3
  169.4 1.6 fusion.48
  171.1 1.7 fusion.49
  172.9 0.7 constant_dynamic-update-slice_fusion.2
  173.5 2.3 multiply_reduce_fusion.3
  175.8 1.6 fusion.48
  177.5 1.7 fusion.49
  179.2 0.7 constant_dynamic-update-slice_fusion.2
  179.9 2.3 multiply_reduce_fusion.3
  182.2 1.6 fusion.48
  183.8 1.7 fusion.49
  185.6 0.7 constant_dynamic-update-slice_fusion.2
  186.3 2.3 multiply_reduce_fusion.3
  188.6 1.6 fusion.48
  190.2 1.7 fusion.49
  192.0 0.7 constant_dynamic-update-slice_fusion.2
  192.7 3.6 all-to-all-start.1
  196.5 4.0 copy.62
  200.5 5.7 all-to-all-done.1
  206.4 1.9 fusion.28
  208.3 0.3 multiply_reduce_fusion.1
  208.6 0.2 add_convert_fusion
  208.8 3.7 convolution_convert_fusion.1
  212.5 0.9 fusion.27
  213.4 1.2 copy.61
  214.6 10.3 %bitcast_reduce_fusion = (f32[1024,16]{0,1:T(8,128)}, f32[16,256,1024]{2,1,0:T(8,128)}) fusion(bf16[256,16,64]{0,2,1:T(8,128)(2,1)S(1)} %bitcast.75, bf16[1024,16,64]{0,2,1:T(8,128)(2,1)} %bitcast.70), kind=kOutput, calls=%fused_computation.15 | convolution fusion | flops 545243136 | bytes 19464192 | tf_op jit(solution)/shard_map/qhd,khd->qhk/dot_general | solution.py:68
  225.2 231.8 %all-reduce.4.cloned.1.call-done = f32[1024,16]{0,1:T(8,128)} async-done(((f32[1024,16]{0,1:T(8,128)}), f32[1024,16]{0,1:T(8,128)}) %all-reduce.4.cloned.1.call-update) | async-done | bytes 65552 | tf_op jit(solution)/shard_map/pmax | solution.py:72
  457.0 10.7 %fusion.21 = f32[16,64,1024]{2,1,0:T(8,128)} fusion(bf16[256,16,64]{0,2,1:T(8,128)(2,1)S(1)} %bitcast.78, f32[16,256,1024]{2,1,0:T(8,128)} %get-tuple-element.72, f32[1024,16]{0,1:T(8,128)} %all-reduce.4.cloned.1.call-done), kind=kOutput, calls=%fused_computation.19 | convolution fusion | flops 549453824 | bytes 21561344 | tf_op jit(solution)/shard_map/qhk,khd->qhd/dot_general | solution.py:75
  467.7 5.4 copy.64
  473.1 9.3 %fusion.19 = f32[1024,16]{0,1:T(8,128)} fusion(f32[16,256,1024]{2,1,0:T(8,128)} %get-tuple-element.72, f32[1024,16]{0,1:T(8,128)S(1)} %copy-done.2), kind=kLoop, calls=%fused_computation.17 | loop fusion | flops 12566528 | bytes 16908288 | tf_op jit(solution)/shard_map/reduce_sum | solution.py:74
  482.4 266.6 %all-reduce.6.cloned.1.call-done = (f32[1024,16]{0,1:T(8,128)}, f32[1024,1024]{1,0:T(8,128)}) async-done(((f32[1024,16]{0,1:T(8,128)}, f32[1024,1024]{1,0:T(8,128)}), (f32[1024,16]{0,1:T(8,128)}, f32[1024,1024]{1,0:T(8,128)})) %all-reduce.6.cloned.1.call-update) | async-done | bytes 4259856 | tf_op jit(solution)/shard_map/psum | solution.py:83
  749.0 0.8 constant_dynamic-slice_fusion
  750.1 1.6 divide_convert_fusion
  (27 shorter events, 1.6 us)
Async XLA Ops:
  7.2 199.2 %copy-start = (bf16[1024,1024]{1,0:T(8,128)(2,1)S(1)}, bf16[1024,1024]{1,0:T(8,128)(2,1)}, u32[]{:S(2)}) copy-start(bf16[1024,1024]{1,0:T(8,128)(2,1)} %param.11) | copy-start | bytes 6291460
  7.2 100.4 %all-gather.2.cloned.1.call-start = ((), (), s32[]{:S(2)}) async-start(), calls=%async_computation.2 | async-start | bytes 6488064 | tf_op jit(solution)/shard_map/all_gather | solution.py:26
  120.2 32.0 %all-to-all-start = ((bf16[256,3,1024]{0,1,2:T(4,128)(2,1)}), bf16[256,3,1024]{0,1,2:T(4,128)(2,1)}, u32[]{:S(2)}, u32[]{:S(2)}) async-start(bf16[256,3,1024]{0,1,2:T(4,128)(2,1)} %copy.51), calls=%async_computation | async-start | bytes 4194304 | tf_op jit(solution)/shard_map/all_to_all | solution.py:30
  192.7 15.9 %copy-start.3 = (f32[1024]{0:T(1024)S(1)}, f32[1024]{0:T(1024)}, u32[]{:S(2)}) copy-start(f32[1024]{0:T(1024)} %param.14) | copy-start | bytes 12292
  192.7 15.9 %copy-start.4 = (f32[1024]{0:T(1024)S(1)}, f32[1024]{0:T(1024)}, u32[]{:S(2)}) copy-start(f32[1024]{0:T(1024)} %param.13) | copy-start | bytes 12292
  192.7 13.5 %all-to-all-start.1 = ((bf16[8,256,128]{2,1,0:T(8,128)(2,1)}), bf16[8,256,128]{2,1,0:T(8,128)(2,1)S(1)}, u32[]{:S(2)}, u32[]{:S(2)}) async-start(bf16[8,256,128]{2,1,0:T(8,128)(2,1)} %bitcast.80), calls=%async_computation.1 | async-start | bytes 1048576 | tf_op jit(solution)/shard_map/all_to_all | solution.py:57
  196.3 260.7 %all-reduce.4.cloned.1.call-start = ((), (), s32[]{:S(2)}) async-start(), calls=%async_computation.3 | async-start | bytes 131072 | tf_op jit(solution)/shard_map/pmax | solution.py:72
  208.8 4.5 copy-start.1
  225.0 524.0 %all-reduce.6.cloned.1.call-start = ((), (), s32[]{:S(2)}) async-start(), calls=%async_computation.4 | async-start | bytes 8519680 | tf_op jit(solution)/shard_map/psum | solution.py:83
  467.7 5.4 copy-start.2
Sparse Core Ops, SparseCore 0:
  10.8 96.7 all-gather.1
  225.1 231.8 all-reduce.3
  482.5 266.4 all-reduce.5
where the time goes:
time: 761 us; the launch traced here: 758 us
  waiting for transfers between devices  632 us (83%)
  matrix products  48.2 us (6%)
  local copies, waits for them, and re-layouts  37.7 us (5%)
  other arithmetic  17.9 us (2%)
  between operations  13.9 us (2%)
  starting transfers between devices  8.26 us (1%)
    psum x1, waiting for transfers between devices, per_device(): summed, sum_total = lax.psum((numerator, cross_total), ('span', 'seq'))  267 us
    pmax x1, waiting for transfers between devices, per_device(): cross_peak = lax.pmax(local_peak, ('span', 'seq'))  232 us
    all_gather x1, waiting for transfers between devices, per_device(): lax.all_gather(w_qkv, 'span', axis=0, tiled=True)  99.7 us
    all_to_all x1, waiting for transfers between devices, per_device(): lax.all_to_all(projected, 'seq', split_axis=2, concat_axis=0, tiled=True)  27.7 us
  transfers between devices with their start and end apart: 5, of which 5 were waited for; matrix products, arithmetic and copies ran while one was open for 1% of the time, Pallas kernels for 0%

commit v1 on v0

v1 whole, which is shorter than its diff:
```python
import functools
import math

import jax
import jax.numpy as jnp
from jax import lax
from jax.experimental import pallas as pl
from jax.experimental.pallas import tpu as pltpu
from jax.sharding import PartitionSpec as P

H = 16
DH = 64
PAIR = 2 * DH
MODEL = 1024
ROWS = 256
SEQ = 8
SPAN = 32
OWN = 32
NQ = 1024
STAT_LANES = 16
score_scale = 0.125
LOG2E = math.log2(math.e)
EXP2_SCALE = score_scale * LOG2E

bf16 = jnp.bfloat16
f32 = jnp.float32


def dot(a, b):
    return jnp.dot(a, b, preferred_element_type=f32)


def params(mib=48):
    return pltpu.CompilerParams(vmem_limit_bytes=mib * 1024 * 1024)


def permute(x, axis, size, target):
    return lax.ppermute(x, axis, [(i, target(i)) for i in range(size)])


def lane_low(shape):
    return lax.broadcasted_iota(jnp.int32, shape, len(shape) - 1) < DH


def gather_weight(w, seq_index, span_index):
    mine = lax.dynamic_slice_in_dim(w.reshape(32, 3, MODEL), seq_index * PAIR, PAIR, 2)
    mine = mine.reshape(1, 32, 3 * PAIR)
    x_hi = span_index // 16
    core = span_index % 2
    other = permute(mine, "span", SPAN, lambda i: i ^ 16)
    both = jnp.where(x_hi == 0, jnp.concatenate([mine, other]), jnp.concatenate([other, mine]))
    z_groups = {}
    for i in range(SPAN):
        z_groups.setdefault((i // 16, i % 2), []).append(i)
    ring = lax.all_to_all(
        jnp.broadcast_to(both[None], (8,) + both.shape),
        "span",
        split_axis=0,
        concat_axis=0,
        tiled=True,
        axis_index_groups=list(z_groups.values()),
    )
    twin = permute(ring, "span", SPAN, lambda i: i ^ 1)
    even = jnp.where(core == 0, ring, twin)
    odd = jnp.where(core == 0, twin, ring)
    whole = jnp.stack([even, odd], axis=2)
    return jnp.transpose(whole, (1, 0, 2, 3, 4)).reshape(MODEL, 3 * PAIR)


def gather_column(x):
    half = x.shape[0] // 2
    up = permute(x, "seq", SEQ, lambda i: (i + 2) % SEQ)
    down = permute(x, "seq", SEQ, lambda i: (i - 2) % SEQ)
    up_far = permute(up[:half], "seq", SEQ, lambda i: (i + 2) % SEQ)
    down_far = permute(down[half:], "seq", SEQ, lambda i: (i - 2) % SEQ)
    return up, down, up_far, down_far


def project_kernel(own, peer, up, down, up_far, down_far, w, out):
    row = 0
    for piece in (own, peer, up, down, up_far, down_far):
        count = piece.shape[0]
        out[row : row + count, :] = dot(piece[...], w[...]).astype(bf16)
        row += count


def softmax_pair(q, k_t, v_ones):
    low = lane_low(q.shape)
    zero = jnp.zeros_like(q)
    mixed, total, peak = [], [], []
    for h in range(2):
        scores = dot(jnp.where(low, q, zero) if h == 0 else jnp.where(low, zero, q), k_t)
        top = jnp.max(scores, axis=-1, keepdims=True)
        probs = jnp.exp2((scores - top) * EXP2_SCALE).astype(bf16)
        both = dot(probs, v_ones)
        mixed.append(both[:, :PAIR])
        total.append(both[:, PAIR:])
        peak.append(top)
    return (
        jnp.where(low, mixed[0], mixed[1]),
        jnp.where(low, total[0], total[1]),
        jnp.where(low, peak[0], peak[1]),
    )


def attend_kernel(table, early, up, down, up_far, down_far, w, out, q_all, k_t, v_ones):
    del table
    step = pl.program_id(0)

    @pl.when(step == 0)
    def _():
        v_ones[:, PAIR:] = jnp.ones_like(v_ones[:, PAIR:])
        done = early.shape[0]
        q_all[:done, :] = early[:, :PAIR]
        k_t[:, :done] = early[:, PAIR : 2 * PAIR].T
        v_ones[:done, :PAIR] = early[:, 2 * PAIR :]
        row = done
        for piece in (up, down, up_far, down_far):
            count = piece.shape[0]
            block = dot(piece[...], w[...]).astype(bf16)
            q_all[row : row + count, :] = block[:, :PAIR]
            k_t[:, row : row + count] = block[:, PAIR : 2 * PAIR].T
            v_ones[row : row + count, :PAIR] = block[:, 2 * PAIR :]
            row += count

    q = q_all[pl.ds(pl.multiple_of(step * ROWS, ROWS), ROWS), :]
    mixed, total, _ = softmax_pair(q, k_t[...], v_ones[...])
    out[0] = (mixed / total).astype(bf16)


def encode_kernel(attn, tokens, w_out, gain, bias, w_key, w_value, encoded, cross_kv):
    @pl.when(pl.program_id(0) == 0)
    def _():
        joined = jnp.concatenate([attn[p] for p in range(SEQ)], axis=1)
        residual = tokens[...].astype(f32) + dot(joined, w_out[...])
        center = residual - jnp.mean(residual, -1, keepdims=True)
        spread = jnp.mean(center * center, -1, keepdims=True)
        encoded[...] = (center * lax.rsqrt(spread + 1e-05) * gain[...] + bias[...]).astype(bf16)

    keys = dot(encoded[...], w_key[...]).astype(bf16)
    values = dot(encoded[...], w_value[...]).astype(bf16)
    for p in range(2):
        cross_kv[p, :, :PAIR] = keys[:, p * PAIR : (p + 1) * PAIR]
        cross_kv[p, :, PAIR:] = values[:, p * PAIR : (p + 1) * PAIR]


def cross_kernel(place, queries, kv, keep, send, k_t, v_ones):
    @pl.when(pl.program_id(0) == 0)
    def _():
        k_t[...] = kv[:, :PAIR].T
        v_ones[:, :PAIR] = kv[:, PAIR:]
        v_ones[:, PAIR:] = jnp.ones_like(v_ones[:, PAIR:])

    mixed, total, peak = softmax_pair(queries[...], k_t[...], v_ones[...])
    mixed = mixed / total
    weight = peak * score_scale + jnp.log(total)
    is_even = place[1] == 0
    for g in range(queries.shape[0] // (2 * OWN)):
        even = slice(2 * g * OWN, (2 * g + 1) * OWN)
        odd = slice((2 * g + 1) * OWN, (2 * g + 2) * OWN)
        rows = slice(g * OWN, (g + 1) * OWN)
        for lanes, value in ((slice(0, PAIR), mixed), (slice(PAIR, 2 * PAIR), weight)):
            keep[rows, lanes] = jnp.where(is_even, value[even], value[odd])
            send[rows, lanes] = jnp.where(is_even, value[odd], value[even])


def merge_kernel(keep, received, out):
    here, there = keep[:, PAIR:], received[:, PAIR:]
    top = jnp.maximum(here, there)
    scale_here, scale_there = jnp.exp(here - top), jnp.exp(there - top)
    total = scale_here + scale_there
    mixed = (keep[:, :PAIR] * scale_here + received[:, :PAIR] * scale_there) / total
    weight = top + jnp.log(total)
    high = weight.astype(bf16)
    rest = weight - high.astype(f32)
    middle = rest.astype(bf16)
    low = (rest - middle.astype(f32)).astype(bf16)
    part = lax.broadcasted_iota(jnp.int32, weight.shape, 1) % DH // STAT_LANES
    out[:, :PAIR] = mixed.astype(bf16)
    out[:, PAIR:] = jnp.where(part == 0, high, jnp.where(part == 1, middle, low))


def finish_kernel(parts, out):
    stat = parts[:, :, PAIR:].astype(f32)
    low = lane_low(stat.shape)
    columns = []
    for h in range(2):
        high, middle, rest = (
            stat[:, :, h * DH + p * STAT_LANES : h * DH + p * STAT_LANES + 1] for p in range(3)
        )
        columns.append(high + (middle + rest))
    weight = jnp.where(low, columns[0], columns[1])
    scale = jnp.exp(weight - jnp.max(weight, axis=0, keepdims=True))
    mixed = jnp.sum(parts[:, :, :PAIR].astype(f32) * scale, axis=0) / jnp.sum(scale, axis=0)
    out[...] = jnp.broadcast_to(mixed.astype(bf16)[None], out.shape)


def per_device(tokens, w_qkv, w_out, w_cross, ln_gain, ln_bias, queries):
    seq_index = lax.axis_index("seq")
    span_index = lax.axis_index("span")
    y, x_lo = seq_index // 2, seq_index % 2

    peer = permute(tokens, "seq", SEQ, lambda i: i ^ 1)
    near = gather_column(tokens)
    far = gather_column(peer)
    weight = gather_weight(w_qkv, seq_index, span_index)

    def whole(shape):
        return pl.BlockSpec(shape, lambda *_: (0,) * len(shape))

    early_rows = 5 * ROWS
    early = pl.pallas_call(
        project_kernel,
        out_shape=jax.ShapeDtypeStruct((early_rows, 3 * PAIR), bf16),
        compiler_params=params(),
        cost_estimate=pl.CostEstimate(
            flops=2 * early_rows * MODEL * 3 * PAIR, bytes_accessed=4 << 20, transcendentals=0
        ),
    )(tokens, peer, *near, weight)

    order = jnp.stack(
        [((y + dy) % 4) * 2 + (x_lo ^ flip) for dy, flip in
         ((0, 0), (0, 1), (3, 0), (1, 0), (2, 0), (3, 1), (1, 1), (2, 1))]
    ).astype(jnp.int32)
    length = SEQ * ROWS
    attn = pl.pallas_call(
        attend_kernel,
        grid_spec=pltpu.PrefetchScalarGridSpec(
            num_scalar_prefetch=1,
            grid=(SEQ,),
            in_specs=[
                whole((early_rows, 3 * PAIR)),
                whole((ROWS, MODEL)),
                whole((ROWS, MODEL)),
                whole((ROWS // 2, MODEL)),
                whole((ROWS // 2, MODEL)),
                whole((MODEL, 3 * PAIR)),
            ],
            out_specs=pl.BlockSpec((1, ROWS, PAIR), lambda b, table: (table[b], 0, 0)),
            scratch_shapes=[
                pltpu.VMEM((length, PAIR), bf16),
                pltpu.VMEM((PAIR, length), bf16),
                pltpu.VMEM((length, 2 * PAIR), bf16),
            ],
        ),
        out_shape=jax.ShapeDtypeStruct((SEQ, ROWS, PAIR), bf16),
        compiler_params=params(),
        cost_estimate=pl.CostEstimate(
            flops=8 * length * length * 2 * PAIR, bytes_accessed=4 << 20,
            transcendentals=2 * length * length,
        ),
    )(order, early, *far, weight)
    attn = lax.all_to_all(attn, "seq", split_axis=0, concat_axis=0, tiled=True)

    encoded, cross_kv = pl.pallas_call(
        encode_kernel,
        grid=(4,),
        in_specs=[
            whole((SEQ, ROWS, PAIR)),
            whole((ROWS, MODEL)),
            whole((MODEL, MODEL)),
            whole((1, MODEL)),
            whole((1, MODEL)),
            pl.BlockSpec((MODEL, 2 * PAIR), lambda g: (0, g)),
            pl.BlockSpec((MODEL, 2 * PAIR), lambda g: (0, 4 + g)),
        ],
        out_specs=[
            whole((ROWS, MODEL)),
            pl.BlockSpec((2, ROWS, 2 * PAIR), lambda g: (g, 0, 0)),
        ],
        out_shape=[
            jax.ShapeDtypeStruct((ROWS, MODEL), bf16),
            jax.ShapeDtypeStruct((SEQ, ROWS, 2 * PAIR), bf16),
        ],
        compiler_params=params(),
        cost_estimate=pl.CostEstimate(
            flops=2 * ROWS * MODEL * 3 * MODEL, bytes_accessed=8 << 20, transcendentals=0
        ),
    )(attn, tokens, w_out, ln_gain[None], ln_bias[None], w_cross, w_cross)

    kv = lax.all_to_all(cross_kv, "seq", split_axis=0, concat_axis=0, tiled=True)
    kv = kv.reshape(length, 2 * PAIR)

    place = jnp.stack([seq_index, span_index % 2]).astype(jnp.int32)
    blocks = NQ // ROWS
    keep, send = pl.pallas_call(
        cross_kernel,
        grid_spec=pltpu.PrefetchScalarGridSpec(
            num_scalar_prefetch=1,
            grid=(blocks,),
            in_specs=[
                pl.BlockSpec((ROWS, PAIR), lambda b, place: (b, place[0])),
                whole((length, 2 * PAIR)),
            ],
            out_specs=[
                pl.BlockSpec((ROWS // 2, 2 * PAIR), lambda b, place: (b, 0)),
                pl.BlockSpec((ROWS // 2, 2 * PAIR), lambda b, place: (b, 0)),
            ],
            scratch_shapes=[
                pltpu.VMEM((PAIR, length), bf16),
                pltpu.VMEM((length, 2 * PAIR), bf16),
            ],
        ),
        out_shape=[jax.ShapeDtypeStruct((NQ // 2, 2 * PAIR), f32)] * 2,
        compiler_params=params(),
        cost_estimate=pl.CostEstimate(
            flops=8 * NQ * length * 2 * PAIR, bytes_accessed=2 << 20,
            transcendentals=2 * NQ * length,
        ),
    )(place, queries, kv)

    received = permute(send, "span", SPAN, lambda i: i ^ 1)
    merged = pl.pallas_call(
        merge_kernel,
        out_shape=jax.ShapeDtypeStruct((NQ // 2, 2 * PAIR), bf16),
        compiler_params=params(),
    )(keep, received)
    parts = lax.all_to_all(
        merged.reshape(16, OWN, 2 * PAIR),
        "span",
        split_axis=0,
        concat_axis=0,
        tiled=True,
        axis_index_groups=[list(range(0, SPAN, 2)), list(range(1, SPAN, 2))],
    )
    mine = pl.pallas_call(
        finish_kernel,
        out_shape=jax.ShapeDtypeStruct((SEQ, OWN, PAIR), bf16),
        compiler_params=params(),
    )(parts)
    heads = lax.all_to_all(mine, "seq", split_axis=0, concat_axis=0, tiled=True)
    cross_out = jnp.transpose(heads, (1, 0, 2)).reshape(OWN, MODEL)
    return encoded, cross_out


def solution(mesh):
    in_specs = (P(("span", "seq"), None), P("span", None), P(), P(), P(), P(), P())
    out_specs = (P(("span", "seq"), None), P("span", None))
    return jax.shard_map(
        per_device, mesh=mesh, in_specs=in_specs, out_specs=out_specs, check_vma=False
    )
```

time: 761 us -> 151 us (0.20)
  waiting for transfers between devices: 632 us -> 38.9 us
  matrix products: 48.2 us -> 0 us
  blocking collectives: 0 us -> 40.7 us
  Pallas kernels: 0 us -> 35.8 us
  local copies, waits for them, and re-layouts: 37.7 us -> 3 us
  starting transfers between devices: 8.26 us -> 30.7 us
  other arithmetic: 17.9 us -> 0.26 us
  between operations: 13.9 us -> 0.92 us
    psum x1 -> x0, waiting for transfers between devices: 267 us -> none  [per_device(): summed, sum_total = lax.psum((numerator, cross_total), ('span', 'seq'))]
    pmax x1 -> x0, waiting for transfers between devices: 232 us -> none  [per_device(): cross_peak = lax.pmax(local_peak, ('span', 'seq'))]
    all_gather x1 -> x0, waiting for transfers between devices: 99.7 us -> none  [per_device(): lax.all_gather(w_qkv, 'span', axis=0, tiled=True)]
    dot_general x13 -> x0, matrix products: 48.2 us -> none  [the longest x1 10.7 us: per_device(): jnp.einsum('qhk,khd->qhd', cross_powers.astype(jnp.bfloat16), cross_value...]
    all_to_all x0 -> x3, blocking collectives: none -> 40.7 us  [the longest x1 20.8 us: per_device(): lax.all_to_all(merged.reshape(16, OWN, 2 * PAIR), 'span', split_axis=0, c...]
    pallas_call x0 -> x6, Pallas kernels: none -> 35.8 us  [the longest x1 18.5 us: per_device(): pl.pallas_call(attend_kernel, grid_spec=pltpu.PrefetchScalarGridSpec(num_...]
    ppermute x0 -> x12, waiting for transfers between devices: none -> 26.5 us  [permute(): return lax.ppermute(x, axis, [(i, target(i)) for i in range(size)])]
    all_to_all x2, waiting for transfers between devices: 33.4 us -> 12.4 us  [the longest x1 12.4 us: per_device(): lax.all_to_all(cross_kv, 'seq', split_axis=0, concat_axis=0, tiled=True)]
  transfers between devices with their start and end apart: 5 -> 14, of which waited for: 5 -> 8; matrix products, arithmetic and copies ran while one was open for 1% -> 0% of each run, Pallas kernels for 0% -> 1%
where the time goes in v1:
time: 151 us; the launch traced here: 150 us
  blocking collectives  40.7 us (27%)
  waiting for transfers between devices  38.9 us (26%)
  Pallas kernels  35.8 us (24%)
  starting transfers between devices  30.7 us (20%)
  local copies, waits for them, and re-layouts  3 us (2%)
    ppermute x12, waiting for transfers between devices, permute(): return lax.ppermute(x, axis, [(i, target(i)) for i in range(size)])  26.5 us
    all_to_all x1, blocking collectives, per_device(): lax.all_to_all(merged.reshape(16, OWN, 2 * PAIR), 'span', split_axis=0, c...  20.8 us
    pallas_call x1, Pallas kernels, per_device(): pl.pallas_call(attend_kernel, grid_spec=pltpu.PrefetchScalarGridSpec(num_...  18.5 us
    ppermute x12, starting transfers between devices, permute(): return lax.ppermute(x, axis, [(i, target(i)) for i in range(size)])  18.5 us
    all_to_all x1, waiting for transfers between devices, per_device(): lax.all_to_all(cross_kv, 'seq', split_axis=0, concat_axis=0, tiled=True)  12.4 us
    all_to_all x1, blocking collectives, per_device(): attn = lax.all_to_all(attn, 'seq', split_axis=0, concat_axis=0, tiled=True)  11.1 us
    pallas_call x1, Pallas kernels, per_device(): pl.pallas_call(cross_kernel, grid_spec=pltpu.PrefetchScalarGridSpec(num_s...  9.32 us
    all_to_all x1, blocking collectives, per_device(): heads = lax.all_to_all(mine, 'seq', split_axis=0, concat_axis=0, tiled=True)  8.81 us
  transfers between devices with their start and end apart: 14, of which 8 were waited for; matrix products, arithmetic and copies ran while one was open for 0% of the time, Pallas kernels for 1%

profile of v1, /device:TPU:32, one launch (start us, length us, event | category | flops | bytes accessed | tf_op | source)
XLA Modules:
  0.0 150.3 jit_solution(2797950031749087775)
XLA Ops:
  0.6 1.2 reshape.51
  1.9 3.1 %collective-permute-start.5 = (bf16[1,32,384]{2,1,0:T(8,128)(2,1)S(1)}, bf16[1,32,384]{2,1,0:T(8,128)(2,1)S(1)}, u32[]{:S(2)}, u32[]{:S(2)}) collective-permute-start(bf16[1,32,384]{2,1,0:T(8,128)(2,1)S(1)} %concatenate.16), channel_id=1, source_target_pairs={{0,128},{8,136},{16,144},{24,152},{32,160},{40,168},{48,176},{56,1... | collective-permute-start | bytes 73736 | tf_op jit(solution)/shard_map/ppermute | solution.py:38
  5.0 2.3 %collective-permute-done.5 = bf16[1,32,384]{2,1,0:T(8,128)(2,1)S(1)} collective-permute-done((bf16[1,32,384]{2,1,0:T(8,128)(2,1)S(1)}, bf16[1,32,384]{2,1,0:T(8,128)(2,1)S(1)}, u32[]{:S(2)}, u32[]{:S(2)}) %collective-permute-start.5) | collective-permute-done | bytes 24608 | tf_op jit(solution)/shard_map/ppermute | solution.py:38
  7.3 0.8 broadcast_in_dim.12
  8.1 8.6 %all-to-all-start = ((bf16[8,2,32,384]{3,2,1,0:T(8,128)(2,1)}), bf16[8,2,32,384]{3,2,1,0:T(8,128)(2,1)S(1)}, u32[]{:S(2)}, u32[]{:S(2)}) async-start(bf16[8,2,32,384]{3,2,1,0:T(8,128)(2,1)} %broadcast_in_dim.12), calls=%async_computation | async-start | bytes 786432 | tf_op jit(solution)/shard_map/all_to_all | solution.py:55
  16.7 1.5 collective-permute-start
  18.2 3.0 %collective-permute-start.2 = (bf16[256,1024]{1,0:T(8,128)(2,1)}, bf16[256,1024]{1,0:T(8,128)(2,1)S(1)}, u32[]{:S(2)}, u32[]{:S(2)}) collective-permute-start(bf16[256,1024]{1,0:T(8,128)(2,1)} %tokens.1), channel_id=1, source_target_pairs={{0,6},{1,7},{2,0},{3,1},{4,2},{5,3},{6,4},{7,5},{8,14},{9,15},{10,... | collective-permute-start | bytes 1572872 | tf_op jit(solution)/shard_map/ppermute | solution.py:38
  21.2 0.0 collective-permute-start.1
  21.2 7.7 %collective-permute-done.peer = bf16[256,1024]{1,0:T(8,128)(2,1)S(1)} collective-permute-done((bf16[256,1024]{1,0:T(8,128)(2,1)}, bf16[256,1024]{1,0:T(8,128)(2,1)S(1)}, u32[]{:S(2)}, u32[]{:S(2)}) %collective-permute-start) | collective-permute-done | bytes 524320 | tf_op jit(solution)/shard_map/ppermute | solution.py:38
  28.9 3.0 %collective-permute-start.8 = (bf16[256,1024]{1,0:T(8,128)(2,1)S(1)}, bf16[256,1024]{1,0:T(8,128)(2,1)S(1)}, u32[]{:S(2)}, u32[]{:S(2)}) collective-permute-start(bf16[256,1024]{1,0:T(8,128)(2,1)S(1)} %collective-permute-done.peer), channel_id=1, source_target_pairs={{0,6},{1,7},{2,0},{3,1},{4,2},{5,3},{6,4},{7,5},{8,14},{9,15},{10,... | collective-permute-start | bytes 1572872 | tf_op jit(solution)/shard_map/ppermute | solution.py:38
  31.9 0.0 collective-permute-start.7
  31.9 0.0 all-to-all-done
  31.9 0.0 collective-permute-start.6
  32.0 0.1 stack.53.table
  32.1 0.0 collective-permute-done.2.down
  32.1 3.6 %collective-permute-start.4 = (bf16[128,1024]{1,0:T(8,128)(2,1)S(1)}, bf16[128,1024]{1,0:T(8,128)(2,1)S(1)}, u32[]{:S(2)}, u32[]{:S(2)}) collective-permute-start(bf16[128,1024]{1,0:T(8,128)(2,1)S(1)} %slice.17), channel_id=1, source_target_pairs={{0,6},{1,7},{2,0},{3,1},{4,2},{5,3},{6,4},{7,5},{8,14},{9,15},{10,... | collective-permute-start | bytes 786440 | tf_op jit(solution)/shard_map/ppermute | solution.py:38
  35.8 0.0 collective-permute-done.1.up
  35.8 0.1 collective-permute-start.3
  35.9 8.4 %collective-permute-done.8.down = bf16[256,1024]{1,0:T(8,128)(2,1)S(1)} collective-permute-done((bf16[256,1024]{1,0:T(8,128)(2,1)S(1)}, bf16[256,1024]{1,0:T(8,128)(2,1)S(1)}, u32[]{:S(2)}, u32[]{:S(2)}) %collective-permute-start.8) | collective-permute-done | bytes 524320 | tf_op jit(solution)/shard_map/ppermute | solution.py:38
  44.3 3.8 %collective-permute-start.10 = (bf16[128,1024]{1,0:T(8,128)(2,1)S(1)}, bf16[128,1024]{1,0:T(8,128)(2,1)S(1)}, u32[]{:S(2)}, u32[]{:S(2)}) collective-permute-start(bf16[128,1024]{1,0:T(8,128)(2,1)S(1)} %slice.19), channel_id=1, source_target_pairs={{0,6},{1,7},{2,0},{3,1},{4,2},{5,3},{6,4},{7,5},{8,14},{9,15},{10,... | collective-permute-start | bytes 786440 | tf_op jit(solution)/shard_map/ppermute | solution.py:38
  48.1 0.0 collective-permute-done.7.up
  48.1 0.0 copy-start.1
  48.1 0.3 collective-permute-start.9
  48.4 0.0 collective-permute-done.6
  48.4 0.1 select_bitcast_fusion.1
  48.5 0.1 maximum_bitcast_fusion
  48.6 0.1 copy.12
  48.7 1.2 collective-permute-done.4.down_far
  49.9 3.7 %collective-permute-done.3.up_far = bf16[128,1024]{1,0:T(8,128)(2,1)S(1)} collective-permute-done((bf16[128,1024]{1,0:T(8,128)(2,1)S(1)}, bf16[128,1024]{1,0:T(8,128)(2,1)S(1)}, u32[]{:S(2)}, u32[]{:S(2)}) %collective-permute-start.3) | collective-permute-done | bytes 262176 | tf_op jit(solution)/shard_map/ppermute | solution.py:38
  53.6 1.5 %shard_map.86.early = bf16[1280,384]{1,0:T(8,128)(2,1)S(1)} custom-call(bf16[256,1024]{1,0:T(8,128)(2,1)S(1)} %copy-done.1, bf16[256,1024]{1,0:T(8,128)(2,1)S(1)} %collective-permute-done.peer, bf16[256,1024]{1,0:T(8,128)(2,1)S(1)} %collective-permute-done.1.up, bf16[256,1024]{1,0:T(8,128)(2,1)S(1)} %collective-permute-done.2.down, ...), custom_call_target="tpu_custom_call" | custom-call | flops 1006632960 | bytes 4194304 | tf_op jit(solution)/shard_map/pallas_call | solution.py:212
  55.1 0.0 copy-start.2
  55.1 0.0 copy-start.3
  55.1 0.0 collective-permute-done.10.down_far
  55.1 1.4 collective-permute-done.9.up_far
  56.5 18.5 %shard_map.87 = bf16[8,256,128]{2,1,0:T(8,128)(2,1)S(1)} custom-call(s32[8]{0:T(128)S(1)} %stack.53.table, bf16[1280,384]{1,0:T(8,128)(2,1)S(1)} %shard_map.86.early, bf16[256,1024]{1,0:T(8,128)(2,1)S(1)} %collective-permute-done.7.up, bf16[256,1024]{1,0:T(8,128)(2,1)S(1)} %collective-permute-done.8.down, ...), custom_call_target="tpu_custom_call" | custom-call | flops 8589934592 | bytes 4194304 | tf_op jit(solution)/shard_map/pallas_call | solution.py:226
  75.0 11.1 %all_to_all.25.attn = bf16[8,256,128]{2,1,0:T(8,128)(2,1)S(1)} all-to-all(bf16[8,256,128]{2,1,0:T(8,128)(2,1)S(1)} %shard_map.87), channel_id=1, replica_groups=mesh['span'=32,'seq'=8] {'seq'}, dimensions={0} | all-to-all | bytes 1048576 | tf_op jit(solution)/shard_map/all_to_all | solution.py:253
  86.1 5.8 %shard_map.88 = (bf16[256,1024]{1,0:T(8,128)(2,1)}, bf16[8,256,256]{2,1,0:T(8,128)(2,1)}) custom-call(bf16[8,256,128]{2,1,0:T(8,128)(2,1)S(1)} %all_to_all.25.attn, bf16[256,1024]{1,0:T(8,128)(2,1)S(1)} %copy-done.1, bf16[1024,1024]{1,0:T(8,128)(2,1)S(1)} %copy-done, f32[1,1024]{1,0:T(1,128)S(1)} %bitcast.31, f32[1,1024]{1,0:T(1,128)S(1)} %bitcast.32, ...), custom_call_target="tpu_custom_call" | custom-call | flops 1610612736 | bytes 8388608 | tf_op jit(solution)/shard_map/pallas_call | solution.py:255
  91.9 3.7 %all-to-all-start.2 = ((bf16[8,256,256]{2,1,0:T(8,128)(2,1)}), bf16[8,256,256]{2,1,0:T(8,128)(2,1)S(1)}, u32[]{:S(2)}, u32[]{:S(2)}) async-start(bf16[8,256,256]{2,1,0:T(8,128)(2,1)} %get-tuple-element.7), calls=%async_computation.2 | async-start | bytes 2097152 | tf_op jit(solution)/shard_map/all_to_all | solution.py:281
  95.6 0.1 pad_add_fusion.place
  95.7 12.4 %all-to-all-done.2 = bf16[8,256,256]{2,1,0:T(8,128)(2,1)S(1)} async-done(((bf16[8,256,256]{2,1,0:T(8,128)(2,1)}), bf16[8,256,256]{2,1,0:T(8,128)(2,1)S(1)}, u32[]{:S(2)}, u32[]{:S(2)}) %all-to-all-start.2) | async-done | bytes 1048608 | tf_op jit(solution)/shard_map/all_to_all | solution.py:281
  108.1 9.3 %shard_map.89 = (f32[512,256]{1,0:T(8,128)S(1)}, f32[512,256]{1,0:T(8,128)S(1)}) custom-call(s32[2]{0:T(128)S(1)} %pad_add_fusion.place, bf16[1024,1024]{1,0:T(8,128)(2,1)S(1)} %copy-done.4, bf16[2048,256]{1,0:T(8,128)(2,1)S(1)} %bitcast.30), custom_call_target="tpu_custom_call" | custom-call | flops 4294967296 | bytes 2097152 | tf_op jit(solution)/shard_map/pallas_call | solution.py:286
  117.4 0.1 collective-permute-start.11
  117.5 1.9 %collective-permute-done.11.received = f32[512,256]{1,0:T(8,128)S(1)} collective-permute-done((f32[512,256]{1,0:T(8,128)S(1)}, f32[512,256]{1,0:T(8,128)S(1)}, u32[]{:S(2)}, u32[]{:S(2)}) %collective-permute-start.11) | collective-permute-done | bytes 524320 | tf_op jit(solution)/shard_map/ppermute | solution.py:38
  119.4 0.2 shard_map.90
  119.6 20.8 %all_to_all.26.parts = bf16[16,32,256]{2,1,0:T(8,128)(2,1)S(1)} all-to-all(bf16[16,32,256]{2,1,0:T(8,128)(2,1)S(1)} %bitcast.29), channel_id=1, replica_groups={{0,16,32,48,64,80,96,112,128,144,160,176,192,208,224,240},{8,24,40,56,7..., dimensions={0} | all-to-all | bytes 524288 | tf_op jit(solution)/shard_map/all_to_all | solution.py:318
  140.4 0.4 shard_map.91
  140.9 8.8 %all_to_all.27 = bf16[8,32,128]{2,1,0:T(8,128)(2,1)S(1)} all-to-all(bf16[8,32,128]{2,1,0:T(8,128)(2,1)S(1)} %shard_map.91), channel_id=1, replica_groups=mesh['span'=32,'seq'=8] {'seq'}, dimensions={0} | all-to-all | bytes 131072 | tf_op jit(solution)/shard_map/all_to_all | solution.py:331
  149.7 0.6 copy_bitcast_fusion
  (14 shorter events, 0.2 us)
Async XLA Ops:
  1.9 5.4 %collective-permute-start.5 = (bf16[1,32,384]{2,1,0:T(8,128)(2,1)S(1)}, bf16[1,32,384]{2,1,0:T(8,128)(2,1)S(1)}, u32[]{:S(2)}, u32[]{:S(2)}) collective-permute-start(bf16[1,32,384]{2,1,0:T(8,128)(2,1)S(1)} %concatenate.16), channel_id=1, source_target_pairs={{0,128},{8,136},{16,144},{24,152},{32,160},{40,168},{48,176},{56,1... | collective-permute-start | bytes 73736 | tf_op jit(solution)/shard_map/ppermute | solution.py:38
  8.1 23.8 %all-to-all-start = ((bf16[8,2,32,384]{3,2,1,0:T(8,128)(2,1)}), bf16[8,2,32,384]{3,2,1,0:T(8,128)(2,1)S(1)}, u32[]{:S(2)}, u32[]{:S(2)}) async-start(bf16[8,2,32,384]{3,2,1,0:T(8,128)(2,1)} %broadcast_in_dim.12), calls=%async_computation | async-start | bytes 786432 | tf_op jit(solution)/shard_map/all_to_all | solution.py:55
  16.7 12.2 %collective-permute-start = (bf16[256,1024]{1,0:T(8,128)(2,1)}, bf16[256,1024]{1,0:T(8,128)(2,1)S(1)}, u32[]{:S(2)}, u32[]{:S(2)}) collective-permute-start(bf16[256,1024]{1,0:T(8,128)(2,1)} %tokens.1), channel_id=1, source_target_pairs={{0,1},{1,0},{2,3},{3,2},{4,5},{5,4},{6,7},{7,6},{8,9},{9,8},{10,11... | collective-permute-start | bytes 1572872 | tf_op jit(solution)/shard_map/ppermute | solution.py:38
  18.2 13.9 %collective-permute-start.2 = (bf16[256,1024]{1,0:T(8,128)(2,1)}, bf16[256,1024]{1,0:T(8,128)(2,1)S(1)}, u32[]{:S(2)}, u32[]{:S(2)}) collective-permute-start(bf16[256,1024]{1,0:T(8,128)(2,1)} %tokens.1), channel_id=1, source_target_pairs={{0,6},{1,7},{2,0},{3,1},{4,2},{5,3},{6,4},{7,5},{8,14},{9,15},{10,... | collective-permute-start | bytes 1572872 | tf_op jit(solution)/shard_map/ppermute | solution.py:38
  21.2 14.5 %collective-permute-start.1 = (bf16[256,1024]{1,0:T(8,128)(2,1)}, bf16[256,1024]{1,0:T(8,128)(2,1)S(1)}, u32[]{:S(2)}, u32[]{:S(2)}) collective-permute-start(bf16[256,1024]{1,0:T(8,128)(2,1)} %tokens.1), channel_id=1, source_target_pairs={{0,2},{1,3},{2,4},{3,5},{4,6},{5,7},{6,0},{7,1},{8,10},{9,11},{10,... | collective-permute-start | bytes 1572872 | tf_op jit(solution)/shard_map/ppermute | solution.py:38
  28.9 15.4 %collective-permute-start.8 = (bf16[256,1024]{1,0:T(8,128)(2,1)S(1)}, bf16[256,1024]{1,0:T(8,128)(2,1)S(1)}, u32[]{:S(2)}, u32[]{:S(2)}) collective-permute-start(bf16[256,1024]{1,0:T(8,128)(2,1)S(1)} %collective-permute-done.peer), channel_id=1, source_target_pairs={{0,6},{1,7},{2,0},{3,1},{4,2},{5,3},{6,4},{7,5},{8,14},{9,15},{10,... | collective-permute-start | bytes 1572872 | tf_op jit(solution)/shard_map/ppermute | solution.py:38
  31.9 16.2 %collective-permute-start.7 = (bf16[256,1024]{1,0:T(8,128)(2,1)S(1)}, bf16[256,1024]{1,0:T(8,128)(2,1)S(1)}, u32[]{:S(2)}, u32[]{:S(2)}) collective-permute-start(bf16[256,1024]{1,0:T(8,128)(2,1)S(1)} %collective-permute-done.peer), channel_id=1, source_target_pairs={{0,2},{1,3},{2,4},{3,5},{4,6},{5,7},{6,0},{7,1},{8,10},{9,11},{10,... | collective-permute-start | bytes 1572872 | tf_op jit(solution)/shard_map/ppermute | solution.py:38
  31.9 16.5 %collective-permute-start.6 = (bf16[8,2,32,384]{3,2,1,0:T(8,128)(2,1)S(1)}, bf16[8,2,32,384]{3,2,1,0:T(8,128)(2,1)S(1)}, u32[]{:S(2)}, u32[]{:S(2)}) collective-permute-start(bf16[8,2,32,384]{3,2,1,0:T(8,128)(2,1)S(1)} %all-to-all-done), channel_id=1, source_target_pairs={{0,8},{8,0},{16,24},{24,16},{32,40},{40,32},{48,56},{56,48},{64,72... | collective-permute-start | bytes 1179656 | tf_op jit(solution)/shard_map/ppermute | solution.py:38
  32.1 17.8 %collective-permute-start.4 = (bf16[128,1024]{1,0:T(8,128)(2,1)S(1)}, bf16[128,1024]{1,0:T(8,128)(2,1)S(1)}, u32[]{:S(2)}, u32[]{:S(2)}) collective-permute-start(bf16[128,1024]{1,0:T(8,128)(2,1)S(1)} %slice.17), channel_id=1, source_target_pairs={{0,6},{1,7},{2,0},{3,1},{4,2},{5,3},{6,4},{7,5},{8,14},{9,15},{10,... | collective-permute-start | bytes 786440 | tf_op jit(solution)/shard_map/ppermute | solution.py:38
  35.8 17.8 %collective-permute-start.3 = (bf16[128,1024]{1,0:T(8,128)(2,1)S(1)}, bf16[128,1024]{1,0:T(8,128)(2,1)S(1)}, u32[]{:S(2)}, u32[]{:S(2)}) collective-permute-start(bf16[128,1024]{1,0:T(8,128)(2,1)S(1)} %slice.16), channel_id=1, source_target_pairs={{0,2},{1,3},{2,4},{3,5},{4,6},{5,7},{6,0},{7,1},{8,10},{9,11},{10,... | collective-permute-start | bytes 786440 | tf_op jit(solution)/shard_map/ppermute | solution.py:38
  44.3 10.8 %collective-permute-start.10 = (bf16[128,1024]{1,0:T(8,128)(2,1)S(1)}, bf16[128,1024]{1,0:T(8,128)(2,1)S(1)}, u32[]{:S(2)}, u32[]{:S(2)}) collective-permute-start(bf16[128,1024]{1,0:T(8,128)(2,1)S(1)} %slice.19), channel_id=1, source_target_pairs={{0,6},{1,7},{2,0},{3,1},{4,2},{5,3},{6,4},{7,5},{8,14},{9,15},{10,... | collective-permute-start | bytes 786440 | tf_op jit(solution)/shard_map/ppermute | solution.py:38
  48.1 5.5 %copy-start.1 = (bf16[256,1024]{1,0:T(8,128)(2,1)S(1)}, bf16[256,1024]{1,0:T(8,128)(2,1)}, u32[]{:S(2)}) copy-start(bf16[256,1024]{1,0:T(8,128)(2,1)} %tokens.1) | copy-start | bytes 1572868
  48.1 8.4 %collective-permute-start.9 = (bf16[128,1024]{1,0:T(8,128)(2,1)S(1)}, bf16[128,1024]{1,0:T(8,128)(2,1)S(1)}, u32[]{:S(2)}, u32[]{:S(2)}) collective-permute-start(bf16[128,1024]{1,0:T(8,128)(2,1)S(1)} %slice.18), channel_id=1, source_target_pairs={{0,2},{1,3},{2,4},{3,5},{4,6},{5,7},{6,0},{7,1},{8,10},{9,11},{10,... | collective-permute-start | bytes 786440 | tf_op jit(solution)/shard_map/ppermute | solution.py:38
  55.1 31.0 %copy-start.2 = (f32[1024]{0:T(1024)S(1)}, f32[1024]{0:T(1024)}, u32[]{:S(2)}) copy-start(f32[1024]{0:T(1024)} %param.11) | copy-start | bytes 12292
  55.1 31.0 %copy-start.3 = (f32[1024]{0:T(1024)S(1)}, f32[1024]{0:T(1024)}, u32[]{:S(2)}) copy-start(f32[1024]{0:T(1024)} %param.12) | copy-start | bytes 12292
  56.5 29.6 %copy-start = (bf16[1024,1024]{1,0:T(8,128)(2,1)S(1)}, bf16[1024,1024]{1,0:T(8,128)(2,1)}, u32[]{:S(2)}) copy-start(bf16[1024,1024]{1,0:T(8,128)(2,1)} %w_out.1) | copy-start | bytes 6291460
  91.9 16.1 %copy-start.4 = (bf16[1024,1024]{1,0:T(8,128)(2,1)S(1)}, bf16[1024,1024]{1,0:T(8,128)(2,1)}, u32[]{:S(2)}) copy-start(bf16[1024,1024]{1,0:T(8,128)(2,1)} %queries.1) | copy-start | bytes 6291460
  91.9 16.1 %all-to-all-start.2 = ((bf16[8,256,256]{2,1,0:T(8,128)(2,1)}), bf16[8,256,256]{2,1,0:T(8,128)(2,1)S(1)}, u32[]{:S(2)}, u32[]{:S(2)}) async-start(bf16[8,256,256]{2,1,0:T(8,128)(2,1)} %get-tuple-element.7), calls=%async_computation.2 | async-start | bytes 2097152 | tf_op jit(solution)/shard_map/all_to_all | solution.py:281
  117.4 2.0 %collective-permute-start.11 = (f32[512,256]{1,0:T(8,128)S(1)}, f32[512,256]{1,0:T(8,128)S(1)}, u32[]{:S(2)}, u32[]{:S(2)}) collective-permute-start(f32[512,256]{1,0:T(8,128)S(1)} %get-tuple-element.9), channel_id=1, source_target_pairs={{0,8},{8,0},{16,24},{24,16},{32,40},{40,32},{48,56},{56,48},{64,72... | collective-permute-start | bytes 1572872 | tf_op jit(solution)/shard_map/ppermute | solution.py:38

commit v2 on v1

v2 whole, which is shorter than its diff:
```python
import functools
import math

import jax
import jax.numpy as jnp
from jax import lax
from jax.experimental import pallas as pl
from jax.experimental.pallas import tpu as pltpu
from jax.sharding import PartitionSpec as P

H = 16
DH = 64
PAIR = 2 * DH
MODEL = 1024
ROWS = 256
SEQ = 8
SPAN = 32
OWN = 32
NQ = 1024
STAT_LANES = 16
BLOCK = 512
SPREAD = (16, 8, 4, 2)
score_scale = 0.125
LOG2E = math.log2(math.e)
EXP2_SCALE = score_scale * LOG2E

bf16 = jnp.bfloat16
f32 = jnp.float32


def dot(a, b):
    return jnp.dot(a, b, preferred_element_type=f32)


def params(mib=48):
    return pltpu.CompilerParams(vmem_limit_bytes=mib * 1024 * 1024)


def permute(x, axis, size, target):
    return lax.ppermute(x, axis, [(i, target(i)) for i in range(size)])


def lane_low(shape):
    return lax.broadcasted_iota(jnp.int32, shape, len(shape) - 1) < DH


def spread(blocks, bit):
    return jnp.concatenate([blocks, permute(blocks, "span", SPAN, lambda i: i ^ bit)])


def from_below(x):
    return permute(x, "seq", SEQ, lambda i: (i + 2) % SEQ)


def from_above(x):
    return permute(x, "seq", SEQ, lambda i: (i - 2) % SEQ)


def across(x):
    return permute(x, "seq", SEQ, lambda i: i ^ 1)


def project_kernel(place, own, peer, up, down, up_far, down_far, mine, twin, out, w):
    for k in range(1 << len(SPREAD)):
        flip = sum(bit for p, bit in enumerate(SPREAD) if k >> p & 1)
        for core, blocks in enumerate((mine, twin)):
            start = pl.multiple_of((place[1] ^ (flip + core)) * 32, 32)
            w[pl.ds(start, 32), :] = blocks[k * 32 : (k + 1) * 32, :]
    row = 0
    for piece in (own, peer, up, down, up_far, down_far):
        count = piece.shape[0]
        out[row : row + count, :] = dot(piece[...], w[...]).astype(bf16)
        row += count


def head_scores(q, k_t, head):
    low = lane_low(q.shape)
    zero = jnp.zeros_like(q)
    return dot(jnp.where(low, q, zero) if head == 0 else jnp.where(low, zero, q), k_t)


def weigh(scores, v_ones):
    top = jnp.max(scores, axis=-1, keepdims=True)
    probs = jnp.exp2((scores - top) * EXP2_SCALE).astype(bf16)
    return dot(probs, v_ones), top


def softmax_pair(step, q_block, k_t, v_ones, scores_0, scores_1):
    scores_1[...] = head_scores(q_block(step), k_t[...], 1)
    mixed_0, peak_0 = weigh(scores_0[...], v_ones[...])
    after = jnp.minimum(step + 1, pl.num_programs(0) - 1)
    scores_0[...] = head_scores(q_block(after), k_t[...], 0)
    mixed_1, peak_1 = weigh(scores_1[...], v_ones[...])
    low = lane_low((scores_0.shape[0], PAIR))
    total = jnp.where(low, mixed_0[:, PAIR:], mixed_1[:, PAIR:])
    mixed = jnp.where(low, mixed_0[:, :PAIR], mixed_1[:, :PAIR]) / total
    return mixed, total, jnp.where(low, peak_0, peak_1)


def attend_kernel(
    table, early, up, down, up_far, down_far, w, out, q_all, k_t, v_ones, scores_0, scores_1
):
    step = pl.program_id(0)

    def q_block(i):
        return q_all[pl.ds(pl.multiple_of(i * BLOCK, BLOCK), BLOCK), :]

    @pl.when(step == 0)
    def _():
        v_ones[:, PAIR:] = jnp.ones_like(v_ones[:, PAIR:])
        done = early.shape[0]
        q_all[:done, :] = early[:, :PAIR]
        k_t[:, :done] = early[:, PAIR : 2 * PAIR].T
        v_ones[:done, :PAIR] = early[:, 2 * PAIR :]
        row = done
        for piece in (up, down, up_far, down_far):
            count = piece.shape[0]
            block = dot(piece[...], w[...]).astype(bf16)
            q_all[row : row + count, :] = block[:, :PAIR]
            k_t[:, row : row + count] = block[:, PAIR : 2 * PAIR].T
            v_ones[row : row + count, :PAIR] = block[:, 2 * PAIR :]
            row += count
        scores_0[...] = head_scores(q_block(0), k_t[...], 0)

    mixed, _, _ = softmax_pair(step, q_block, k_t, v_ones, scores_0, scores_1)
    mixed = mixed.astype(bf16)
    for p in range(BLOCK // ROWS):
        out[table[step * (BLOCK // ROWS) + p]] = mixed[p * ROWS : (p + 1) * ROWS]


def encode_kernel(attn, tokens, w_out, gain, bias, w_cross, encoded, cross_kv):
    joined = jnp.concatenate([attn[p] for p in range(SEQ)], axis=1)
    residual = tokens[...].astype(f32) + dot(joined, w_out[...])
    center = residual - jnp.mean(residual, -1, keepdims=True)
    spread = jnp.mean(center * center, -1, keepdims=True)
    state = (center * lax.rsqrt(spread + 1e-05) * gain[...] + bias[...]).astype(bf16)
    encoded[...] = state
    for g in range(SEQ // 2):
        for part in range(2):
            start = part * MODEL + 2 * g * PAIR
            both = dot(state, w_cross[:, start : start + 2 * PAIR]).astype(bf16)
            for p in range(2):
                cross_kv[2 * g + p, :, part * PAIR : (part + 1) * PAIR] = both[
                    :, p * PAIR : (p + 1) * PAIR
                ]


def cross_kernel(place, queries, kv, keep, send, k_t, v_ones, scores_0, scores_1):
    step = pl.program_id(0)

    def q_block(i):
        return queries[pl.ds(pl.multiple_of(i * BLOCK, BLOCK), BLOCK), :]

    @pl.when(step == 0)
    def _():
        k_t[...] = kv[:, :PAIR].T
        v_ones[:, :PAIR] = kv[:, PAIR:]
        v_ones[:, PAIR:] = jnp.ones_like(v_ones[:, PAIR:])
        scores_0[...] = head_scores(q_block(0), k_t[...], 0)

    mixed, total, peak = softmax_pair(step, q_block, k_t, v_ones, scores_0, scores_1)
    weight = peak * score_scale + jnp.log(total)
    is_even = place[1] % 2 == 0
    for g in range(BLOCK // (2 * OWN)):
        even = slice(2 * g * OWN, (2 * g + 1) * OWN)
        odd = slice((2 * g + 1) * OWN, (2 * g + 2) * OWN)
        rows = slice(g * OWN, (g + 1) * OWN)
        for lanes, value in ((slice(0, PAIR), mixed), (slice(PAIR, 2 * PAIR), weight)):
            keep[rows, lanes] = jnp.where(is_even, value[even], value[odd])
            send[rows, lanes] = jnp.where(is_even, value[odd], value[even])


def merge_kernel(keep, received, out):
    here, there = keep[:, PAIR:], received[:, PAIR:]
    top = jnp.maximum(here, there)
    scale_here, scale_there = jnp.exp(here - top), jnp.exp(there - top)
    total = scale_here + scale_there
    mixed = (keep[:, :PAIR] * scale_here + received[:, :PAIR] * scale_there) / total
    weight = top + jnp.log(total)
    high = weight.astype(bf16)
    rest = weight - high.astype(f32)
    middle = rest.astype(bf16)
    low = (rest - middle.astype(f32)).astype(bf16)
    part = lax.broadcasted_iota(jnp.int32, weight.shape, 1) % DH // STAT_LANES
    out[:, :PAIR] = mixed.astype(bf16)
    out[:, PAIR:] = jnp.where(part == 0, high, jnp.where(part == 1, middle, low))


def finish_kernel(parts, out):
    stat = parts[:, :, PAIR:].astype(f32)
    low = lane_low(stat.shape)
    columns = []
    for h in range(2):
        high, middle, rest = (
            stat[:, :, h * DH + p * STAT_LANES : h * DH + p * STAT_LANES + 1] for p in range(3)
        )
        columns.append(high + (middle + rest))
    weight = jnp.where(low, columns[0], columns[1])
    scale = jnp.exp(weight - jnp.max(weight, axis=0, keepdims=True))
    mixed = jnp.sum(parts[:, :, :PAIR].astype(f32) * scale, axis=0) / jnp.sum(scale, axis=0)
    out[...] = jnp.broadcast_to(mixed.astype(bf16)[None], out.shape)


def per_device(tokens, w_qkv, w_out, w_cross, ln_gain, ln_bias, queries):
    seq_index = lax.axis_index("seq")
    span_index = lax.axis_index("span")
    y, x_lo = seq_index // 2, seq_index % 2

    half = ROWS // 2
    peer, up, down = across(tokens), from_below(tokens), from_above(tokens)
    mine = lax.dynamic_slice_in_dim(w_qkv.reshape(32, 3, MODEL), seq_index * PAIR, PAIR, 2)
    mine = mine.reshape(32, 3 * PAIR)
    for bit in SPREAD[:2]:
        mine = spread(mine, bit)
    peer, up, down, mine = lax.optimization_barrier((peer, up, down, mine))
    far_up, far_down = from_below(peer), from_above(peer)
    near = (up, down, from_below(up[:half]), from_above(down[half:]))
    far = (far_up, far_down, across(near[2]), across(near[3]))
    for bit in SPREAD[2:]:
        mine = spread(mine, bit)
    twin = permute(mine, "span", SPAN, lambda i: i ^ 1)

    def whole(shape):
        return pl.BlockSpec(shape, lambda *_: (0,) * len(shape))

    place = jnp.stack([seq_index, span_index]).astype(jnp.int32)
    early_rows = 5 * ROWS
    early, weight = pl.pallas_call(
        project_kernel,
        in_specs=[pl.BlockSpec(memory_space=pltpu.SMEM)] + [pl.BlockSpec(memory_space=pltpu.VMEM)] * 8,
        out_shape=[
            jax.ShapeDtypeStruct((early_rows, 3 * PAIR), bf16),
            jax.ShapeDtypeStruct((MODEL, 3 * PAIR), bf16),
        ],
        compiler_params=params(),
        cost_estimate=pl.CostEstimate(
            flops=2 * early_rows * MODEL * 3 * PAIR, bytes_accessed=4 << 20, transcendentals=0
        ),
    )(place, tokens, peer, *near, mine, twin)

    order = jnp.stack(
        [((y + dy) % 4) * 2 + (x_lo ^ flip) for dy, flip in
         ((0, 0), (0, 1), (3, 0), (1, 0), (2, 0), (3, 1), (1, 1), (2, 1))]
    ).astype(jnp.int32)
    length = SEQ * ROWS
    attn = pl.pallas_call(
        attend_kernel,
        grid_spec=pltpu.PrefetchScalarGridSpec(
            num_scalar_prefetch=1,
            grid=(length // BLOCK,),
            in_specs=[
                whole((early_rows, 3 * PAIR)),
                whole((ROWS, MODEL)),
                whole((ROWS, MODEL)),
                whole((ROWS // 2, MODEL)),
                whole((ROWS // 2, MODEL)),
                whole((MODEL, 3 * PAIR)),
            ],
            out_specs=whole((SEQ, ROWS, PAIR)),
            scratch_shapes=[
                pltpu.VMEM((length, PAIR), bf16),
                pltpu.VMEM((PAIR, length), bf16),
                pltpu.VMEM((length, 2 * PAIR), bf16),
                pltpu.VMEM((BLOCK, length), f32),
                pltpu.VMEM((BLOCK, length), f32),
            ],
        ),
        out_shape=jax.ShapeDtypeStruct((SEQ, ROWS, PAIR), bf16),
        compiler_params=params(),
        cost_estimate=pl.CostEstimate(
            flops=8 * length * length * 2 * PAIR, bytes_accessed=4 << 20,
            transcendentals=2 * length * length,
        ),
    )(order, early, *far, weight)
    attn = lax.all_to_all(attn, "seq", split_axis=0, concat_axis=0, tiled=True)

    encoded, cross_kv = pl.pallas_call(
        encode_kernel,
        out_shape=[
            jax.ShapeDtypeStruct((ROWS, MODEL), bf16),
            jax.ShapeDtypeStruct((SEQ, ROWS, 2 * PAIR), bf16),
        ],
        compiler_params=params(),
        cost_estimate=pl.CostEstimate(
            flops=2 * ROWS * MODEL * 3 * MODEL, bytes_accessed=8 << 20, transcendentals=0
        ),
    )(attn, tokens, w_out, ln_gain[None], ln_bias[None], w_cross)

    kv = lax.all_to_all(cross_kv, "seq", split_axis=0, concat_axis=0, tiled=True)
    kv = kv.reshape(length, 2 * PAIR)

    blocks = NQ // BLOCK
    keep, send = pl.pallas_call(
        cross_kernel,
        grid_spec=pltpu.PrefetchScalarGridSpec(
            num_scalar_prefetch=1,
            grid=(blocks,),
            in_specs=[
                pl.BlockSpec((NQ, PAIR), lambda b, place: (0, place[0])),
                whole((length, 2 * PAIR)),
            ],
            out_specs=[
                pl.BlockSpec((BLOCK // 2, 2 * PAIR), lambda b, place: (b, 0)),
                pl.BlockSpec((BLOCK // 2, 2 * PAIR), lambda b, place: (b, 0)),
            ],
            scratch_shapes=[
                pltpu.VMEM((PAIR, length), bf16),
                pltpu.VMEM((length, 2 * PAIR), bf16),
                pltpu.VMEM((BLOCK, length), f32),
                pltpu.VMEM((BLOCK, length), f32),
            ],
        ),
        out_shape=[jax.ShapeDtypeStruct((NQ // 2, 2 * PAIR), f32)] * 2,
        compiler_params=params(),
        cost_estimate=pl.CostEstimate(
            flops=8 * NQ * length * 2 * PAIR, bytes_accessed=2 << 20,
            transcendentals=2 * NQ * length,
        ),
    )(place, queries, kv)

    received = permute(send, "span", SPAN, lambda i: i ^ 1)
    merged = pl.pallas_call(
        merge_kernel,
        out_shape=jax.ShapeDtypeStruct((NQ // 2, 2 * PAIR), bf16),
        compiler_params=params(),
    )(keep, received)
    parts = lax.all_to_all(
        merged.reshape(16, OWN, 2 * PAIR),
        "span",
        split_axis=0,
        concat_axis=0,
        tiled=True,
        axis_index_groups=[list(range(0, SPAN, 2)), list(range(1, SPAN, 2))],
    )
    mine = pl.pallas_call(
        finish_kernel,
        out_shape=jax.ShapeDtypeStruct((SEQ, OWN, PAIR), bf16),
        compiler_params=params(),
    )(parts)
    heads = lax.all_to_all(mine, "seq", split_axis=0, concat_axis=0, tiled=True)
    cross_out = jnp.transpose(heads, (1, 0, 2)).reshape(OWN, MODEL)
    return encoded, cross_out


def solution(mesh):
    in_specs = (P(("span", "seq"), None), P("span", None), P(), P(), P(), P(), P())
    out_specs = (P(("span", "seq"), None), P("span", None))
    return jax.shard_map(
        per_device, mesh=mesh, in_specs=in_specs, out_specs=out_specs, check_vma=False
    )
```

time: 151 us -> 139 us (0.921)
  blocking collectives: 40.7 us -> 53.6 us
  waiting for transfers between devices: 38.9 us -> 28.3 us
  Pallas kernels: 35.8 us -> 27.3 us
  starting transfers between devices: 30.7 us -> 26.1 us
    all_to_all x0 -> x1, blocking collectives: none -> 14.2 us  [per_device(): lax.all_to_all(cross_kv, 'seq', split_axis=0, concat_axis=0, tiled=True)]
    all_to_all x2 -> x0, waiting for transfers between devices: 12.4 us -> none  [the longest x1 12.4 us: per_device(): lax.all_to_all(cross_kv, 'seq', split_axis=0, concat_axis=0, tiled=True)]
    all_to_all x2 -> x0, starting transfers between devices: 12.3 us -> none  [the longest x1 8.57 us: gather_weight(): lax.all_to_all(jnp.broadcast_to(both[None], (8,) + both.shape), 'span', s...]
    ppermute x12 -> x15, starting transfers between devices: 18.5 us -> 26.1 us  [permute(): return lax.ppermute(x, axis, [(i, target(i)) for i in range(size)])]
    pallas_call x1, Pallas kernels: 18.5 us -> 13.1 us  [per_device(): pl.pallas_call(attend_kernel, grid_spec=pltpu.PrefetchScalarGridSpec(num_...]
    pallas_call x1, Pallas kernels: 9.32 us -> 6.38 us  [per_device(): pl.pallas_call(cross_kernel, grid_spec=pltpu.PrefetchScalarGridSpec(num_s...]
    all_to_all x1, blocking collectives: 20.8 us -> 19 us  [per_device(): lax.all_to_all(merged.reshape(16, OWN, 2 * PAIR), 'span', split_axis=0, c...]
    ppermute x12 -> x15, waiting for transfers between devices: 26.5 us -> 28.3 us  [permute(): return lax.ppermute(x, axis, [(i, target(i)) for i in range(size)])]
  transfers between devices with their start and end apart: 14 -> 15, of which waited for: 8 -> 7; matrix products, arithmetic and copies ran while one was open for 0% -> 1% of each run, Pallas kernels for 1% -> 2%
where the time goes in v2:
time: 139 us; the launch traced here: 138 us
  blocking collectives  53.6 us (39%)
  waiting for transfers between devices  28.3 us (20%)
  Pallas kernels  27.3 us (20%)
  starting transfers between devices  26.1 us (19%)
  local copies, waits for them, and re-layouts  2.08 us (1%)
    ppermute x15, waiting for transfers between devices, permute(): return lax.ppermute(x, axis, [(i, target(i)) for i in range(size)])  28.3 us
    ppermute x15, starting transfers between devices, permute(): return lax.ppermute(x, axis, [(i, target(i)) for i in range(size)])  26.1 us
    all_to_all x1, blocking collectives, per_device(): lax.all_to_all(merged.reshape(16, OWN, 2 * PAIR), 'span', split_axis=0, c...  19 us
    all_to_all x1, blocking collectives, per_device(): lax.all_to_all(cross_kv, 'seq', split_axis=0, concat_axis=0, tiled=True)  14.2 us
    pallas_call x1, Pallas kernels, per_device(): pl.pallas_call(attend_kernel, grid_spec=pltpu.PrefetchScalarGridSpec(num_...  13.1 us
    all_to_all x1, blocking collectives, per_device(): attn = lax.all_to_all(attn, 'seq', split_axis=0, concat_axis=0, tiled=True)  11.7 us
    all_to_all x1, blocking collectives, per_device(): heads = lax.all_to_all(mine, 'seq', split_axis=0, concat_axis=0, tiled=True)  8.72 us
    pallas_call x1, Pallas kernels, per_device(): pl.pallas_call(cross_kernel, grid_spec=pltpu.PrefetchScalarGridSpec(num_s...  6.38 us
  transfers between devices with their start and end apart: 15, of which 7 were waited for; matrix products, arithmetic and copies ran while one was open for 1% of the time, Pallas kernels for 2%

profile of v2, /device:TPU:32, one launch (start us, length us, event | category | flops | bytes accessed | tf_op | source)
XLA Modules:
  0.0 138.2 jit_solution(5121290667738197720)
XLA Ops:
  0.6 1.6 %collective-permute-start = (bf16[256,1024]{1,0:T(8,128)(2,1)}, bf16[256,1024]{1,0:T(8,128)(2,1)S(1)}, u32[]{:S(2)}, u32[]{:S(2)}) collective-permute-start(bf16[256,1024]{1,0:T(8,128)(2,1)} %tokens.1), channel_id=1, source_target_pairs={{0,1},{1,0},{2,3},{3,2},{4,5},{5,4},{6,7},{7,6},{8,9},{9,8},{10,11... | collective-permute-start | bytes 1572872 | tf_op jit(solution)/shard_map/ppermute | solution.py:40
  2.2 1.6 %collective-permute-start.1 = (bf16[256,1024]{1,0:T(8,128)(2,1)}, bf16[256,1024]{1,0:T(8,128)(2,1)S(1)}, u32[]{:S(2)}, u32[]{:S(2)}) collective-permute-start(bf16[256,1024]{1,0:T(8,128)(2,1)} %tokens.1), channel_id=1, source_target_pairs={{0,2},{1,3},{2,4},{3,5},{4,6},{5,7},{6,0},{7,1},{8,10},{9,11},{10,... | collective-permute-start | bytes 1572872 | tf_op jit(solution)/shard_map/ppermute | solution.py:40
  3.8 1.7 %collective-permute-start.2 = (bf16[256,1024]{1,0:T(8,128)(2,1)}, bf16[256,1024]{1,0:T(8,128)(2,1)S(1)}, u32[]{:S(2)}, u32[]{:S(2)}) collective-permute-start(bf16[256,1024]{1,0:T(8,128)(2,1)} %tokens.1), channel_id=1, source_target_pairs={{0,6},{1,7},{2,0},{3,1},{4,2},{5,3},{6,4},{7,5},{8,14},{9,15},{10,... | collective-permute-start | bytes 1572872 | tf_op jit(solution)/shard_map/ppermute | solution.py:40
  5.5 1.2 reshape.19
  6.7 2.8 %collective-permute-start.3 = (bf16[32,384]{1,0:T(8,128)(2,1)S(1)}, bf16[32,384]{1,0:T(8,128)(2,1)S(1)}, u32[]{:S(2)}, u32[]{:S(2)}) collective-permute-start(bf16[32,384]{1,0:T(8,128)(2,1)S(1)} %bitcast.28), channel_id=1, source_target_pairs={{0,128},{8,136},{16,144},{24,152},{32,160},{40,168},{48,176},{56,1... | collective-permute-start | bytes 73736 | tf_op jit(solution)/shard_map/ppermute | solution.py:40
  9.5 7.8 %collective-permute-done.3 = bf16[32,384]{1,0:T(8,128)(2,1)S(1)} collective-permute-done((bf16[32,384]{1,0:T(8,128)(2,1)S(1)}, bf16[32,384]{1,0:T(8,128)(2,1)S(1)}, u32[]{:S(2)}, u32[]{:S(2)}) %collective-permute-start.3) | collective-permute-done | bytes 24608 | tf_op jit(solution)/shard_map/ppermute | solution.py:40
  17.3 6.3 %collective-permute-start.4 = (bf16[64,384]{1,0:T(8,128)(2,1)S(1)}, bf16[64,384]{1,0:T(8,128)(2,1)S(1)}, u32[]{:S(2)}, u32[]{:S(2)}) collective-permute-start(bf16[64,384]{1,0:T(8,128)(2,1)S(1)} %pad_maximum_fusion.2), channel_id=1, source_target_pairs={{0,64},{8,72},{16,80},{24,88},{32,96},{40,104},{48,112},{56,120},{... | collective-permute-start | bytes 147464 | tf_op jit(solution)/shard_map/ppermute | solution.py:40
  23.6 2.6 %collective-permute-done.4 = bf16[64,384]{1,0:T(8,128)(2,1)S(1)} collective-permute-done((bf16[64,384]{1,0:T(8,128)(2,1)S(1)}, bf16[64,384]{1,0:T(8,128)(2,1)S(1)}, u32[]{:S(2)}, u32[]{:S(2)}) %collective-permute-start.4) | collective-permute-done | bytes 49184 | tf_op jit(solution)/shard_map/ppermute | solution.py:40
  26.2 0.0 collective-permute-done.peer
  26.2 0.0 collective-permute-done.1.up
  26.2 0.0 collective-permute-done.2.down
  26.3 2.5 %collective-permute-start.7 = (bf16[128,384]{1,0:T(8,128)(2,1)S(1)}, bf16[128,384]{1,0:T(8,128)(2,1)S(1)}, u32[]{:S(2)}, u32[]{:S(2)}) collective-permute-start(bf16[128,384]{1,0:T(8,128)(2,1)S(1)} %pad_maximum_fusion.1), channel_id=1, source_target_pairs={{0,32},{8,40},{16,48},{24,56},{32,0},{40,8},{48,16},{56,24},{64,96... | collective-permute-start | bytes 294920 | tf_op jit(solution)/shard_map/ppermute | solution.py:40
  28.7 1.6 %collective-permute-start.10 = (bf16[256,1024]{1,0:T(8,128)(2,1)S(1)}, bf16[256,1024]{1,0:T(8,128)(2,1)S(1)}, u32[]{:S(2)}, u32[]{:S(2)}) collective-permute-start(bf16[256,1024]{1,0:T(8,128)(2,1)S(1)} %collective-permute-done.peer), channel_id=1, source_target_pairs={{0,2},{1,3},{2,4},{3,5},{4,6},{5,7},{6,0},{7,1},{8,10},{9,11},{10,... | collective-permute-start | bytes 1572872 | tf_op jit(solution)/shard_map/ppermute | solution.py:40
  30.3 1.7 %collective-permute-start.11 = (bf16[256,1024]{1,0:T(8,128)(2,1)S(1)}, bf16[256,1024]{1,0:T(8,128)(2,1)S(1)}, u32[]{:S(2)}, u32[]{:S(2)}) collective-permute-start(bf16[256,1024]{1,0:T(8,128)(2,1)S(1)} %collective-permute-done.peer), channel_id=1, source_target_pairs={{0,6},{1,7},{2,0},{3,1},{4,2},{5,3},{6,4},{7,5},{8,14},{9,15},{10,... | collective-permute-start | bytes 1572872 | tf_op jit(solution)/shard_map/ppermute | solution.py:40
  32.0 0.4 collective-permute-start.5
  32.5 2.9 %collective-permute-start.6 = (bf16[128,1024]{1,0:T(8,128)(2,1)S(1)}, bf16[128,1024]{1,0:T(8,128)(2,1)}, u32[]{:S(2)}, u32[]{:S(2)}) collective-permute-start(bf16[128,1024]{1,0:T(8,128)(2,1)S(1)} %slice.7), channel_id=1, source_target_pairs={{0,6},{1,7},{2,0},{3,1},{4,2},{5,3},{6,4},{7,5},{8,14},{9,15},{10,... | collective-permute-start | bytes 786440 | tf_op jit(solution)/shard_map/ppermute | solution.py:40
  35.4 0.0 collective-permute-done.7
  35.4 0.8 collective-permute-start.8
  36.3 4.9 %collective-permute-done.8 = bf16[256,384]{1,0:T(8,128)(2,1)S(1)} collective-permute-done((bf16[256,384]{1,0:T(8,128)(2,1)S(1)}, bf16[256,384]{1,0:T(8,128)(2,1)S(1)}, u32[]{:S(2)}, u32[]{:S(2)}) %collective-permute-start.8) | collective-permute-done | bytes 196640 | tf_op jit(solution)/shard_map/ppermute | solution.py:40
  41.2 0.1 collective-permute-start.9
  41.3 5.6 %collective-permute-done.5.up_far = bf16[128,1024]{1,0:T(8,128)(2,1)} collective-permute-done((bf16[128,1024]{1,0:T(8,128)(2,1)S(1)}, bf16[128,1024]{1,0:T(8,128)(2,1)}, u32[]{:S(2)}, u32[]{:S(2)}) %collective-permute-start.5) | collective-permute-done | bytes 262176 | tf_op jit(solution)/shard_map/ppermute | solution.py:40
  46.9 0.5 collective-permute-start.12
  47.4 0.0 collective-permute-done.6.down_far
  47.4 1.5 %collective-permute-start.13 = (bf16[128,1024]{1,0:T(8,128)(2,1)}, bf16[128,1024]{1,0:T(8,128)(2,1)}, u32[]{:S(2)}, u32[]{:S(2)}) collective-permute-start(bf16[128,1024]{1,0:T(8,128)(2,1)} %collective-permute-done.6.down_far), channel_id=1, source_target_pairs={{0,1},{1,0},{2,3},{3,2},{4,5},{5,4},{6,7},{7,6},{8,9},{9,8},{10,11... | collective-permute-start | bytes 786440 | tf_op jit(solution)/shard_map/ppermute | solution.py:40
  48.9 0.1 stack.44.table
  49.0 0.1 pad_add_fusion.place
  49.1 0.0 collective-permute-done.9.twin
  49.1 2.8 %shard_map.86 = (bf16[1280,384]{1,0:T(8,128)(2,1)S(1)}, bf16[1024,384]{1,0:T(8,128)(2,1)S(1)}) custom-call(s32[2]{0:T(128)S(1)} %pad_add_fusion.place, bf16[256,1024]{1,0:T(8,128)(2,1)S(1)} %copy-done.1, bf16[256,1024]{1,0:T(8,128)(2,1)S(1)} %collective-permute-done.peer, bf16[256,1024]{1,0:T(8,128)(2,1)S(1)} %collective-permute-done.1.up, ...), custom_call_target="tpu_custom_call" | custom-call | flops 1006632960 | bytes 4194304 | tf_op jit(solution)/shard_map/pallas_call | solution.py:228
  51.9 2.7 %collective-permute-done.12.up_far = bf16[128,1024]{1,0:T(8,128)(2,1)} collective-permute-done((bf16[128,1024]{1,0:T(8,128)(2,1)}, bf16[128,1024]{1,0:T(8,128)(2,1)}, u32[]{:S(2)}, u32[]{:S(2)}) %collective-permute-start.12) | collective-permute-done | bytes 262176 | tf_op jit(solution)/shard_map/ppermute | solution.py:40
  54.6 2.8 %collective-permute-done.13.down_far = bf16[128,1024]{1,0:T(8,128)(2,1)} collective-permute-done((bf16[128,1024]{1,0:T(8,128)(2,1)}, bf16[128,1024]{1,0:T(8,128)(2,1)}, u32[]{:S(2)}, u32[]{:S(2)}) %collective-permute-start.13) | collective-permute-done | bytes 262176 | tf_op jit(solution)/shard_map/ppermute | solution.py:40
  57.4 0.0 collective-permute-done.10.up
  57.4 0.0 collective-permute-done.11.down
  57.4 0.0 copy-start.2
  57.4 0.0 copy-start.3
  57.4 13.1 %shard_map.87 = bf16[8,256,128]{2,1,0:T(8,128)(2,1)S(1)} custom-call(s32[8]{0:T(128)S(1)} %stack.44.table, bf16[1280,384]{1,0:T(8,128)(2,1)S(1)} %get-tuple-element.16.early, bf16[256,1024]{1,0:T(8,128)(2,1)S(1)} %collective-permute-done.10.up, bf16[256,1024]{1,0:T(8,128)(2,1)S(1)} %collective-permute-done.11.down, ...), custom_call_target="tpu_custom_call" | custom-call | flops 8589934592 | bytes 4194304 | tf_op jit(solution)/shard_map/pallas_call | solution.py:246
  70.5 11.7 %all_to_all.20.attn = bf16[8,256,128]{2,1,0:T(8,128)(2,1)S(1)} all-to-all(bf16[8,256,128]{2,1,0:T(8,128)(2,1)S(1)} %shard_map.87), channel_id=1, replica_groups=mesh['span'=32,'seq'=8] {'seq'}, dimensions={0} | all-to-all | bytes 1048576 | tf_op jit(solution)/shard_map/all_to_all | solution.py:275
  82.2 0.0 copy-done.2
  82.2 4.4 %shard_map.88 = (bf16[256,1024]{1,0:T(8,128)(2,1)}, bf16[8,256,256]{2,1,0:T(8,128)(2,1)S(1)}) custom-call(bf16[8,256,128]{2,1,0:T(8,128)(2,1)S(1)} %all_to_all.20.attn, bf16[256,1024]{1,0:T(8,128)(2,1)S(1)} %copy-done.1, bf16[1024,1024]{1,0:T(8,128)(2,1)S(1)} %copy-done, f32[1,1024]{1,0:T(1,128)S(1)} %bitcast.26, f32[1,1024]{1,0:T(1,128)S(1)} %bitcast.27, ...), custom_call_target="tpu_custom_call" | custom-call | flops 1610612736 | bytes 8388608 | tf_op jit(solution)/shard_map/pallas_call | solution.py:277
  86.6 0.0 copy-start.4
  86.6 14.2 %all_to_all.21 = bf16[8,256,256]{2,1,0:T(8,128)(2,1)S(1)} all-to-all(bf16[8,256,256]{2,1,0:T(8,128)(2,1)S(1)} %get-tuple-element.19), channel_id=1, replica_groups=mesh['span'=32,'seq'=8] {'seq'}, dimensions={0} | all-to-all | bytes 2097152 | tf_op jit(solution)/shard_map/all_to_all | solution.py:289
  100.8 6.4 %shard_map.89 = (f32[512,256]{1,0:T(8,128)S(1)}, f32[512,256]{1,0:T(8,128)S(1)}) custom-call(s32[2]{0:T(128)S(1)} %pad_add_fusion.place, bf16[1024,1024]{1,0:T(8,128)(2,1)S(1)} %copy-done.4, bf16[2048,256]{1,0:T(8,128)(2,1)S(1)} %bitcast.25), custom_call_target="tpu_custom_call" | custom-call | flops 4294967296 | bytes 2097152 | tf_op jit(solution)/shard_map/pallas_call | solution.py:293
  107.2 0.1 collective-permute-start.14
  107.3 1.9 %collective-permute-done.14.received = f32[512,256]{1,0:T(8,128)S(1)} collective-permute-done((f32[512,256]{1,0:T(8,128)S(1)}, f32[512,256]{1,0:T(8,128)S(1)}, u32[]{:S(2)}, u32[]{:S(2)}) %collective-permute-start.14) | collective-permute-done | bytes 524320 | tf_op jit(solution)/shard_map/ppermute | solution.py:40
  109.2 0.2 shard_map.90
  109.4 19.0 %all_to_all.22.parts = bf16[16,32,256]{2,1,0:T(8,128)(2,1)S(1)} all-to-all(bf16[16,32,256]{2,1,0:T(8,128)(2,1)S(1)} %bitcast.24), channel_id=1, replica_groups={{0,16,32,48,64,80,96,112,128,144,160,176,192,208,224,240},{8,24,40,56,7..., dimensions={0} | all-to-all | bytes 524288 | tf_op jit(solution)/shard_map/all_to_all | solution.py:327
  128.4 0.4 shard_map.91
  128.8 8.7 %all_to_all.23 = bf16[8,32,128]{2,1,0:T(8,128)(2,1)S(1)} all-to-all(bf16[8,32,128]{2,1,0:T(8,128)(2,1)S(1)} %shard_map.91), channel_id=1, replica_groups=mesh['span'=32,'seq'=8] {'seq'}, dimensions={0} | all-to-all | bytes 131072 | tf_op jit(solution)/shard_map/all_to_all | solution.py:340
  137.6 0.6 copy_bitcast_fusion
  (16 shorter events, 0.2 us)
Async XLA Ops:
  0.6 48.5 %copy-start.1 = (bf16[256,1024]{1,0:T(8,128)(2,1)S(1)}, bf16[256,1024]{1,0:T(8,128)(2,1)}, u32[]{:S(2)}) copy-start(bf16[256,1024]{1,0:T(8,128)(2,1)} %tokens.1) | copy-start | bytes 1572868
  0.6 25.6 %collective-permute-start = (bf16[256,1024]{1,0:T(8,128)(2,1)}, bf16[256,1024]{1,0:T(8,128)(2,1)S(1)}, u32[]{:S(2)}, u32[]{:S(2)}) collective-permute-start(bf16[256,1024]{1,0:T(8,128)(2,1)} %tokens.1), channel_id=1, source_target_pairs={{0,1},{1,0},{2,3},{3,2},{4,5},{5,4},{6,7},{7,6},{8,9},{9,8},{10,11... | collective-permute-start | bytes 1572872 | tf_op jit(solution)/shard_map/ppermute | solution.py:40
  2.2 24.0 %collective-permute-start.1 = (bf16[256,1024]{1,0:T(8,128)(2,1)}, bf16[256,1024]{1,0:T(8,128)(2,1)S(1)}, u32[]{:S(2)}, u32[]{:S(2)}) collective-permute-start(bf16[256,1024]{1,0:T(8,128)(2,1)} %tokens.1), channel_id=1, source_target_pairs={{0,2},{1,3},{2,4},{3,5},{4,6},{5,7},{6,0},{7,1},{8,10},{9,11},{10,... | collective-permute-start | bytes 1572872 | tf_op jit(solution)/shard_map/ppermute | solution.py:40
  3.8 22.5 %collective-permute-start.2 = (bf16[256,1024]{1,0:T(8,128)(2,1)}, bf16[256,1024]{1,0:T(8,128)(2,1)S(1)}, u32[]{:S(2)}, u32[]{:S(2)}) collective-permute-start(bf16[256,1024]{1,0:T(8,128)(2,1)} %tokens.1), channel_id=1, source_target_pairs={{0,6},{1,7},{2,0},{3,1},{4,2},{5,3},{6,4},{7,5},{8,14},{9,15},{10,... | collective-permute-start | bytes 1572872 | tf_op jit(solution)/shard_map/ppermute | solution.py:40
  6.7 10.6 %collective-permute-start.3 = (bf16[32,384]{1,0:T(8,128)(2,1)S(1)}, bf16[32,384]{1,0:T(8,128)(2,1)S(1)}, u32[]{:S(2)}, u32[]{:S(2)}) collective-permute-start(bf16[32,384]{1,0:T(8,128)(2,1)S(1)} %bitcast.28), channel_id=1, source_target_pairs={{0,128},{8,136},{16,144},{24,152},{32,160},{40,168},{48,176},{56,1... | collective-permute-start | bytes 73736 | tf_op jit(solution)/shard_map/ppermute | solution.py:40
  17.3 8.9 %collective-permute-start.4 = (bf16[64,384]{1,0:T(8,128)(2,1)S(1)}, bf16[64,384]{1,0:T(8,128)(2,1)S(1)}, u32[]{:S(2)}, u32[]{:S(2)}) collective-permute-start(bf16[64,384]{1,0:T(8,128)(2,1)S(1)} %pad_maximum_fusion.2), channel_id=1, source_target_pairs={{0,64},{8,72},{16,80},{24,88},{32,96},{40,104},{48,112},{56,120},{... | collective-permute-start | bytes 147464 | tf_op jit(solution)/shard_map/ppermute | solution.py:40
  26.3 9.1 %collective-permute-start.7 = (bf16[128,384]{1,0:T(8,128)(2,1)S(1)}, bf16[128,384]{1,0:T(8,128)(2,1)S(1)}, u32[]{:S(2)}, u32[]{:S(2)}) collective-permute-start(bf16[128,384]{1,0:T(8,128)(2,1)S(1)} %pad_maximum_fusion.1), channel_id=1, source_target_pairs={{0,32},{8,40},{16,48},{24,56},{32,0},{40,8},{48,16},{56,24},{64,96... | collective-permute-start | bytes 294920 | tf_op jit(solution)/shard_map/ppermute | solution.py:40
  28.7 28.7 %collective-permute-start.10 = (bf16[256,1024]{1,0:T(8,128)(2,1)S(1)}, bf16[256,1024]{1,0:T(8,128)(2,1)S(1)}, u32[]{:S(2)}, u32[]{:S(2)}) collective-permute-start(bf16[256,1024]{1,0:T(8,128)(2,1)S(1)} %collective-permute-done.peer), channel_id=1, source_target_pairs={{0,2},{1,3},{2,4},{3,5},{4,6},{5,7},{6,0},{7,1},{8,10},{9,11},{10,... | collective-permute-start | bytes 1572872 | tf_op jit(solution)/shard_map/ppermute | solution.py:40
  30.3 27.1 %collective-permute-start.11 = (bf16[256,1024]{1,0:T(8,128)(2,1)S(1)}, bf16[256,1024]{1,0:T(8,128)(2,1)S(1)}, u32[]{:S(2)}, u32[]{:S(2)}) collective-permute-start(bf16[256,1024]{1,0:T(8,128)(2,1)S(1)} %collective-permute-done.peer), channel_id=1, source_target_pairs={{0,6},{1,7},{2,0},{3,1},{4,2},{5,3},{6,4},{7,5},{8,14},{9,15},{10,... | collective-permute-start | bytes 1572872 | tf_op jit(solution)/shard_map/ppermute | solution.py:40
  32.0 14.9 %collective-permute-start.5 = (bf16[128,1024]{1,0:T(8,128)(2,1)S(1)}, bf16[128,1024]{1,0:T(8,128)(2,1)}, u32[]{:S(2)}, u32[]{:S(2)}) collective-permute-start(bf16[128,1024]{1,0:T(8,128)(2,1)S(1)} %slice.6), channel_id=1, source_target_pairs={{0,2},{1,3},{2,4},{3,5},{4,6},{5,7},{6,0},{7,1},{8,10},{9,11},{10,... | collective-permute-start | bytes 786440 | tf_op jit(solution)/shard_map/ppermute | solution.py:40
  32.5 15.0 %collective-permute-start.6 = (bf16[128,1024]{1,0:T(8,128)(2,1)S(1)}, bf16[128,1024]{1,0:T(8,128)(2,1)}, u32[]{:S(2)}, u32[]{:S(2)}) collective-permute-start(bf16[128,1024]{1,0:T(8,128)(2,1)S(1)} %slice.7), channel_id=1, source_target_pairs={{0,6},{1,7},{2,0},{3,1},{4,2},{5,3},{6,4},{7,5},{8,14},{9,15},{10,... | collective-permute-start | bytes 786440 | tf_op jit(solution)/shard_map/ppermute | solution.py:40
  35.4 5.8 %collective-permute-start.8 = (bf16[256,384]{1,0:T(8,128)(2,1)S(1)}, bf16[256,384]{1,0:T(8,128)(2,1)S(1)}, u32[]{:S(2)}, u32[]{:S(2)}) collective-permute-start(bf16[256,384]{1,0:T(8,128)(2,1)S(1)} %pad_maximum_fusion), channel_id=1, source_target_pairs={{0,16},{8,24},{16,0},{24,8},{32,48},{40,56},{48,32},{56,40},{64,80... | collective-permute-start | bytes 589832 | tf_op jit(solution)/shard_map/ppermute | solution.py:40
  41.2 7.9 %collective-permute-start.9 = (bf16[512,384]{1,0:T(8,128)(2,1)S(1)}, bf16[512,384]{1,0:T(8,128)(2,1)}, u32[]{:S(2)}, u32[]{:S(2)}) collective-permute-start(bf16[512,384]{1,0:T(8,128)(2,1)S(1)} %constant_dynamic-update-slice_fusion.mine), channel_id=1, source_target_pairs={{0,8},{8,0},{16,24},{24,16},{32,40},{40,32},{48,56},{56,48},{64,72... | collective-permute-start | bytes 1179656 | tf_op jit(solution)/shard_map/ppermute | solution.py:40
  46.9 7.7 %collective-permute-start.12 = (bf16[128,1024]{1,0:T(8,128)(2,1)}, bf16[128,1024]{1,0:T(8,128)(2,1)}, u32[]{:S(2)}, u32[]{:S(2)}) collective-permute-start(bf16[128,1024]{1,0:T(8,128)(2,1)} %collective-permute-done.5.up_far), channel_id=1, source_target_pairs={{0,1},{1,0},{2,3},{3,2},{4,5},{5,4},{6,7},{7,6},{8,9},{9,8},{10,11... | collective-permute-start | bytes 786440 | tf_op jit(solution)/shard_map/ppermute | solution.py:40
  47.4 10.0 %collective-permute-start.13 = (bf16[128,1024]{1,0:T(8,128)(2,1)}, bf16[128,1024]{1,0:T(8,128)(2,1)}, u32[]{:S(2)}, u32[]{:S(2)}) collective-permute-start(bf16[128,1024]{1,0:T(8,128)(2,1)} %collective-permute-done.6.down_far), channel_id=1, source_target_pairs={{0,1},{1,0},{2,3},{3,2},{4,5},{5,4},{6,7},{7,6},{8,9},{9,8},{10,11... | collective-permute-start | bytes 786440 | tf_op jit(solution)/shard_map/ppermute | solution.py:40
  57.4 24.8 %copy-start = (bf16[1024,1024]{1,0:T(8,128)(2,1)S(1)}, bf16[1024,1024]{1,0:T(8,128)(2,1)}, u32[]{:S(2)}) copy-start(bf16[1024,1024]{1,0:T(8,128)(2,1)} %w_out.1) | copy-start | bytes 6291460
  57.4 24.8 %copy-start.2 = (f32[1024]{0:T(1024)S(1)}, f32[1024]{0:T(1024)}, u32[]{:S(2)}) copy-start(f32[1024]{0:T(1024)} %param.11) | copy-start | bytes 12292
  57.4 24.8 %copy-start.3 = (f32[1024]{0:T(1024)S(1)}, f32[1024]{0:T(1024)}, u32[]{:S(2)}) copy-start(f32[1024]{0:T(1024)} %param.12) | copy-start | bytes 12292
  86.6 14.2 %copy-start.4 = (bf16[1024,1024]{1,0:T(8,128)(2,1)S(1)}, bf16[1024,1024]{1,0:T(8,128)(2,1)}, u32[]{:S(2)}) copy-start(bf16[1024,1024]{1,0:T(8,128)(2,1)} %queries.1) | copy-start | bytes 6291460
  107.2 2.0 %collective-permute-start.14 = (f32[512,256]{1,0:T(8,128)S(1)}, f32[512,256]{1,0:T(8,128)S(1)}, u32[]{:S(2)}, u32[]{:S(2)}) collective-permute-start(f32[512,256]{1,0:T(8,128)S(1)} %get-tuple-element.21), channel_id=1, source_target_pairs={{0,8},{8,0},{16,24},{24,16},{32,40},{40,32},{48,56},{56,48},{64,72... | collective-permute-start | bytes 1572872 | tf_op jit(solution)/shard_map/ppermute | solution.py:40

commit v3 on v2

--- a/solution.py
+++ b/solution.py
@@ -19,7 +19,7 @@
 NQ = 1024
 STAT_LANES = 16
 BLOCK = 512
-SPREAD = (16, 8, 4, 2)
+SPREAD = (8, 4, 2, 16)
 score_scale = 0.125
 LOG2E = math.log2(math.e)
 EXP2_SCALE = score_scale * LOG2E
@@ -44,8 +44,9 @@
     return lax.broadcasted_iota(jnp.int32, shape, len(shape) - 1) < DH
 
 
-def spread(blocks, bit):
-    return jnp.concatenate([blocks, permute(blocks, "span", SPAN, lambda i: i ^ bit)])
+def spread(blocks, bits):
+    flips = (bits[0], bits[1], bits[0] | bits[1])
+    return jnp.concatenate([blocks] + [permute(blocks, "span", SPAN, lambda i, f=f: i ^ f) for f in flips])
 
 
 def from_below(x):
@@ -208,16 +209,19 @@
 
     half = ROWS // 2
     peer, up, down = across(tokens), from_below(tokens), from_above(tokens)
-    mine = lax.dynamic_slice_in_dim(w_qkv.reshape(32, 3, MODEL), seq_index * PAIR, PAIR, 2)
-    mine = mine.reshape(32, 3 * PAIR)
-    for bit in SPREAD[:2]:
-        mine = spread(mine, bit)
+    mine = jnp.concatenate(
+        [
+            lax.dynamic_slice_in_dim(w_qkv, part * MODEL + seq_index * PAIR, PAIR, 1)
+            for part in range(3)
+        ],
+        axis=1,
+    )
+    mine = spread(mine, SPREAD[:2])
     peer, up, down, mine = lax.optimization_barrier((peer, up, down, mine))
-    far_up, far_down = from_below(peer), from_above(peer)
     near = (up, down, from_below(up[:half]), from_above(down[half:]))
-    far = (far_up, far_down, across(near[2]), across(near[3]))
-    for bit in SPREAD[2:]:
-        mine = spread(mine, bit)
+    mine = spread(mine, SPREAD[2:])
+    peer, mine = lax.optimization_barrier((peer, mine))
+    far = (from_below(peer), from_above(peer), across(near[2]), across(near[3]))
     twin = permute(mine, "span", SPAN, lambda i: i ^ 1)
 
     def whole(shape):

time: 139 us -> 131 us (0.942)
  waiting for transfers between devices: 28.3 us -> 17.8 us
  starting transfers between devices: 26.1 us -> 29.9 us
    ppermute x15 -> x17, waiting for transfers between devices: 28.3 us -> 17.8 us  [permute(): return lax.ppermute(x, axis, [(i, target(i)) for i in range(size)])]
    ppermute x15 -> x17, starting transfers between devices: 26.1 us -> 29.9 us  [permute(): return lax.ppermute(x, axis, [(i, target(i)) for i in range(size)])]
  transfers between devices with their start and end apart: 15 -> 17, of which waited for: 7 -> 8; matrix products, arithmetic and copies ran while one was open for 1% -> 1% of each run, Pallas kernels for 2% -> 2%
where the time goes in v3:
time: 131 us
  blocking collectives  53.6 us (41%)
  starting transfers between devices  29.9 us (23%)
  Pallas kernels  27.3 us (21%)
  waiting for transfers between devices  17.8 us (14%)
  local copies, waits for them, and re-layouts  1.52 us (1%)
    ppermute x17, starting transfers between devices, permute(): return lax.ppermute(x, axis, [(i, target(i)) for i in range(size)])  29.9 us
    all_to_all x1, blocking collectives, per_device(): lax.all_to_all(merged.reshape(16, OWN, 2 * PAIR), 'span', split_axis=0, c...  19.3 us
    ppermute x17, waiting for transfers between devices, permute(): return lax.ppermute(x, axis, [(i, target(i)) for i in range(size)])  17.8 us
    all_to_all x1, blocking collectives, per_device(): lax.all_to_all(cross_kv, 'seq', split_axis=0, concat_axis=0, tiled=True)  14.4 us
    pallas_call x1, Pallas kernels, per_device(): pl.pallas_call(attend_kernel, grid_spec=pltpu.PrefetchScalarGridSpec(num_...  13.1 us
    all_to_all x1, blocking collectives, per_device(): attn = lax.all_to_all(attn, 'seq', split_axis=0, concat_axis=0, tiled=True)  11.1 us
    all_to_all x1, blocking collectives, per_device(): heads = lax.all_to_all(mine, 'seq', split_axis=0, concat_axis=0, tiled=True)  8.72 us
    pallas_call x1, Pallas kernels, per_device(): pl.pallas_call(cross_kernel, grid_spec=pltpu.PrefetchScalarGridSpec(num_s...  6.38 us
  transfers between devices with their start and end apart: 17, of which 8 were waited for; matrix products, arithmetic and copies ran while one was open for 1% of the time, Pallas kernels for 2%

profile of v3, /device:TPU:32, one launch (start us, length us, event | category | flops | bytes accessed | tf_op | source)
XLA Modules:
  0.0 130.9 jit_solution(15342657603217965491)
XLA Ops:
  0.6 1.6 %collective-permute-start = (bf16[256,1024]{1,0:T(8,128)(2,1)}, bf16[256,1024]{1,0:T(8,128)(2,1)S(1)}, u32[]{:S(2)}, u32[]{:S(2)}) collective-permute-start(bf16[256,1024]{1,0:T(8,128)(2,1)} %tokens.1), channel_id=1, source_target_pairs={{0,1},{1,0},{2,3},{3,2},{4,5},{5,4},{6,7},{7,6},{8,9},{9,8},{10,11... | collective-permute-start | bytes 1572872 | tf_op jit(solution)/shard_map/ppermute | solution.py:40
  2.2 1.6 %collective-permute-start.1 = (bf16[256,1024]{1,0:T(8,128)(2,1)}, bf16[256,1024]{1,0:T(8,128)(2,1)S(1)}, u32[]{:S(2)}, u32[]{:S(2)}) collective-permute-start(bf16[256,1024]{1,0:T(8,128)(2,1)} %tokens.1), channel_id=1, source_target_pairs={{0,2},{1,3},{2,4},{3,5},{4,6},{5,7},{6,0},{7,1},{8,10},{9,11},{10,... | collective-permute-start | bytes 1572872 | tf_op jit(solution)/shard_map/ppermute | solution.py:40
  3.8 1.7 %collective-permute-start.2 = (bf16[256,1024]{1,0:T(8,128)(2,1)}, bf16[256,1024]{1,0:T(8,128)(2,1)S(1)}, u32[]{:S(2)}, u32[]{:S(2)}) collective-permute-start(bf16[256,1024]{1,0:T(8,128)(2,1)} %tokens.1), channel_id=1, source_target_pairs={{0,6},{1,7},{2,0},{3,1},{4,2},{5,3},{6,4},{7,5},{8,14},{9,15},{10,... | collective-permute-start | bytes 1572872 | tf_op jit(solution)/shard_map/ppermute | solution.py:40
  5.5 0.7 constant_dynamic-slice_fusion.2
  6.2 6.4 %collective-permute-start.3 = (bf16[32,384]{1,0:T(8,128)(2,1)S(1)}, bf16[32,384]{1,0:T(8,128)(2,1)S(1)}, u32[]{:S(2)}, u32[]{:S(2)}) collective-permute-start(bf16[32,384]{1,0:T(8,128)(2,1)S(1)} %pad_maximum_fusion.2), channel_id=1, source_target_pairs={{0,64},{8,72},{16,80},{24,88},{32,96},{40,104},{48,112},{56,120},{... | collective-permute-start | bytes 73736 | tf_op jit(solution)/shard_map/ppermute | solution.py:40
  12.6 1.5 %collective-permute-start.4 = (bf16[32,384]{1,0:T(8,128)(2,1)S(1)}, bf16[32,384]{1,0:T(8,128)(2,1)S(1)}, u32[]{:S(2)}, u32[]{:S(2)}) collective-permute-start(bf16[32,384]{1,0:T(8,128)(2,1)S(1)} %pad_maximum_fusion.2), channel_id=1, source_target_pairs={{0,32},{8,40},{16,48},{24,56},{32,0},{40,8},{48,16},{56,24},{64,96... | collective-permute-start | bytes 73736 | tf_op jit(solution)/shard_map/ppermute | solution.py:40
  14.0 0.9 collective-permute-done.3
  14.9 4.5 %collective-permute-start.5 = (bf16[32,384]{1,0:T(8,128)(2,1)S(1)}, bf16[32,384]{1,0:T(8,128)(2,1)S(1)}, u32[]{:S(2)}, u32[]{:S(2)}) collective-permute-start(bf16[32,384]{1,0:T(8,128)(2,1)S(1)} %pad_maximum_fusion.2), channel_id=1, source_target_pairs={{0,96},{8,104},{16,112},{24,120},{32,64},{40,72},{48,80},{56,88},{... | collective-permute-start | bytes 73736 | tf_op jit(solution)/shard_map/ppermute | solution.py:40
  19.4 0.0 collective-permute-done.4
  19.4 1.8 %collective-permute-done.5 = bf16[32,384]{1,0:T(8,128)(2,1)S(1)} collective-permute-done((bf16[32,384]{1,0:T(8,128)(2,1)S(1)}, bf16[32,384]{1,0:T(8,128)(2,1)S(1)}, u32[]{:S(2)}, u32[]{:S(2)}) %collective-permute-start.5) | collective-permute-done | bytes 24608 | tf_op jit(solution)/shard_map/ppermute | solution.py:40
  21.3 0.0 collective-permute-done.peer
  21.3 0.0 collective-permute-done.1.up
  21.3 0.0 collective-permute-done.2.down
  21.3 1.1 collective-permute-start.6
  22.4 2.7 %collective-permute-start.7 = (bf16[128,384]{1,0:T(8,128)(2,1)S(1)}, bf16[128,384]{1,0:T(8,128)(2,1)S(1)}, u32[]{:S(2)}, u32[]{:S(2)}) collective-permute-start(bf16[128,384]{1,0:T(8,128)(2,1)S(1)} %pad_maximum_fusion.1), channel_id=1, source_target_pairs={{0,128},{8,136},{16,144},{24,152},{32,160},{40,168},{48,176},{56,1... | collective-permute-start | bytes 294920 | tf_op jit(solution)/shard_map/ppermute | solution.py:40
  25.1 1.3 collective-permute-start.8
  26.4 2.0 %collective-permute-start.10 = (bf16[128,1024]{1,0:T(8,128)(2,1)S(1)}, bf16[128,1024]{1,0:T(8,128)(2,1)}, u32[]{:S(2)}, u32[]{:S(2)}) collective-permute-start(bf16[128,1024]{1,0:T(8,128)(2,1)S(1)} %slice.7), channel_id=1, source_target_pairs={{0,6},{1,7},{2,0},{3,1},{4,2},{5,3},{6,4},{7,5},{8,14},{9,15},{10,... | collective-permute-start | bytes 786440 | tf_op jit(solution)/shard_map/ppermute | solution.py:40
  28.4 0.2 collective-permute-start.9
  28.6 0.0 collective-permute-done.6
  28.6 0.4 collective-permute-done.7
  29.0 3.1 %collective-permute-done.8 = bf16[128,384]{1,0:T(8,128)(2,1)S(1)} collective-permute-done((bf16[128,384]{1,0:T(8,128)(2,1)S(1)}, bf16[128,384]{1,0:T(8,128)(2,1)S(1)}, u32[]{:S(2)}, u32[]{:S(2)}) %collective-permute-start.8) | collective-permute-done | bytes 98336 | tf_op jit(solution)/shard_map/ppermute | solution.py:40
  32.2 0.4 collective-permute-start.12
  32.6 2.9 %collective-permute-start.13 = (bf16[256,1024]{1,0:T(8,128)(2,1)S(1)}, bf16[256,1024]{1,0:T(8,128)(2,1)S(1)}, u32[]{:S(2)}, u32[]{:S(2)}) collective-permute-start(bf16[256,1024]{1,0:T(8,128)(2,1)S(1)} %collective-permute-done.peer), channel_id=1, source_target_pairs={{0,6},{1,7},{2,0},{3,1},{4,2},{5,3},{6,4},{7,5},{8,14},{9,15},{10,... | collective-permute-start | bytes 1572872 | tf_op jit(solution)/shard_map/ppermute | solution.py:40
  35.5 3.5 %collective-permute-done.9.up_far = bf16[128,1024]{1,0:T(8,128)(2,1)} collective-permute-done((bf16[128,1024]{1,0:T(8,128)(2,1)S(1)}, bf16[128,1024]{1,0:T(8,128)(2,1)}, u32[]{:S(2)}, u32[]{:S(2)}) %collective-permute-start.9) | collective-permute-done | bytes 262176 | tf_op jit(solution)/shard_map/ppermute | solution.py:40
  39.0 0.6 collective-permute-start.14
  39.5 1.5 %collective-permute-start.15 = (bf16[128,1024]{1,0:T(8,128)(2,1)}, bf16[128,1024]{1,0:T(8,128)(2,1)}, u32[]{:S(2)}, u32[]{:S(2)}) collective-permute-start(bf16[128,1024]{1,0:T(8,128)(2,1)} %collective-permute-done.10.down_far), channel_id=1, source_target_pairs={{0,1},{1,0},{2,3},{3,2},{4,5},{5,4},{6,7},{7,6},{8,9},{9,8},{10,11... | collective-permute-start | bytes 786440 | tf_op jit(solution)/shard_map/ppermute | solution.py:40
  41.0 0.1 stack.44.table
  41.1 0.1 pad_add_fusion.place
  41.2 0.0 collective-permute-done.11.twin
  41.2 2.8 %shard_map.86 = (bf16[1280,384]{1,0:T(8,128)(2,1)S(1)}, bf16[1024,384]{1,0:T(8,128)(2,1)S(1)}) custom-call(s32[2]{0:T(128)S(1)} %pad_add_fusion.place, bf16[256,1024]{1,0:T(8,128)(2,1)S(1)} %copy-done.1, bf16[256,1024]{1,0:T(8,128)(2,1)S(1)} %collective-permute-done.peer, bf16[256,1024]{1,0:T(8,128)(2,1)S(1)} %collective-permute-done.1.up, ...), custom_call_target="tpu_custom_call" | custom-call | flops 1006632960 | bytes 4194304 | tf_op jit(solution)/shard_map/pallas_call | solution.py:232
  43.9 3.4 %collective-permute-done.14.up_far = bf16[128,1024]{1,0:T(8,128)(2,1)} collective-permute-done((bf16[128,1024]{1,0:T(8,128)(2,1)}, bf16[128,1024]{1,0:T(8,128)(2,1)}, u32[]{:S(2)}, u32[]{:S(2)}) %collective-permute-start.14) | collective-permute-done | bytes 262176 | tf_op jit(solution)/shard_map/ppermute | solution.py:40
  47.3 2.8 %collective-permute-done.15.down_far = bf16[128,1024]{1,0:T(8,128)(2,1)} collective-permute-done((bf16[128,1024]{1,0:T(8,128)(2,1)}, bf16[128,1024]{1,0:T(8,128)(2,1)}, u32[]{:S(2)}, u32[]{:S(2)}) %collective-permute-start.15) | collective-permute-done | bytes 262176 | tf_op jit(solution)/shard_map/ppermute | solution.py:40
  50.1 0.0 collective-permute-done.13.down
  50.1 0.0 copy-start.2
  50.2 0.0 copy-start.3
  50.2 13.1 %shard_map.87 = bf16[8,256,128]{2,1,0:T(8,128)(2,1)S(1)} custom-call(s32[8]{0:T(128)S(1)} %stack.44.table, bf16[1280,384]{1,0:T(8,128)(2,1)S(1)} %get-tuple-element.20.early, bf16[256,1024]{1,0:T(8,128)(2,1)S(1)} %collective-permute-done.12.up, bf16[256,1024]{1,0:T(8,128)(2,1)S(1)} %collective-permute-done.13.down, ...), custom_call_target="tpu_custom_call" | custom-call | flops 8589934592 | bytes 4194304 | tf_op jit(solution)/shard_map/pallas_call | solution.py:250
  63.2 11.1 %all_to_all.20.attn = bf16[8,256,128]{2,1,0:T(8,128)(2,1)S(1)} all-to-all(bf16[8,256,128]{2,1,0:T(8,128)(2,1)S(1)} %shard_map.87), channel_id=1, replica_groups=mesh['span'=32,'seq'=8] {'seq'}, dimensions={0} | all-to-all | bytes 1048576 | tf_op jit(solution)/shard_map/all_to_all | solution.py:279
  74.4 4.4 %shard_map.88 = (bf16[256,1024]{1,0:T(8,128)(2,1)}, bf16[8,256,256]{2,1,0:T(8,128)(2,1)S(1)}) custom-call(bf16[8,256,128]{2,1,0:T(8,128)(2,1)S(1)} %all_to_all.20.attn, bf16[256,1024]{1,0:T(8,128)(2,1)S(1)} %copy-done.1, bf16[1024,1024]{1,0:T(8,128)(2,1)S(1)} %copy-done, f32[1,1024]{1,0:T(1,128)S(1)} %bitcast.22, f32[1,1024]{1,0:T(1,128)S(1)} %bitcast.23, ...), custom_call_target="tpu_custom_call" | custom-call | flops 1610612736 | bytes 8388608 | tf_op jit(solution)/shard_map/pallas_call | solution.py:281
  78.8 0.0 copy-start.4
  78.8 14.4 %all_to_all.21 = bf16[8,256,256]{2,1,0:T(8,128)(2,1)S(1)} all-to-all(bf16[8,256,256]{2,1,0:T(8,128)(2,1)S(1)} %get-tuple-element.23), channel_id=1, replica_groups=mesh['span'=32,'seq'=8] {'seq'}, dimensions={0} | all-to-all | bytes 2097152 | tf_op jit(solution)/shard_map/all_to_all | solution.py:293
  93.2 6.4 %shard_map.89 = (f32[512,256]{1,0:T(8,128)S(1)}, f32[512,256]{1,0:T(8,128)S(1)}) custom-call(s32[2]{0:T(128)S(1)} %pad_add_fusion.place, bf16[1024,1024]{1,0:T(8,128)(2,1)S(1)} %copy-done.4, bf16[2048,256]{1,0:T(8,128)(2,1)S(1)} %bitcast.21), custom_call_target="tpu_custom_call" | custom-call | flops 4294967296 | bytes 2097152 | tf_op jit(solution)/shard_map/pallas_call | solution.py:297
  99.6 0.1 collective-permute-start.16
  99.7 1.9 %collective-permute-done.16.received = f32[512,256]{1,0:T(8,128)S(1)} collective-permute-done((f32[512,256]{1,0:T(8,128)S(1)}, f32[512,256]{1,0:T(8,128)S(1)}, u32[]{:S(2)}, u32[]{:S(2)}) %collective-permute-start.16) | collective-permute-done | bytes 524320 | tf_op jit(solution)/shard_map/ppermute | solution.py:40
  101.6 0.2 shard_map.90
  101.8 19.3 %all_to_all.22.parts = bf16[16,32,256]{2,1,0:T(8,128)(2,1)S(1)} all-to-all(bf16[16,32,256]{2,1,0:T(8,128)(2,1)S(1)} %bitcast.20), channel_id=1, replica_groups={{0,16,32,48,64,80,96,112,128,144,160,176,192,208,224,240},{8,24,40,56,7..., dimensions={0} | all-to-all | bytes 524288 | tf_op jit(solution)/shard_map/all_to_all | solution.py:331
  121.1 0.4 shard_map.91
  121.5 8.7 %all_to_all.23 = bf16[8,32,128]{2,1,0:T(8,128)(2,1)S(1)} all-to-all(bf16[8,32,128]{2,1,0:T(8,128)(2,1)S(1)} %shard_map.91), channel_id=1, replica_groups=mesh['span'=32,'seq'=8] {'seq'}, dimensions={0} | all-to-all | bytes 131072 | tf_op jit(solution)/shard_map/all_to_all | solution.py:344
  130.3 0.6 copy_bitcast_fusion
  (15 shorter events, 0.1 us)
Async XLA Ops:
  0.6 40.5 %copy-start.1 = (bf16[256,1024]{1,0:T(8,128)(2,1)S(1)}, bf16[256,1024]{1,0:T(8,128)(2,1)}, u32[]{:S(2)}) copy-start(bf16[256,1024]{1,0:T(8,128)(2,1)} %tokens.1) | copy-start | bytes 1572868
  0.6 20.6 %collective-permute-start = (bf16[256,1024]{1,0:T(8,128)(2,1)}, bf16[256,1024]{1,0:T(8,128)(2,1)S(1)}, u32[]{:S(2)}, u32[]{:S(2)}) collective-permute-start(bf16[256,1024]{1,0:T(8,128)(2,1)} %tokens.1), channel_id=1, source_target_pairs={{0,1},{1,0},{2,3},{3,2},{4,5},{5,4},{6,7},{7,6},{8,9},{9,8},{10,11... | collective-permute-start | bytes 1572872 | tf_op jit(solution)/shard_map/ppermute | solution.py:40
  2.2 19.0 %collective-permute-start.1 = (bf16[256,1024]{1,0:T(8,128)(2,1)}, bf16[256,1024]{1,0:T(8,128)(2,1)S(1)}, u32[]{:S(2)}, u32[]{:S(2)}) collective-permute-start(bf16[256,1024]{1,0:T(8,128)(2,1)} %tokens.1), channel_id=1, source_target_pairs={{0,2},{1,3},{2,4},{3,5},{4,6},{5,7},{6,0},{7,1},{8,10},{9,11},{10,... | collective-permute-start | bytes 1572872 | tf_op jit(solution)/shard_map/ppermute | solution.py:40
  3.8 17.5 %collective-permute-start.2 = (bf16[256,1024]{1,0:T(8,128)(2,1)}, bf16[256,1024]{1,0:T(8,128)(2,1)S(1)}, u32[]{:S(2)}, u32[]{:S(2)}) collective-permute-start(bf16[256,1024]{1,0:T(8,128)(2,1)} %tokens.1), channel_id=1, source_target_pairs={{0,6},{1,7},{2,0},{3,1},{4,2},{5,3},{6,4},{7,5},{8,14},{9,15},{10,... | collective-permute-start | bytes 1572872 | tf_op jit(solution)/shard_map/ppermute | solution.py:40
  6.2 8.7 %collective-permute-start.3 = (bf16[32,384]{1,0:T(8,128)(2,1)S(1)}, bf16[32,384]{1,0:T(8,128)(2,1)S(1)}, u32[]{:S(2)}, u32[]{:S(2)}) collective-permute-start(bf16[32,384]{1,0:T(8,128)(2,1)S(1)} %pad_maximum_fusion.2), channel_id=1, source_target_pairs={{0,64},{8,72},{16,80},{24,88},{32,96},{40,104},{48,112},{56,120},{... | collective-permute-start | bytes 73736 | tf_op jit(solution)/shard_map/ppermute | solution.py:40
  12.6 6.8 %collective-permute-start.4 = (bf16[32,384]{1,0:T(8,128)(2,1)S(1)}, bf16[32,384]{1,0:T(8,128)(2,1)S(1)}, u32[]{:S(2)}, u32[]{:S(2)}) collective-permute-start(bf16[32,384]{1,0:T(8,128)(2,1)S(1)} %pad_maximum_fusion.2), channel_id=1, source_target_pairs={{0,32},{8,40},{16,48},{24,56},{32,0},{40,8},{48,16},{56,24},{64,96... | collective-permute-start | bytes 73736 | tf_op jit(solution)/shard_map/ppermute | solution.py:40
  14.9 6.3 %collective-permute-start.5 = (bf16[32,384]{1,0:T(8,128)(2,1)S(1)}, bf16[32,384]{1,0:T(8,128)(2,1)S(1)}, u32[]{:S(2)}, u32[]{:S(2)}) collective-permute-start(bf16[32,384]{1,0:T(8,128)(2,1)S(1)} %pad_maximum_fusion.2), channel_id=1, source_target_pairs={{0,96},{8,104},{16,112},{24,120},{32,64},{40,72},{48,80},{56,88},{... | collective-permute-start | bytes 73736 | tf_op jit(solution)/shard_map/ppermute | solution.py:40
  21.3 7.3 %collective-permute-start.6 = (bf16[128,384]{1,0:T(8,128)(2,1)S(1)}, bf16[128,384]{1,0:T(8,128)(2,1)S(1)}, u32[]{:S(2)}, u32[]{:S(2)}) collective-permute-start(bf16[128,384]{1,0:T(8,128)(2,1)S(1)} %pad_maximum_fusion.1), channel_id=1, source_target_pairs={{0,16},{8,24},{16,0},{24,8},{32,48},{40,56},{48,32},{56,40},{64,80... | collective-permute-start | bytes 294920 | tf_op jit(solution)/shard_map/ppermute | solution.py:40
  22.4 6.6 %collective-permute-start.7 = (bf16[128,384]{1,0:T(8,128)(2,1)S(1)}, bf16[128,384]{1,0:T(8,128)(2,1)S(1)}, u32[]{:S(2)}, u32[]{:S(2)}) collective-permute-start(bf16[128,384]{1,0:T(8,128)(2,1)S(1)} %pad_maximum_fusion.1), channel_id=1, source_target_pairs={{0,128},{8,136},{16,144},{24,152},{32,160},{40,168},{48,176},{56,1... | collective-permute-start | bytes 294920 | tf_op jit(solution)/shard_map/ppermute | solution.py:40
  25.1 7.0 %collective-permute-start.8 = (bf16[128,384]{1,0:T(8,128)(2,1)S(1)}, bf16[128,384]{1,0:T(8,128)(2,1)S(1)}, u32[]{:S(2)}, u32[]{:S(2)}) collective-permute-start(bf16[128,384]{1,0:T(8,128)(2,1)S(1)} %pad_maximum_fusion.1), channel_id=1, source_target_pairs={{0,144},{8,152},{16,128},{24,136},{32,176},{40,184},{48,160},{56,1... | collective-permute-start | bytes 294920 | tf_op jit(solution)/shard_map/ppermute | solution.py:40
  26.4 13.2 %collective-permute-start.10 = (bf16[128,1024]{1,0:T(8,128)(2,1)S(1)}, bf16[128,1024]{1,0:T(8,128)(2,1)}, u32[]{:S(2)}, u32[]{:S(2)}) collective-permute-start(bf16[128,1024]{1,0:T(8,128)(2,1)S(1)} %slice.7), channel_id=1, source_target_pairs={{0,6},{1,7},{2,0},{3,1},{4,2},{5,3},{6,4},{7,5},{8,14},{9,15},{10,... | collective-permute-start | bytes 786440 | tf_op jit(solution)/shard_map/ppermute | solution.py:40
  28.4 10.6 %collective-permute-start.9 = (bf16[128,1024]{1,0:T(8,128)(2,1)S(1)}, bf16[128,1024]{1,0:T(8,128)(2,1)}, u32[]{:S(2)}, u32[]{:S(2)}) collective-permute-start(bf16[128,1024]{1,0:T(8,128)(2,1)S(1)} %slice.6), channel_id=1, source_target_pairs={{0,2},{1,3},{2,4},{3,5},{4,6},{5,7},{6,0},{7,1},{8,10},{9,11},{10,... | collective-permute-start | bytes 786440 | tf_op jit(solution)/shard_map/ppermute | solution.py:40
  32.2 18.0 %collective-permute-start.12 = (bf16[256,1024]{1,0:T(8,128)(2,1)S(1)}, bf16[256,1024]{1,0:T(8,128)(2,1)S(1)}, u32[]{:S(2)}, u32[]{:S(2)}) collective-permute-start(bf16[256,1024]{1,0:T(8,128)(2,1)S(1)} %collective-permute-done.peer), channel_id=1, source_target_pairs={{0,2},{1,3},{2,4},{3,5},{4,6},{5,7},{6,0},{7,1},{8,10},{9,11},{10,... | collective-permute-start | bytes 1572872 | tf_op jit(solution)/shard_map/ppermute | solution.py:40
  32.6 17.5 %collective-permute-start.13 = (bf16[256,1024]{1,0:T(8,128)(2,1)S(1)}, bf16[256,1024]{1,0:T(8,128)(2,1)S(1)}, u32[]{:S(2)}, u32[]{:S(2)}) collective-permute-start(bf16[256,1024]{1,0:T(8,128)(2,1)S(1)} %collective-permute-done.peer), channel_id=1, source_target_pairs={{0,6},{1,7},{2,0},{3,1},{4,2},{5,3},{6,4},{7,5},{8,14},{9,15},{10,... | collective-permute-start | bytes 1572872 | tf_op jit(solution)/shard_map/ppermute | solution.py:40
  35.5 5.7 %collective-permute-start.11 = (bf16[512,384]{1,0:T(8,128)(2,1)S(1)}, bf16[512,384]{1,0:T(8,128)(2,1)}, u32[]{:S(2)}, u32[]{:S(2)}) collective-permute-start(bf16[512,384]{1,0:T(8,128)(2,1)S(1)} %pad_maximum_fusion.mine), channel_id=1, source_target_pairs={{0,8},{8,0},{16,24},{24,16},{32,40},{40,32},{48,56},{56,48},{64,72... | collective-permute-start | bytes 1179656 | tf_op jit(solution)/shard_map/ppermute | solution.py:40
  39.0 8.4 %collective-permute-start.14 = (bf16[128,1024]{1,0:T(8,128)(2,1)}, bf16[128,1024]{1,0:T(8,128)(2,1)}, u32[]{:S(2)}, u32[]{:S(2)}) collective-permute-start(bf16[128,1024]{1,0:T(8,128)(2,1)} %collective-permute-done.9.up_far), channel_id=1, source_target_pairs={{0,1},{1,0},{2,3},{3,2},{4,5},{5,4},{6,7},{7,6},{8,9},{9,8},{10,11... | collective-permute-start | bytes 786440 | tf_op jit(solution)/shard_map/ppermute | solution.py:40
  39.5 10.6 %collective-permute-start.15 = (bf16[128,1024]{1,0:T(8,128)(2,1)}, bf16[128,1024]{1,0:T(8,128)(2,1)}, u32[]{:S(2)}, u32[]{:S(2)}) collective-permute-start(bf16[128,1024]{1,0:T(8,128)(2,1)} %collective-permute-done.10.down_far), channel_id=1, source_target_pairs={{0,1},{1,0},{2,3},{3,2},{4,5},{5,4},{6,7},{7,6},{8,9},{9,8},{10,11... | collective-permute-start | bytes 786440 | tf_op jit(solution)/shard_map/ppermute | solution.py:40
  50.1 24.2 %copy-start = (bf16[1024,1024]{1,0:T(8,128)(2,1)S(1)}, bf16[1024,1024]{1,0:T(8,128)(2,1)}, u32[]{:S(2)}) copy-start(bf16[1024,1024]{1,0:T(8,128)(2,1)} %w_out.1) | copy-start | bytes 6291460
  50.1 24.2 %copy-start.2 = (f32[1024]{0:T(1024)S(1)}, f32[1024]{0:T(1024)}, u32[]{:S(2)}) copy-start(f32[1024]{0:T(1024)} %param.11) | copy-start | bytes 12292
  50.2 24.2 %copy-start.3 = (f32[1024]{0:T(1024)S(1)}, f32[1024]{0:T(1024)}, u32[]{:S(2)}) copy-start(f32[1024]{0:T(1024)} %param.12) | copy-start | bytes 12292
  78.8 14.4 %copy-start.4 = (bf16[1024,1024]{1,0:T(8,128)(2,1)S(1)}, bf16[1024,1024]{1,0:T(8,128)(2,1)}, u32[]{:S(2)}) copy-start(bf16[1024,1024]{1,0:T(8,128)(2,1)} %queries.1) | copy-start | bytes 6291460
  99.6 2.0 %collective-permute-start.16 = (f32[512,256]{1,0:T(8,128)S(1)}, f32[512,256]{1,0:T(8,128)S(1)}, u32[]{:S(2)}, u32[]{:S(2)}) collective-permute-start(f32[512,256]{1,0:T(8,128)S(1)} %get-tuple-element.25), channel_id=1, source_target_pairs={{0,8},{8,0},{16,24},{24,16},{32,40},{40,32},{48,56},{56,48},{64,72... | collective-permute-start | bytes 1572872 | tf_op jit(solution)/shard_map/ppermute | solution.py:40

commit v4 on v3

--- a/solution.py
+++ b/solution.py
@@ -19,7 +19,7 @@
 NQ = 1024
 STAT_LANES = 16
 BLOCK = 512
-SPREAD = (8, 4, 2, 16)
+Z_OFFSETS = (0, -1, 1, -3, -4, -2, 3, 2)
 score_scale = 0.125
 LOG2E = math.log2(math.e)
 EXP2_SCALE = score_scale * LOG2E
@@ -44,9 +44,11 @@
     return lax.broadcasted_iota(jnp.int32, shape, len(shape) - 1) < DH
 
 
-def spread(blocks, bits):
-    flips = (bits[0], bits[1], bits[0] | bits[1])
-    return jnp.concatenate([blocks] + [permute(blocks, "span", SPAN, lambda i, f=f: i ^ f) for f in flips])
+def along_z(blocks, step):
+    def target(i):
+        return (i & 17) | (((i >> 1) - step) % 8) << 1
+
+    return permute(blocks, "span", SPAN, target)
 
 
 def from_below(x):
@@ -62,10 +64,12 @@
 
 
 def project_kernel(place, own, peer, up, down, up_far, down_far, mine, twin, out, w):
-    for k in range(1 << len(SPREAD)):
-        flip = sum(bit for p, bit in enumerate(SPREAD) if k >> p & 1)
-        for core, blocks in enumerate((mine, twin)):
-            start = pl.multiple_of((place[1] ^ (flip + core)) * 32, 32)
+    x_hi, z, side = place[1] // 16, place[1] // 2 % 8, place[1] % 2
+    for k in range(2 * len(Z_OFFSETS)):
+        across_x, offset = k // len(Z_OFFSETS), Z_OFFSETS[k % len(Z_OFFSETS)]
+        for flip, blocks in enumerate((mine, twin)):
+            block = ((x_hi ^ across_x) * 8 + (z + offset + 8) % 8) * 2 + (side ^ flip)
+            start = pl.multiple_of(block * 32, 32)
             w[pl.ds(start, 32), :] = blocks[k * 32 : (k + 1) * 32, :]
     row = 0
     for piece in (own, peer, up, down, up_far, down_far):
@@ -216,12 +220,16 @@
         ],
         axis=1,
     )
-    mine = spread(mine, SPREAD[:2])
+    mine = jnp.concatenate([mine, along_z(mine, -1), along_z(mine, 1)])
     peer, up, down, mine = lax.optimization_barrier((peer, up, down, mine))
-    near = (up, down, from_below(up[:half]), from_above(down[half:]))
-    mine = spread(mine, SPREAD[2:])
-    peer, mine = lax.optimization_barrier((peer, mine))
-    far = (from_below(peer), from_above(peer), across(near[2]), across(near[3]))
+    up_far, down_far = from_below(up[:half]), from_above(down[half:])
+    mine = jnp.concatenate([mine, along_z(mine, -3), along_z(mine[: 2 * 32], 3)])
+    peer, mine, up_far, down_far = lax.optimization_barrier((peer, mine, up_far, down_far))
+    near = (up, down, up_far, down_far)
+    side = (across(up_far), across(down_far))
+    mine = jnp.concatenate([mine, permute(mine, "span", SPAN, lambda i: i ^ 16)])
+    mine, *side = lax.optimization_barrier((mine, *side))
+    far = (from_below(peer), from_above(peer), *side)
     twin = permute(mine, "span", SPAN, lambda i: i ^ 1)
 
     def whole(shape):

time: 131 us -> 142 us (1.084)
  waiting for transfers between devices: 17.8 us -> 28.8 us
  starting transfers between devices: 29.9 us -> 22.9 us
  blocking collectives: 53.6 us -> 58.2 us
  local copies, waits for them, and re-layouts: 1.52 us -> 4.86 us
    ppermute x17 -> x16, waiting for transfers between devices: 17.8 us -> 28.8 us  [permute(): return lax.ppermute(x, axis, [(i, target(i)) for i in range(size)])]
    ppermute x17 -> x16, starting transfers between devices: 29.9 us -> 22.9 us  [permute(): return lax.ppermute(x, axis, [(i, target(i)) for i in range(size)])]
    all_to_all x1, blocking collectives: 11.1 us -> 15 us  [per_device(): attn = lax.all_to_all(attn, 'seq', split_axis=0, concat_axis=0, tiled=True)]
    all_to_all x1, blocking collectives: 14.4 us -> 17.9 us  [per_device(): lax.all_to_all(cross_kv, 'seq', split_axis=0, concat_axis=0, tiled=True)]
    unnamed x10 -> x26, local copies, waits for them, and re-layouts: 0.03 us -> 3.36 us
    all_to_all x1, blocking collectives: 19.3 us -> 16.7 us  [per_device(): lax.all_to_all(merged.reshape(16, OWN, 2 * PAIR), 'span', split_axis=0, c...]
  transfers between devices with their start and end apart: 17 -> 16, of which waited for: 8 -> 10; matrix products, arithmetic and copies ran while one was open for 1% -> 1% of each run, Pallas kernels for 2% -> 2%
where the time goes in v4:
time: 142 us
  blocking collectives  58.2 us (41%)
  waiting for transfers between devices  28.8 us (20%)
  Pallas kernels  26.1 us (18%)
  starting transfers between devices  22.9 us (16%)
  local copies, waits for them, and re-layouts  4.86 us (3%)
    ppermute x16, waiting for transfers between devices, permute(): return lax.ppermute(x, axis, [(i, target(i)) for i in range(size)])  28.8 us
    ppermute x16, starting transfers between devices, permute(): return lax.ppermute(x, axis, [(i, target(i)) for i in range(size)])  22.9 us
    all_to_all x1, blocking collectives, per_device(): lax.all_to_all(cross_kv, 'seq', split_axis=0, concat_axis=0, tiled=True)  17.9 us
    all_to_all x1, blocking collectives, per_device(): lax.all_to_all(merged.reshape(16, OWN, 2 * PAIR), 'span', split_axis=0, c...  16.7 us
    all_to_all x1, blocking collectives, per_device(): attn = lax.all_to_all(attn, 'seq', split_axis=0, concat_axis=0, tiled=True)  15 us
    pallas_call x1, Pallas kernels, per_device(): pl.pallas_call(attend_kernel, grid_spec=pltpu.PrefetchScalarGridSpec(num_...  11.9 us
    all_to_all x1, blocking collectives, per_device(): heads = lax.all_to_all(mine, 'seq', split_axis=0, concat_axis=0, tiled=True)  8.72 us
    pallas_call x1, Pallas kernels, per_device(): pl.pallas_call(cross_kernel, grid_spec=pltpu.PrefetchScalarGridSpec(num_s...  6.38 us
  transfers between devices with their start and end apart: 16, of which 10 were waited for; matrix products, arithmetic and copies ran while one was open for 1% of the time, Pallas kernels for 2%

profile of v4, /device:TPU:32, one launch (start us, length us, event | category | flops | bytes accessed | tf_op | source)
XLA Modules:
  0.0 141.8 jit_solution(4017801387274550340)
XLA Ops:
  0.6 3.1 %collective-permute-start.2 = (bf16[256,1024]{1,0:T(8,128)(2,1)}, bf16[256,1024]{1,0:T(8,128)(2,1)S(1)}, u32[]{:S(2)}, u32[]{:S(2)}) collective-permute-start(bf16[256,1024]{1,0:T(8,128)(2,1)} %tokens.1), channel_id=1, source_target_pairs={{0,6},{1,7},{2,0},{3,1},{4,2},{5,3},{6,4},{7,5},{8,14},{9,15},{10,... | collective-permute-start | bytes 1572872 | tf_op jit(solution)/shard_map/ppermute | solution.py:40
  3.7 0.0 collective-permute-start.1
  3.7 1.5 %collective-permute-start = (bf16[256,1024]{1,0:T(8,128)(2,1)}, bf16[256,1024]{1,0:T(8,128)(2,1)S(1)}, u32[]{:S(2)}, u32[]{:S(2)}) collective-permute-start(bf16[256,1024]{1,0:T(8,128)(2,1)} %tokens.1), channel_id=1, source_target_pairs={{0,1},{1,0},{2,3},{3,2},{4,5},{5,4},{6,7},{7,6},{8,9},{9,8},{10,11... | collective-permute-start | bytes 1572872 | tf_op jit(solution)/shard_map/ppermute | solution.py:40
  5.2 0.7 constant_dynamic-slice_fusion.2
  6.0 0.2 collective-permute-start.4
  6.1 1.9 %collective-permute-start.3 = (bf16[32,384]{1,0:T(8,128)(2,1)S(1)}, bf16[32,384]{1,0:T(8,128)(2,1)S(1)}, u32[]{:S(2)}, u32[]{:S(2)}) collective-permute-start(bf16[32,384]{1,0:T(8,128)(2,1)S(1)} %pad_maximum_fusion.3), channel_id=1, source_target_pairs={{0,16},{8,24},{16,32},{24,40},{32,48},{40,56},{48,64},{56,72},{64,... | collective-permute-start | bytes 73736 | tf_op jit(solution)/shard_map/ppermute | solution.py:40
  8.1 1.8 %collective-permute-done.4 = bf16[32,384]{1,0:T(8,128)(2,1)S(1)} collective-permute-done((bf16[32,384]{1,0:T(8,128)(2,1)S(1)}, bf16[32,384]{1,0:T(8,128)(2,1)S(1)}, u32[]{:S(2)}, u32[]{:S(2)}) %collective-permute-start.4) | collective-permute-done | bytes 24608 | tf_op jit(solution)/shard_map/ppermute | solution.py:40
  9.9 3.9 %collective-permute-done.3 = bf16[32,384]{1,0:T(8,128)(2,1)S(1)} collective-permute-done((bf16[32,384]{1,0:T(8,128)(2,1)S(1)}, bf16[32,384]{1,0:T(8,128)(2,1)S(1)}, u32[]{:S(2)}, u32[]{:S(2)}) %collective-permute-start.3) | collective-permute-done | bytes 24608 | tf_op jit(solution)/shard_map/ppermute | solution.py:40
  13.8 1.4 collective-permute-done.2.down
  15.2 3.3 %collective-permute-done.1.up = bf16[256,1024]{1,0:T(8,128)(2,1)S(1)} collective-permute-done((bf16[256,1024]{1,0:T(8,128)(2,1)}, bf16[256,1024]{1,0:T(8,128)(2,1)S(1)}, u32[]{:S(2)}, u32[]{:S(2)}) %collective-permute-start.1) | collective-permute-done | bytes 524320 | tf_op jit(solution)/shard_map/ppermute | solution.py:40
  18.6 1.8 %collective-permute-start.8 = (bf16[128,1024]{1,0:T(8,128)(2,1)S(1)}, bf16[128,1024]{1,0:T(8,128)(2,1)S(1)}, u32[]{:S(2)}, u32[]{:S(2)}) collective-permute-start(bf16[128,1024]{1,0:T(8,128)(2,1)S(1)} %slice.11), channel_id=1, source_target_pairs={{0,6},{1,7},{2,0},{3,1},{4,2},{5,3},{6,4},{7,5},{8,14},{9,15},{10,... | collective-permute-start | bytes 786440 | tf_op jit(solution)/shard_map/ppermute | solution.py:40
  20.4 0.3 collective-permute-start.7
  20.7 5.8 %collective-permute-start.5 = (bf16[96,384]{1,0:T(8,128)(2,1)S(1)}, bf16[96,384]{1,0:T(8,128)(2,1)S(1)}, u32[]{:S(2)}, u32[]{:S(2)}) collective-permute-start(bf16[96,384]{1,0:T(8,128)(2,1)S(1)} %pad_maximum_fusion.2), channel_id=1, source_target_pairs={{0,48},{8,56},{16,64},{24,72},{32,80},{40,88},{48,96},{56,104},{64... | collective-permute-start | bytes 221192 | tf_op jit(solution)/shard_map/ppermute | solution.py:40
  26.5 0.1 collective-permute-start.6
  26.6 7.0 %collective-permute-done.6 = bf16[64,384]{1,0:T(8,128)(2,1)S(1)} collective-permute-done((bf16[64,384]{1,0:T(8,128)(2,1)S(1)}, bf16[64,384]{1,0:T(8,128)(2,1)S(1)}, u32[]{:S(2)}, u32[]{:S(2)}) %collective-permute-start.6) | collective-permute-done | bytes 49184 | tf_op jit(solution)/shard_map/ppermute | solution.py:40
  33.7 0.0 copy-start.7
  33.7 3.1 %collective-permute-start.9 = (bf16[256,384]{1,0:T(8,128)(2,1)S(1)}, bf16[256,384]{1,0:T(8,128)(2,1)S(1)}, u32[]{:S(2)}, u32[]{:S(2)}) collective-permute-start(bf16[256,384]{1,0:T(8,128)(2,1)S(1)} %pad_maximum_fusion.1), channel_id=1, source_target_pairs={{0,128},{8,136},{16,144},{24,152},{32,160},{40,168},{48,176},{56,1... | collective-permute-start | bytes 589832 | tf_op jit(solution)/shard_map/ppermute | solution.py:40
  36.8 0.6 collective-permute-start.10
  37.4 1.4 %collective-permute-start.11 = (bf16[128,1024]{1,0:T(8,128)(2,1)S(1)}, bf16[128,1024]{1,0:T(8,128)(2,1)S(1)}, u32[]{:S(2)}, u32[]{:S(2)}) collective-permute-start(bf16[128,1024]{1,0:T(8,128)(2,1)S(1)} %collective-permute-done.8.down_far), channel_id=1, source_target_pairs={{0,1},{1,0},{2,3},{3,2},{4,5},{5,4},{6,7},{7,6},{8,9},{9,8},{10,11... | collective-permute-start | bytes 786440 | tf_op jit(solution)/shard_map/ppermute | solution.py:40
  38.9 3.0 %collective-permute-start.14 = (bf16[256,1024]{1,0:T(8,128)(2,1)S(1)}, bf16[256,1024]{1,0:T(8,128)(2,1)S(1)}, u32[]{:S(2)}, u32[]{:S(2)}) collective-permute-start(bf16[256,1024]{1,0:T(8,128)(2,1)S(1)} %collective-permute-done.peer), channel_id=1, source_target_pairs={{0,6},{1,7},{2,0},{3,1},{4,2},{5,3},{6,4},{7,5},{8,14},{9,15},{10,... | collective-permute-start | bytes 1572872 | tf_op jit(solution)/shard_map/ppermute | solution.py:40
  41.8 1.3 collective-permute-done.9
  43.2 4.3 %collective-permute-done.10.up_far = bf16[128,1024]{1,0:T(8,128)(2,1)S(1)} collective-permute-done((bf16[128,1024]{1,0:T(8,128)(2,1)S(1)}, bf16[128,1024]{1,0:T(8,128)(2,1)S(1)}, u32[]{:S(2)}, u32[]{:S(2)}) %collective-permute-start.10) | collective-permute-done | bytes 262176 | tf_op jit(solution)/shard_map/ppermute | solution.py:40
  47.5 0.7 copy-done.9
  48.2 2.1 %collective-permute-done.11.down_far = bf16[128,1024]{1,0:T(8,128)(2,1)S(1)} collective-permute-done((bf16[128,1024]{1,0:T(8,128)(2,1)S(1)}, bf16[128,1024]{1,0:T(8,128)(2,1)S(1)}, u32[]{:S(2)}, u32[]{:S(2)}) %collective-permute-start.11) | collective-permute-done | bytes 262176 | tf_op jit(solution)/shard_map/ppermute | solution.py:40
  50.3 0.7 copy-done.11
  51.0 0.0 collective-permute-start.12
  51.0 0.1 stack.44.table
  51.1 0.1 pad_add_fusion.place
  51.2 1.7 %collective-permute-done.12.twin = bf16[512,384]{1,0:T(8,128)(2,1)} collective-permute-done((bf16[512,384]{1,0:T(8,128)(2,1)S(1)}, bf16[512,384]{1,0:T(8,128)(2,1)}, u32[]{:S(2)}, u32[]{:S(2)}) %collective-permute-start.12) | collective-permute-done | bytes 393248 | tf_op jit(solution)/shard_map/ppermute | solution.py:40
  52.9 0.9 copy-done.6
  53.8 0.9 copy-done.8
  54.8 2.7 %shard_map.86 = (bf16[1280,384]{1,0:T(8,128)(2,1)S(1)}, bf16[1024,384]{1,0:T(8,128)(2,1)S(1)}) custom-call(s32[2]{0:T(128)S(1)} %pad_add_fusion.place, bf16[256,1024]{1,0:T(8,128)(2,1)S(1)} %copy-done.1, bf16[256,1024]{1,0:T(8,128)(2,1)S(1)} %collective-permute-done.peer, bf16[256,1024]{1,0:T(8,128)(2,1)S(1)} %collective-permute-done.1.up, ...), custom_call_target="tpu_custom_call" | custom-call | flops 1006632960 | bytes 4194304 | tf_op jit(solution)/shard_map/pallas_call | solution.py:240
  57.5 0.0 copy-start
  57.5 0.0 copy-start.2
  57.5 0.0 copy-start.3
  57.5 11.9 %shard_map.87 = bf16[8,256,128]{2,1,0:T(8,128)(2,1)S(1)} custom-call(s32[8]{0:T(128)S(1)} %stack.44.table, bf16[1280,384]{1,0:T(8,128)(2,1)S(1)} %get-tuple-element.28.early, bf16[256,1024]{1,0:T(8,128)(2,1)S(1)} %collective-permute-done.13.up, bf16[256,1024]{1,0:T(8,128)(2,1)S(1)} %collective-permute-done.14.down, bf16[128,1024]{1,0:T(8,128)(2,1)S(1)} %copy-done.10, ...), custom_call_target="tpu_custom_call" | custom-call | flops 8589934592 | bytes 4194304 | tf_op jit(solution)/shard_map/pallas_call | solution.py:258
  69.5 15.0 %all_to_all.20.attn = bf16[8,256,128]{2,1,0:T(8,128)(2,1)S(1)} all-to-all(bf16[8,256,128]{2,1,0:T(8,128)(2,1)S(1)} %shard_map.87), channel_id=1, replica_groups=mesh['span'=32,'seq'=8] {'seq'}, dimensions={0} | all-to-all | bytes 1048576 | tf_op jit(solution)/shard_map/all_to_all | solution.py:287
  84.5 4.4 %shard_map.88 = (bf16[256,1024]{1,0:T(8,128)(2,1)}, bf16[8,256,256]{2,1,0:T(8,128)(2,1)S(1)}) custom-call(bf16[8,256,128]{2,1,0:T(8,128)(2,1)S(1)} %all_to_all.20.attn, bf16[256,1024]{1,0:T(8,128)(2,1)S(1)} %copy-done.1, bf16[1024,1024]{1,0:T(8,128)(2,1)S(1)} %copy-done, f32[1,1024]{1,0:T(1,128)S(1)} %bitcast.22, f32[1,1024]{1,0:T(1,128)S(1)} %bitcast.23, ...), custom_call_target="tpu_custom_call" | custom-call | flops 1610612736 | bytes 8388608 | tf_op jit(solution)/shard_map/pallas_call | solution.py:289
  88.9 0.0 copy-start.4
  88.9 17.9 %all_to_all.21 = bf16[8,256,256]{2,1,0:T(8,128)(2,1)S(1)} all-to-all(bf16[8,256,256]{2,1,0:T(8,128)(2,1)S(1)} %get-tuple-element.33), channel_id=1, replica_groups=mesh['span'=32,'seq'=8] {'seq'}, dimensions={0} | all-to-all | bytes 2097152 | tf_op jit(solution)/shard_map/all_to_all | solution.py:301
  106.8 6.4 %shard_map.89 = (f32[512,256]{1,0:T(8,128)S(1)}, f32[512,256]{1,0:T(8,128)S(1)}) custom-call(s32[2]{0:T(128)S(1)} %pad_add_fusion.place, bf16[1024,1024]{1,0:T(8,128)(2,1)S(1)} %copy-done.4, bf16[2048,256]{1,0:T(8,128)(2,1)S(1)} %bitcast.21), custom_call_target="tpu_custom_call" | custom-call | flops 4294967296 | bytes 2097152 | tf_op jit(solution)/shard_map/pallas_call | solution.py:305
  113.2 0.1 collective-permute-start.15
  113.3 1.9 %collective-permute-done.15.received = f32[512,256]{1,0:T(8,128)S(1)} collective-permute-done((f32[512,256]{1,0:T(8,128)S(1)}, f32[512,256]{1,0:T(8,128)S(1)}, u32[]{:S(2)}, u32[]{:S(2)}) %collective-permute-start.15) | collective-permute-done | bytes 524320 | tf_op jit(solution)/shard_map/ppermute | solution.py:40
  115.2 0.2 shard_map.90
  115.4 16.7 %all_to_all.22.parts = bf16[16,32,256]{2,1,0:T(8,128)(2,1)S(1)} all-to-all(bf16[16,32,256]{2,1,0:T(8,128)(2,1)S(1)} %bitcast.20), channel_id=1, replica_groups={{0,16,32,48,64,80,96,112,128,144,160,176,192,208,224,240},{8,24,40,56,7..., dimensions={0} | all-to-all | bytes 524288 | tf_op jit(solution)/shard_map/all_to_all | solution.py:339
  132.1 0.4 shard_map.91
  132.5 8.7 %all_to_all.23 = bf16[8,32,128]{2,1,0:T(8,128)(2,1)S(1)} all-to-all(bf16[8,32,128]{2,1,0:T(8,128)(2,1)S(1)} %shard_map.91), channel_id=1, replica_groups=mesh['span'=32,'seq'=8] {'seq'}, dimensions={0} | all-to-all | bytes 131072 | tf_op jit(solution)/shard_map/all_to_all | solution.py:352
  141.2 0.6 copy_bitcast_fusion
  (31 shorter events, 0.2 us)
Async XLA Ops:
  0.6 52.2 %copy-start.1 = (bf16[256,1024]{1,0:T(8,128)(2,1)S(1)}, bf16[256,1024]{1,0:T(8,128)(2,1)}, u32[]{:S(2)}) copy-start(bf16[256,1024]{1,0:T(8,128)(2,1)} %tokens.1) | copy-start | bytes 1572868
  0.6 14.6 %collective-permute-start.2 = (bf16[256,1024]{1,0:T(8,128)(2,1)}, bf16[256,1024]{1,0:T(8,128)(2,1)S(1)}, u32[]{:S(2)}, u32[]{:S(2)}) collective-permute-start(bf16[256,1024]{1,0:T(8,128)(2,1)} %tokens.1), channel_id=1, source_target_pairs={{0,6},{1,7},{2,0},{3,1},{4,2},{5,3},{6,4},{7,5},{8,14},{9,15},{10,... | collective-permute-start | bytes 1572872 | tf_op jit(solution)/shard_map/ppermute | solution.py:40
  3.7 14.8 %collective-permute-start.1 = (bf16[256,1024]{1,0:T(8,128)(2,1)}, bf16[256,1024]{1,0:T(8,128)(2,1)S(1)}, u32[]{:S(2)}, u32[]{:S(2)}) collective-permute-start(bf16[256,1024]{1,0:T(8,128)(2,1)} %tokens.1), channel_id=1, source_target_pairs={{0,2},{1,3},{2,4},{3,5},{4,6},{5,7},{6,0},{7,1},{8,10},{9,11},{10,... | collective-permute-start | bytes 1572872 | tf_op jit(solution)/shard_map/ppermute | solution.py:40
  3.7 14.8 %collective-permute-start = (bf16[256,1024]{1,0:T(8,128)(2,1)}, bf16[256,1024]{1,0:T(8,128)(2,1)S(1)}, u32[]{:S(2)}, u32[]{:S(2)}) collective-permute-start(bf16[256,1024]{1,0:T(8,128)(2,1)} %tokens.1), channel_id=1, source_target_pairs={{0,1},{1,0},{2,3},{3,2},{4,5},{5,4},{6,7},{7,6},{8,9},{9,8},{10,11... | collective-permute-start | bytes 1572872 | tf_op jit(solution)/shard_map/ppermute | solution.py:40
  6.0 3.9 %collective-permute-start.4 = (bf16[32,384]{1,0:T(8,128)(2,1)S(1)}, bf16[32,384]{1,0:T(8,128)(2,1)S(1)}, u32[]{:S(2)}, u32[]{:S(2)}) collective-permute-start(bf16[32,384]{1,0:T(8,128)(2,1)S(1)} %pad_maximum_fusion.3), channel_id=1, source_target_pairs={{0,112},{8,120},{16,0},{24,8},{32,16},{40,24},{48,32},{56,40},{64,... | collective-permute-start | bytes 73736 | tf_op jit(solution)/shard_map/ppermute | solution.py:40
  6.1 7.7 %collective-permute-start.3 = (bf16[32,384]{1,0:T(8,128)(2,1)S(1)}, bf16[32,384]{1,0:T(8,128)(2,1)S(1)}, u32[]{:S(2)}, u32[]{:S(2)}) collective-permute-start(bf16[32,384]{1,0:T(8,128)(2,1)S(1)} %pad_maximum_fusion.3), channel_id=1, source_target_pairs={{0,16},{8,24},{16,32},{24,40},{32,48},{40,56},{48,64},{56,72},{64,... | collective-permute-start | bytes 73736 | tf_op jit(solution)/shard_map/ppermute | solution.py:40
  18.6 15.1 %collective-permute-start.8 = (bf16[128,1024]{1,0:T(8,128)(2,1)S(1)}, bf16[128,1024]{1,0:T(8,128)(2,1)S(1)}, u32[]{:S(2)}, u32[]{:S(2)}) collective-permute-start(bf16[128,1024]{1,0:T(8,128)(2,1)S(1)} %slice.11), channel_id=1, source_target_pairs={{0,6},{1,7},{2,0},{3,1},{4,2},{5,3},{6,4},{7,5},{8,14},{9,15},{10,... | collective-permute-start | bytes 786440 | tf_op jit(solution)/shard_map/ppermute | solution.py:40
  20.4 13.3 %collective-permute-start.7 = (bf16[128,1024]{1,0:T(8,128)(2,1)S(1)}, bf16[128,1024]{1,0:T(8,128)(2,1)S(1)}, u32[]{:S(2)}, u32[]{:S(2)}) collective-permute-start(bf16[128,1024]{1,0:T(8,128)(2,1)S(1)} %slice.10), channel_id=1, source_target_pairs={{0,2},{1,3},{2,4},{3,5},{4,6},{5,7},{6,0},{7,1},{8,10},{9,11},{10,... | collective-permute-start | bytes 786440 | tf_op jit(solution)/shard_map/ppermute | solution.py:40
  20.7 13.0 %collective-permute-start.5 = (bf16[96,384]{1,0:T(8,128)(2,1)S(1)}, bf16[96,384]{1,0:T(8,128)(2,1)S(1)}, u32[]{:S(2)}, u32[]{:S(2)}) collective-permute-start(bf16[96,384]{1,0:T(8,128)(2,1)S(1)} %pad_maximum_fusion.2), channel_id=1, source_target_pairs={{0,48},{8,56},{16,64},{24,72},{32,80},{40,88},{48,96},{56,104},{64... | collective-permute-start | bytes 221192 | tf_op jit(solution)/shard_map/ppermute | solution.py:40
  26.5 7.1 %collective-permute-start.6 = (bf16[64,384]{1,0:T(8,128)(2,1)S(1)}, bf16[64,384]{1,0:T(8,128)(2,1)S(1)}, u32[]{:S(2)}, u32[]{:S(2)}) collective-permute-start(bf16[64,384]{1,0:T(8,128)(2,1)S(1)} %slice.9), channel_id=1, source_target_pairs={{0,80},{8,88},{16,96},{24,104},{32,112},{40,120},{48,0},{56,8},{64... | collective-permute-start | bytes 147464 | tf_op jit(solution)/shard_map/ppermute | solution.py:40
  33.7 13.8 %copy-start.5 = (bf16[128,1024]{1,0:T(8,128)(2,1)}, bf16[128,1024]{1,0:T(8,128)(2,1)S(1)}, u32[]{:S(2)}) copy-start(bf16[128,1024]{1,0:T(8,128)(2,1)S(1)} %collective-permute-done.8.down_far) | copy-start | bytes 786436
  33.7 16.6 %copy-start.7 = (bf16[128,1024]{1,0:T(8,128)(2,1)}, bf16[128,1024]{1,0:T(8,128)(2,1)S(1)}, u32[]{:S(2)}) copy-start(bf16[128,1024]{1,0:T(8,128)(2,1)S(1)} %collective-permute-done.7.up_far) | copy-start | bytes 786436
  33.7 9.4 %collective-permute-start.9 = (bf16[256,384]{1,0:T(8,128)(2,1)S(1)}, bf16[256,384]{1,0:T(8,128)(2,1)S(1)}, u32[]{:S(2)}, u32[]{:S(2)}) collective-permute-start(bf16[256,384]{1,0:T(8,128)(2,1)S(1)} %pad_maximum_fusion.1), channel_id=1, source_target_pairs={{0,128},{8,136},{16,144},{24,152},{32,160},{40,168},{48,176},{56,1... | collective-permute-start | bytes 589832 | tf_op jit(solution)/shard_map/ppermute | solution.py:40
  36.8 10.6 %collective-permute-start.10 = (bf16[128,1024]{1,0:T(8,128)(2,1)S(1)}, bf16[128,1024]{1,0:T(8,128)(2,1)S(1)}, u32[]{:S(2)}, u32[]{:S(2)}) collective-permute-start(bf16[128,1024]{1,0:T(8,128)(2,1)S(1)} %collective-permute-done.7.up_far), channel_id=1, source_target_pairs={{0,1},{1,0},{2,3},{3,2},{4,5},{5,4},{6,7},{7,6},{8,9},{9,8},{10,11... | collective-permute-start | bytes 786440 | tf_op jit(solution)/shard_map/ppermute | solution.py:40
  37.4 12.9 %collective-permute-start.11 = (bf16[128,1024]{1,0:T(8,128)(2,1)S(1)}, bf16[128,1024]{1,0:T(8,128)(2,1)S(1)}, u32[]{:S(2)}, u32[]{:S(2)}) collective-permute-start(bf16[128,1024]{1,0:T(8,128)(2,1)S(1)} %collective-permute-done.8.down_far), channel_id=1, source_target_pairs={{0,1},{1,0},{2,3},{3,2},{4,5},{5,4},{6,7},{7,6},{8,9},{9,8},{10,11... | collective-permute-start | bytes 786440 | tf_op jit(solution)/shard_map/ppermute | solution.py:40
  38.9 18.6 %collective-permute-start.14 = (bf16[256,1024]{1,0:T(8,128)(2,1)S(1)}, bf16[256,1024]{1,0:T(8,128)(2,1)S(1)}, u32[]{:S(2)}, u32[]{:S(2)}) collective-permute-start(bf16[256,1024]{1,0:T(8,128)(2,1)S(1)} %collective-permute-done.peer), channel_id=1, source_target_pairs={{0,6},{1,7},{2,0},{3,1},{4,2},{5,3},{6,4},{7,5},{8,14},{9,15},{10,... | collective-permute-start | bytes 1572872 | tf_op jit(solution)/shard_map/ppermute | solution.py:40
  41.8 15.7 %collective-permute-start.13 = (bf16[256,1024]{1,0:T(8,128)(2,1)S(1)}, bf16[256,1024]{1,0:T(8,128)(2,1)S(1)}, u32[]{:S(2)}, u32[]{:S(2)}) collective-permute-start(bf16[256,1024]{1,0:T(8,128)(2,1)S(1)} %collective-permute-done.peer), channel_id=1, source_target_pairs={{0,2},{1,3},{2,4},{3,5},{4,6},{5,7},{6,0},{7,1},{8,10},{9,11},{10,... | collective-permute-start | bytes 1572872 | tf_op jit(solution)/shard_map/ppermute | solution.py:40
  47.5 0.7 copy-start.9
  50.3 0.7 copy-start.11
  51.0 1.9 %collective-permute-start.12 = (bf16[512,384]{1,0:T(8,128)(2,1)S(1)}, bf16[512,384]{1,0:T(8,128)(2,1)}, u32[]{:S(2)}, u32[]{:S(2)}) collective-permute-start(bf16[512,384]{1,0:T(8,128)(2,1)S(1)} %pad_maximum_fusion.mine), channel_id=1, source_target_pairs={{0,8},{8,0},{16,24},{24,16},{32,40},{40,32},{48,56},{56,48},{64,72... | collective-permute-start | bytes 1179656 | tf_op jit(solution)/shard_map/ppermute | solution.py:40
  52.9 1.0 copy-start.6
  53.8 0.9 copy-start.8
  54.8 2.7 %copy-start.10 = (bf16[128,1024]{1,0:T(8,128)(2,1)S(1)}, bf16[128,1024]{1,0:T(8,128)(2,1)}, u32[]{:S(2)}) copy-start(bf16[128,1024]{1,0:T(8,128)(2,1)} %copy-done.9) | copy-start | bytes 786436
  54.8 2.7 %copy-start.12 = (bf16[128,1024]{1,0:T(8,128)(2,1)S(1)}, bf16[128,1024]{1,0:T(8,128)(2,1)}, u32[]{:S(2)}) copy-start(bf16[128,1024]{1,0:T(8,128)(2,1)} %copy-done.11) | copy-start | bytes 786436
  57.5 27.0 %copy-start = (bf16[1024,1024]{1,0:T(8,128)(2,1)S(1)}, bf16[1024,1024]{1,0:T(8,128)(2,1)}, u32[]{:S(2)}) copy-start(bf16[1024,1024]{1,0:T(8,128)(2,1)} %w_out.1) | copy-start | bytes 6291460
  57.5 27.0 %copy-start.2 = (f32[1024]{0:T(1024)S(1)}, f32[1024]{0:T(1024)}, u32[]{:S(2)}) copy-start(f32[1024]{0:T(1024)} %param.11) | copy-start | bytes 12292
  57.5 27.0 %copy-start.3 = (f32[1024]{0:T(1024)S(1)}, f32[1024]{0:T(1024)}, u32[]{:S(2)}) copy-start(f32[1024]{0:T(1024)} %param.12) | copy-start | bytes 12292
  88.9 17.9 %copy-start.4 = (bf16[1024,1024]{1,0:T(8,128)(2,1)S(1)}, bf16[1024,1024]{1,0:T(8,128)(2,1)}, u32[]{:S(2)}) copy-start(bf16[1024,1024]{1,0:T(8,128)(2,1)} %queries.1) | copy-start | bytes 6291460
  113.2 2.0 %collective-permute-start.15 = (f32[512,256]{1,0:T(8,128)S(1)}, f32[512,256]{1,0:T(8,128)S(1)}, u32[]{:S(2)}, u32[]{:S(2)}) collective-permute-start(f32[512,256]{1,0:T(8,128)S(1)} %get-tuple-element.35), channel_id=1, source_target_pairs={{0,8},{8,0},{16,24},{24,16},{32,40},{40,32},{48,56},{56,48},{64,72... | collective-permute-start | bytes 1572872 | tf_op jit(solution)/shard_map/ppermute | solution.py:40

commit v5 on v3

--- a/solution.py
+++ b/solution.py
@@ -19,7 +19,6 @@
 NQ = 1024
 STAT_LANES = 16
 BLOCK = 512
-SPREAD = (8, 4, 2, 16)
 score_scale = 0.125
 LOG2E = math.log2(math.e)
 EXP2_SCALE = score_scale * LOG2E
@@ -44,9 +43,19 @@
     return lax.broadcasted_iota(jnp.int32, shape, len(shape) - 1) < DH
 
 
-def spread(blocks, bits):
-    flips = (bits[0], bits[1], bits[0] | bits[1])
-    return jnp.concatenate([blocks] + [permute(blocks, "span", SPAN, lambda i, f=f: i ^ f) for f in flips])
+def along_z(block):
+    groups = {}
+    for i in range(SPAN):
+        groups.setdefault((i // 16, i % 2), []).append(i)
+    ring = lax.all_to_all(
+        jnp.broadcast_to(block[None], (8,) + block.shape),
+        "span",
+        split_axis=0,
+        concat_axis=0,
+        tiled=True,
+        axis_index_groups=list(groups.values()),
+    )
+    return ring.reshape(8 * block.shape[0], block.shape[1])
 
 
 def from_below(x):
@@ -62,10 +71,10 @@
 
 
 def project_kernel(place, own, peer, up, down, up_far, down_far, mine, twin, out, w):
-    for k in range(1 << len(SPREAD)):
-        flip = sum(bit for p, bit in enumerate(SPREAD) if k >> p & 1)
+    for k in range(16):
         for core, blocks in enumerate((mine, twin)):
-            start = pl.multiple_of((place[1] ^ (flip + core)) * 32, 32)
+            block = (place[1] & 17) ^ (k // 8 * 16 + core) | k % 8 * 2
+            start = pl.multiple_of(block * 32, 32)
             w[pl.ds(start, 32), :] = blocks[k * 32 : (k + 1) * 32, :]
     row = 0
     for piece in (own, peer, up, down, up_far, down_far):
@@ -216,12 +225,13 @@
         ],
         axis=1,
     )
-    mine = spread(mine, SPREAD[:2])
+    mine = along_z(mine)
     peer, up, down, mine = lax.optimization_barrier((peer, up, down, mine))
-    near = (up, down, from_below(up[:half]), from_above(down[half:]))
-    mine = spread(mine, SPREAD[2:])
-    peer, mine = lax.optimization_barrier((peer, mine))
-    far = (from_below(peer), from_above(peer), across(near[2]), across(near[3]))
+    up_far, down_far = from_below(up[:half]), from_above(down[half:])
+    mine = jnp.concatenate([mine, permute(mine, "span", SPAN, lambda i: i ^ 16)])
+    peer, mine, up_far, down_far = lax.optimization_barrier((peer, mine, up_far, down_far))
+    near = (up, down, up_far, down_far)
+    far = (from_below(peer), from_above(peer), across(up_far), across(down_far))
     twin = permute(mine, "span", SPAN, lambda i: i ^ 1)
 
     def whole(shape):

time: 131 us -> 135 us (1.031)
  blocking collectives: 53.6 us -> 72.3 us
  starting transfers between devices: 29.9 us -> 16.5 us
  waiting for transfers between devices: 17.8 us -> 15.9 us
    all_to_all x0 -> x1, blocking collectives: none -> 16.7 us  [along_z(): lax.all_to_all(jnp.broadcast_to(block[None], (8,) + block.shape), 'span',...]
    ppermute x17 -> x12, starting transfers between devices: 29.9 us -> 16.5 us  [permute(): return lax.ppermute(x, axis, [(i, target(i)) for i in range(size)])]
    all_to_all x1, blocking collectives: 14.4 us -> 17.3 us  [per_device(): lax.all_to_all(cross_kv, 'seq', split_axis=0, concat_axis=0, tiled=True)]
    all_to_all x1, blocking collectives: 19.3 us -> 16.5 us  [per_device(): lax.all_to_all(merged.reshape(16, OWN, 2 * PAIR), 'span', split_axis=0, c...]
    all_to_all x1, blocking collectives: 11.1 us -> 13.1 us  [per_device(): attn = lax.all_to_all(attn, 'seq', split_axis=0, concat_axis=0, tiled=True)]
    ppermute x17 -> x12, waiting for transfers between devices: 17.8 us -> 15.9 us  [permute(): return lax.ppermute(x, axis, [(i, target(i)) for i in range(size)])]
  transfers between devices with their start and end apart: 17 -> 12, of which waited for: 8 -> 5; matrix products, arithmetic and copies ran while one was open for 1% -> 1% of each run, Pallas kernels for 2% -> 2%
where the time goes in v5:
time: 135 us; the launch traced here: 134 us
  blocking collectives  72.3 us (54%)
  Pallas kernels  27.3 us (20%)
  starting transfers between devices  16.5 us (12%)
  waiting for transfers between devices  15.9 us (12%)
  local copies, waits for them, and re-layouts  1.54 us (1%)
    all_to_all x1, blocking collectives, per_device(): lax.all_to_all(cross_kv, 'seq', split_axis=0, concat_axis=0, tiled=True)  17.3 us
    all_to_all x1, blocking collectives, along_z(): lax.all_to_all(jnp.broadcast_to(block[None], (8,) + block.shape), 'span',...  16.7 us
    ppermute x12, starting transfers between devices, permute(): return lax.ppermute(x, axis, [(i, target(i)) for i in range(size)])  16.5 us
    all_to_all x1, blocking collectives, per_device(): lax.all_to_all(merged.reshape(16, OWN, 2 * PAIR), 'span', split_axis=0, c...  16.5 us
    ppermute x12, waiting for transfers between devices, permute(): return lax.ppermute(x, axis, [(i, target(i)) for i in range(size)])  15.9 us
    all_to_all x1, blocking collectives, per_device(): attn = lax.all_to_all(attn, 'seq', split_axis=0, concat_axis=0, tiled=True)  13.1 us
    pallas_call x1, Pallas kernels, per_device(): pl.pallas_call(attend_kernel, grid_spec=pltpu.PrefetchScalarGridSpec(num_...  13.1 us
    all_to_all x1, blocking collectives, per_device(): heads = lax.all_to_all(mine, 'seq', split_axis=0, concat_axis=0, tiled=True)  8.72 us
  transfers between devices with their start and end apart: 12, of which 5 were waited for; matrix products, arithmetic and copies ran while one was open for 1% of the time, Pallas kernels for 2%

profile of v5, /device:TPU:32, one launch (start us, length us, event | category | flops | bytes accessed | tf_op | source)
XLA Modules:
  0.0 134.4 jit_solution(12935353891969750913)
XLA Ops:
  0.6 0.0 copy-start.1
  0.6 1.6 %collective-permute-start = (bf16[256,1024]{1,0:T(8,128)(2,1)}, bf16[256,1024]{1,0:T(8,128)(2,1)S(1)}, u32[]{:S(2)}, u32[]{:S(2)}) collective-permute-start(bf16[256,1024]{1,0:T(8,128)(2,1)} %tokens.1), channel_id=1, source_target_pairs={{0,1},{1,0},{2,3},{3,2},{4,5},{5,4},{6,7},{7,6},{8,9},{9,8},{10,11... | collective-permute-start | bytes 1572872 | tf_op jit(solution)/shard_map/ppermute | solution.py:39
  2.2 1.6 %collective-permute-start.1 = (bf16[256,1024]{1,0:T(8,128)(2,1)}, bf16[256,1024]{1,0:T(8,128)(2,1)S(1)}, u32[]{:S(2)}, u32[]{:S(2)}) collective-permute-start(bf16[256,1024]{1,0:T(8,128)(2,1)} %tokens.1), channel_id=1, source_target_pairs={{0,2},{1,3},{2,4},{3,5},{4,6},{5,7},{6,0},{7,1},{8,10},{9,11},{10,... | collective-permute-start | bytes 1572872 | tf_op jit(solution)/shard_map/ppermute | solution.py:39
  3.8 1.7 %collective-permute-start.2 = (bf16[256,1024]{1,0:T(8,128)(2,1)}, bf16[256,1024]{1,0:T(8,128)(2,1)S(1)}, u32[]{:S(2)}, u32[]{:S(2)}) collective-permute-start(bf16[256,1024]{1,0:T(8,128)(2,1)} %tokens.1), channel_id=1, source_target_pairs={{0,6},{1,7},{2,0},{3,1},{4,2},{5,3},{6,4},{7,5},{8,14},{9,15},{10,... | collective-permute-start | bytes 1572872 | tf_op jit(solution)/shard_map/ppermute | solution.py:39
  5.5 0.7 constant_dynamic-slice_fusion.2
  6.2 16.7 %all_to_all.25 = bf16[8,32,384]{2,1,0:T(8,128)(2,1)S(1)} all-to-all(bf16[8,32,384]{2,1,0:T(8,128)(2,1)S(1)} %broadcast_in_dim.12), channel_id=1, replica_groups={{0,16,32,48,64,80,96,112},{8,24,40,56,72,88,104,120},{128,144,160,176,1..., dimensions={0} | all-to-all | bytes 393216 | tf_op jit(solution)/shard_map/all_to_all | solution.py:50
  22.9 0.0 collective-permute-done.peer
  22.9 0.0 collective-permute-done.1.up
  22.9 0.0 collective-permute-done.2.down
  22.9 2.8 %collective-permute-start.3 = (bf16[256,384]{1,0:T(8,128)(2,1)S(1)}, bf16[256,384]{1,0:T(8,128)(2,1)S(1)}, u32[]{:S(2)}, u32[]{:S(2)}) collective-permute-start(bf16[256,384]{1,0:T(8,128)(2,1)S(1)} %bitcast.25), channel_id=1, source_target_pairs={{0,128},{8,136},{16,144},{24,152},{32,160},{40,168},{48,176},{56,1... | collective-permute-start | bytes 589832 | tf_op jit(solution)/shard_map/ppermute | solution.py:39
  25.8 0.4 collective-permute-start.4
  26.2 3.0 %collective-permute-start.5 = (bf16[128,1024]{1,0:T(8,128)(2,1)S(1)}, bf16[128,1024]{1,0:T(8,128)(2,1)}, u32[]{:S(2)}, u32[]{:S(2)}) collective-permute-start(bf16[128,1024]{1,0:T(8,128)(2,1)S(1)} %slice.7), channel_id=1, source_target_pairs={{0,6},{1,7},{2,0},{3,1},{4,2},{5,3},{6,4},{7,5},{8,14},{9,15},{10,... | collective-permute-start | bytes 786440 | tf_op jit(solution)/shard_map/ppermute | solution.py:39
  29.2 1.0 collective-permute-done.3
  30.2 3.3 %collective-permute-done.4.up_far = bf16[128,1024]{1,0:T(8,128)(2,1)} collective-permute-done((bf16[128,1024]{1,0:T(8,128)(2,1)S(1)}, bf16[128,1024]{1,0:T(8,128)(2,1)}, u32[]{:S(2)}, u32[]{:S(2)}) %collective-permute-start.4) | collective-permute-done | bytes 262176 | tf_op jit(solution)/shard_map/ppermute | solution.py:39
  33.5 0.0 collective-permute-done.5.down_far
  33.5 0.8 collective-permute-start.7
  34.4 2.6 %collective-permute-start.8 = (bf16[256,1024]{1,0:T(8,128)(2,1)S(1)}, bf16[256,1024]{1,0:T(8,128)(2,1)S(1)}, u32[]{:S(2)}, u32[]{:S(2)}) collective-permute-start(bf16[256,1024]{1,0:T(8,128)(2,1)S(1)} %collective-permute-done.peer), channel_id=1, source_target_pairs={{0,6},{1,7},{2,0},{3,1},{4,2},{5,3},{6,4},{7,5},{8,14},{9,15},{10,... | collective-permute-start | bytes 1572872 | tf_op jit(solution)/shard_map/ppermute | solution.py:39
  36.9 0.0 collective-permute-start.6
  36.9 0.3 collective-permute-start.10
  37.2 1.7 %collective-permute-start.9 = (bf16[128,1024]{1,0:T(8,128)(2,1)}, bf16[128,1024]{1,0:T(8,128)(2,1)}, u32[]{:S(2)}, u32[]{:S(2)}) collective-permute-start(bf16[128,1024]{1,0:T(8,128)(2,1)} %collective-permute-done.4.up_far), channel_id=1, source_target_pairs={{0,1},{1,0},{2,3},{3,2},{4,5},{5,4},{6,7},{7,6},{8,9},{9,8},{10,11... | collective-permute-start | bytes 786440 | tf_op jit(solution)/shard_map/ppermute | solution.py:39
  39.0 0.1 stack.44.table
  39.0 0.1 pad_add_fusion.place
  39.1 0.0 collective-permute-done.6.twin
  39.1 0.0 copy-done.1
  39.1 2.8 %shard_map.86 = (bf16[1280,384]{1,0:T(8,128)(2,1)S(1)}, bf16[1024,384]{1,0:T(8,128)(2,1)S(1)}) custom-call(s32[2]{0:T(128)S(1)} %pad_add_fusion.place, bf16[256,1024]{1,0:T(8,128)(2,1)S(1)} %copy-done.1, bf16[256,1024]{1,0:T(8,128)(2,1)S(1)} %collective-permute-done.peer, bf16[256,1024]{1,0:T(8,128)(2,1)S(1)} %collective-permute-done.1.up, ...), custom_call_target="tpu_custom_call" | custom-call | flops 1006632960 | bytes 4194304 | tf_op jit(solution)/shard_map/pallas_call | solution.py:242
  41.9 4.4 %collective-permute-done.10.down_far = bf16[128,1024]{1,0:T(8,128)(2,1)} collective-permute-done((bf16[128,1024]{1,0:T(8,128)(2,1)}, bf16[128,1024]{1,0:T(8,128)(2,1)}, u32[]{:S(2)}, u32[]{:S(2)}) %collective-permute-start.10) | collective-permute-done | bytes 262176 | tf_op jit(solution)/shard_map/ppermute | solution.py:39
  46.4 5.2 %collective-permute-done.9.up_far = bf16[128,1024]{1,0:T(8,128)(2,1)} collective-permute-done((bf16[128,1024]{1,0:T(8,128)(2,1)}, bf16[128,1024]{1,0:T(8,128)(2,1)}, u32[]{:S(2)}, u32[]{:S(2)}) %collective-permute-start.9) | collective-permute-done | bytes 262176 | tf_op jit(solution)/shard_map/ppermute | solution.py:39
  51.6 0.0 collective-permute-done.7.up
  51.6 0.0 collective-permute-done.8.down
  51.6 0.0 copy-start.2
  51.6 0.0 copy-start.3
  51.6 13.1 %shard_map.87 = bf16[8,256,128]{2,1,0:T(8,128)(2,1)S(1)} custom-call(s32[8]{0:T(128)S(1)} %stack.44.table, bf16[1280,384]{1,0:T(8,128)(2,1)S(1)} %get-tuple-element.24.early, bf16[256,1024]{1,0:T(8,128)(2,1)S(1)} %collective-permute-done.7.up, bf16[256,1024]{1,0:T(8,128)(2,1)S(1)} %collective-permute-done.8.down, ...), custom_call_target="tpu_custom_call" | custom-call | flops 8589934592 | bytes 4194304 | tf_op jit(solution)/shard_map/pallas_call | solution.py:260
  64.7 13.1 %all_to_all.26.attn = bf16[8,256,128]{2,1,0:T(8,128)(2,1)S(1)} all-to-all(bf16[8,256,128]{2,1,0:T(8,128)(2,1)S(1)} %shard_map.87), channel_id=1, replica_groups=mesh['span'=32,'seq'=8] {'seq'}, dimensions={0} | all-to-all | bytes 1048576 | tf_op jit(solution)/shard_map/all_to_all | solution.py:289
  77.8 0.0 copy-done
  77.8 0.0 copy-done.2
  77.8 0.0 copy-done.3
  77.8 4.4 %shard_map.88 = (bf16[256,1024]{1,0:T(8,128)(2,1)}, bf16[8,256,256]{2,1,0:T(8,128)(2,1)S(1)}) custom-call(bf16[8,256,128]{2,1,0:T(8,128)(2,1)S(1)} %all_to_all.26.attn, bf16[256,1024]{1,0:T(8,128)(2,1)S(1)} %copy-done.1, bf16[1024,1024]{1,0:T(8,128)(2,1)S(1)} %copy-done, f32[1,1024]{1,0:T(1,128)S(1)} %bitcast.23, f32[1,1024]{1,0:T(1,128)S(1)} %bitcast.24, ...), custom_call_target="tpu_custom_call" | custom-call | flops 1610612736 | bytes 8388608 | tf_op jit(solution)/shard_map/pallas_call | solution.py:291
  82.2 0.0 copy-start.4
  82.2 17.3 %all_to_all.27 = bf16[8,256,256]{2,1,0:T(8,128)(2,1)S(1)} all-to-all(bf16[8,256,256]{2,1,0:T(8,128)(2,1)S(1)} %get-tuple-element.27), channel_id=1, replica_groups=mesh['span'=32,'seq'=8] {'seq'}, dimensions={0} | all-to-all | bytes 2097152 | tf_op jit(solution)/shard_map/all_to_all | solution.py:303
  99.6 0.0 copy-done.4
  99.6 6.4 %shard_map.89 = (f32[512,256]{1,0:T(8,128)S(1)}, f32[512,256]{1,0:T(8,128)S(1)}) custom-call(s32[2]{0:T(128)S(1)} %pad_add_fusion.place, bf16[1024,1024]{1,0:T(8,128)(2,1)S(1)} %copy-done.4, bf16[2048,256]{1,0:T(8,128)(2,1)S(1)} %bitcast.22), custom_call_target="tpu_custom_call" | custom-call | flops 4294967296 | bytes 2097152 | tf_op jit(solution)/shard_map/pallas_call | solution.py:307
  105.9 0.1 collective-permute-start.11
  106.0 1.9 %collective-permute-done.11.received = f32[512,256]{1,0:T(8,128)S(1)} collective-permute-done((f32[512,256]{1,0:T(8,128)S(1)}, f32[512,256]{1,0:T(8,128)S(1)}, u32[]{:S(2)}, u32[]{:S(2)}) %collective-permute-start.11) | collective-permute-done | bytes 524320 | tf_op jit(solution)/shard_map/ppermute | solution.py:39
  107.9 0.2 shard_map.90
  108.2 16.5 %all_to_all.28.parts = bf16[16,32,256]{2,1,0:T(8,128)(2,1)S(1)} all-to-all(bf16[16,32,256]{2,1,0:T(8,128)(2,1)S(1)} %bitcast.21), channel_id=1, replica_groups={{0,16,32,48,64,80,96,112,128,144,160,176,192,208,224,240},{8,24,40,56,7..., dimensions={0} | all-to-all | bytes 524288 | tf_op jit(solution)/shard_map/all_to_all | solution.py:341
  124.6 0.4 shard_map.91
  125.0 8.7 %all_to_all.29 = bf16[8,32,128]{2,1,0:T(8,128)(2,1)S(1)} all-to-all(bf16[8,32,128]{2,1,0:T(8,128)(2,1)S(1)} %shard_map.91), channel_id=1, replica_groups=mesh['span'=32,'seq'=8] {'seq'}, dimensions={0} | all-to-all | bytes 131072 | tf_op jit(solution)/shard_map/all_to_all | solution.py:354
  133.8 0.6 copy_bitcast_fusion
  (6 shorter events, 0.1 us)
Async XLA Ops:
  0.6 38.5 %copy-start.1 = (bf16[256,1024]{1,0:T(8,128)(2,1)S(1)}, bf16[256,1024]{1,0:T(8,128)(2,1)}, u32[]{:S(2)}) copy-start(bf16[256,1024]{1,0:T(8,128)(2,1)} %tokens.1) | copy-start | bytes 1572868
  0.6 22.3 %collective-permute-start = (bf16[256,1024]{1,0:T(8,128)(2,1)}, bf16[256,1024]{1,0:T(8,128)(2,1)S(1)}, u32[]{:S(2)}, u32[]{:S(2)}) collective-permute-start(bf16[256,1024]{1,0:T(8,128)(2,1)} %tokens.1), channel_id=1, source_target_pairs={{0,1},{1,0},{2,3},{3,2},{4,5},{5,4},{6,7},{7,6},{8,9},{9,8},{10,11... | collective-permute-start | bytes 1572872 | tf_op jit(solution)/shard_map/ppermute | solution.py:39
  2.2 20.7 %collective-permute-start.1 = (bf16[256,1024]{1,0:T(8,128)(2,1)}, bf16[256,1024]{1,0:T(8,128)(2,1)S(1)}, u32[]{:S(2)}, u32[]{:S(2)}) collective-permute-start(bf16[256,1024]{1,0:T(8,128)(2,1)} %tokens.1), channel_id=1, source_target_pairs={{0,2},{1,3},{2,4},{3,5},{4,6},{5,7},{6,0},{7,1},{8,10},{9,11},{10,... | collective-permute-start | bytes 1572872 | tf_op jit(solution)/shard_map/ppermute | solution.py:39
  3.8 19.1 %collective-permute-start.2 = (bf16[256,1024]{1,0:T(8,128)(2,1)}, bf16[256,1024]{1,0:T(8,128)(2,1)S(1)}, u32[]{:S(2)}, u32[]{:S(2)}) collective-permute-start(bf16[256,1024]{1,0:T(8,128)(2,1)} %tokens.1), channel_id=1, source_target_pairs={{0,6},{1,7},{2,0},{3,1},{4,2},{5,3},{6,4},{7,5},{8,14},{9,15},{10,... | collective-permute-start | bytes 1572872 | tf_op jit(solution)/shard_map/ppermute | solution.py:39
  22.9 7.3 %collective-permute-start.3 = (bf16[256,384]{1,0:T(8,128)(2,1)S(1)}, bf16[256,384]{1,0:T(8,128)(2,1)S(1)}, u32[]{:S(2)}, u32[]{:S(2)}) collective-permute-start(bf16[256,384]{1,0:T(8,128)(2,1)S(1)} %bitcast.25), channel_id=1, source_target_pairs={{0,128},{8,136},{16,144},{24,152},{32,160},{40,168},{48,176},{56,1... | collective-permute-start | bytes 589832 | tf_op jit(solution)/shard_map/ppermute | solution.py:39
  25.8 7.8 %collective-permute-start.4 = (bf16[128,1024]{1,0:T(8,128)(2,1)S(1)}, bf16[128,1024]{1,0:T(8,128)(2,1)}, u32[]{:S(2)}, u32[]{:S(2)}) collective-permute-start(bf16[128,1024]{1,0:T(8,128)(2,1)S(1)} %slice.6), channel_id=1, source_target_pairs={{0,2},{1,3},{2,4},{3,5},{4,6},{5,7},{6,0},{7,1},{8,10},{9,11},{10,... | collective-permute-start | bytes 786440 | tf_op jit(solution)/shard_map/ppermute | solution.py:39
  26.2 7.3 %collective-permute-start.5 = (bf16[128,1024]{1,0:T(8,128)(2,1)S(1)}, bf16[128,1024]{1,0:T(8,128)(2,1)}, u32[]{:S(2)}, u32[]{:S(2)}) collective-permute-start(bf16[128,1024]{1,0:T(8,128)(2,1)S(1)} %slice.7), channel_id=1, source_target_pairs={{0,6},{1,7},{2,0},{3,1},{4,2},{5,3},{6,4},{7,5},{8,14},{9,15},{10,... | collective-permute-start | bytes 786440 | tf_op jit(solution)/shard_map/ppermute | solution.py:39
  33.5 18.1 %collective-permute-start.7 = (bf16[256,1024]{1,0:T(8,128)(2,1)S(1)}, bf16[256,1024]{1,0:T(8,128)(2,1)S(1)}, u32[]{:S(2)}, u32[]{:S(2)}) collective-permute-start(bf16[256,1024]{1,0:T(8,128)(2,1)S(1)} %collective-permute-done.peer), channel_id=1, source_target_pairs={{0,2},{1,3},{2,4},{3,5},{4,6},{5,7},{6,0},{7,1},{8,10},{9,11},{10,... | collective-permute-start | bytes 1572872 | tf_op jit(solution)/shard_map/ppermute | solution.py:39
  34.4 17.2 %collective-permute-start.8 = (bf16[256,1024]{1,0:T(8,128)(2,1)S(1)}, bf16[256,1024]{1,0:T(8,128)(2,1)S(1)}, u32[]{:S(2)}, u32[]{:S(2)}) collective-permute-start(bf16[256,1024]{1,0:T(8,128)(2,1)S(1)} %collective-permute-done.peer), channel_id=1, source_target_pairs={{0,6},{1,7},{2,0},{3,1},{4,2},{5,3},{6,4},{7,5},{8,14},{9,15},{10,... | collective-permute-start | bytes 1572872 | tf_op jit(solution)/shard_map/ppermute | solution.py:39
  36.9 2.2 %collective-permute-start.6 = (bf16[512,384]{1,0:T(8,128)(2,1)S(1)}, bf16[512,384]{1,0:T(8,128)(2,1)}, u32[]{:S(2)}, u32[]{:S(2)}) collective-permute-start(bf16[512,384]{1,0:T(8,128)(2,1)S(1)} %pad_maximum_fusion.mine), channel_id=1, source_target_pairs={{0,8},{8,0},{16,24},{24,16},{32,40},{40,32},{48,56},{56,48},{64,72... | collective-permute-start | bytes 1179656 | tf_op jit(solution)/shard_map/ppermute | solution.py:39
  36.9 9.4 %collective-permute-start.10 = (bf16[128,1024]{1,0:T(8,128)(2,1)}, bf16[128,1024]{1,0:T(8,128)(2,1)}, u32[]{:S(2)}, u32[]{:S(2)}) collective-permute-start(bf16[128,1024]{1,0:T(8,128)(2,1)} %collective-permute-done.5.down_far), channel_id=1, source_target_pairs={{0,1},{1,0},{2,3},{3,2},{4,5},{5,4},{6,7},{7,6},{8,9},{9,8},{10,11... | collective-permute-start | bytes 786440 | tf_op jit(solution)/shard_map/ppermute | solution.py:39
  37.2 14.3 %collective-permute-start.9 = (bf16[128,1024]{1,0:T(8,128)(2,1)}, bf16[128,1024]{1,0:T(8,128)(2,1)}, u32[]{:S(2)}, u32[]{:S(2)}) collective-permute-start(bf16[128,1024]{1,0:T(8,128)(2,1)} %collective-permute-done.4.up_far), channel_id=1, source_target_pairs={{0,1},{1,0},{2,3},{3,2},{4,5},{5,4},{6,7},{7,6},{8,9},{9,8},{10,11... | collective-permute-start | bytes 786440 | tf_op jit(solution)/shard_map/ppermute | solution.py:39
  51.6 26.2 %copy-start = (bf16[1024,1024]{1,0:T(8,128)(2,1)S(1)}, bf16[1024,1024]{1,0:T(8,128)(2,1)}, u32[]{:S(2)}) copy-start(bf16[1024,1024]{1,0:T(8,128)(2,1)} %w_out.1) | copy-start | bytes 6291460
  51.6 26.2 %copy-start.2 = (f32[1024]{0:T(1024)S(1)}, f32[1024]{0:T(1024)}, u32[]{:S(2)}) copy-start(f32[1024]{0:T(1024)} %param.11) | copy-start | bytes 12292
  51.6 26.2 %copy-start.3 = (f32[1024]{0:T(1024)S(1)}, f32[1024]{0:T(1024)}, u32[]{:S(2)}) copy-start(f32[1024]{0:T(1024)} %param.12) | copy-start | bytes 12292
  82.2 17.3 %copy-start.4 = (bf16[1024,1024]{1,0:T(8,128)(2,1)S(1)}, bf16[1024,1024]{1,0:T(8,128)(2,1)}, u32[]{:S(2)}) copy-start(bf16[1024,1024]{1,0:T(8,128)(2,1)} %queries.1) | copy-start | bytes 6291460
  105.9 2.0 %collective-permute-start.11 = (f32[512,256]{1,0:T(8,128)S(1)}, f32[512,256]{1,0:T(8,128)S(1)}, u32[]{:S(2)}, u32[]{:S(2)}) collective-permute-start(f32[512,256]{1,0:T(8,128)S(1)} %get-tuple-element.29), channel_id=1, source_target_pairs={{0,8},{8,0},{16,24},{24,16},{32,40},{40,32},{48,56},{56,48},{64,72... | collective-permute-start | bytes 1572872 | tf_op jit(solution)/shard_map/ppermute | solution.py:39

commit v6 on v3

--- a/solution.py
+++ b/solution.py
@@ -20,6 +20,9 @@
 STAT_LANES = 16
 BLOCK = 512
 SPREAD = (8, 4, 2, 16)
+NEAR, FAR = 5 * ROWS, 3 * ROWS
+NEAR_BLOCK, FAR_BLOCK = 640, 384
+FAR_PIECES = 4
 score_scale = 0.125
 LOG2E = math.log2(math.e)
 EXP2_SCALE = score_scale * LOG2E
@@ -59,19 +62,6 @@
 
 def across(x):
     return permute(x, "seq", SEQ, lambda i: i ^ 1)
-
-
-def project_kernel(place, own, peer, up, down, up_far, down_far, mine, twin, out, w):
-    for k in range(1 << len(SPREAD)):
-        flip = sum(bit for p, bit in enumerate(SPREAD) if k >> p & 1)
-        for core, blocks in enumerate((mine, twin)):
-            start = pl.multiple_of((place[1] ^ (flip + core)) * 32, 32)
-            w[pl.ds(start, 32), :] = blocks[k * 32 : (k + 1) * 32, :]
-    row = 0
-    for piece in (own, peer, up, down, up_far, down_far):
-        count = piece.shape[0]
-        out[row : row + count, :] = dot(piece[...], w[...]).astype(bf16)
-        row += count
 
 
 def head_scores(q, k_t, head):
@@ -86,56 +76,113 @@
     return dot(probs, v_ones), top
 
 
-def softmax_pair(step, q_block, k_t, v_ones, scores_0, scores_1):
+def softmax_pair(step, steps, q_block, k_t, v_ones, scores_0, scores_1):
     scores_1[...] = head_scores(q_block(step), k_t[...], 1)
     mixed_0, peak_0 = weigh(scores_0[...], v_ones[...])
-    after = jnp.minimum(step + 1, pl.num_programs(0) - 1)
-    scores_0[...] = head_scores(q_block(after), k_t[...], 0)
+    scores_0[...] = head_scores(q_block(jnp.minimum(step + 1, steps - 1)), k_t[...], 0)
     mixed_1, peak_1 = weigh(scores_1[...], v_ones[...])
     low = lane_low((scores_0.shape[0], PAIR))
     total = jnp.where(low, mixed_0[:, PAIR:], mixed_1[:, PAIR:])
     mixed = jnp.where(low, mixed_0[:, :PAIR], mixed_1[:, :PAIR]) / total
-    return mixed, total, jnp.where(low, peak_0, peak_1)
-
-
-def attend_kernel(
-    table, early, up, down, up_far, down_far, w, out, q_all, k_t, v_ones, scores_0, scores_1
+    return mixed, jnp.where(low, peak_0, peak_1) * score_scale + jnp.log(total)
+
+
+def merge_pair(mixed_a, weight_a, mixed_b, weight_b):
+    top = jnp.maximum(weight_a, weight_b)
+    scale_a, scale_b = jnp.exp(weight_a - top), jnp.exp(weight_b - top)
+    total = scale_a + scale_b
+    return (mixed_a * scale_a + mixed_b * scale_b) / total, top + jnp.log(total)
+
+
+def project(pieces, w, q_all, k_t, v_ones, row):
+    for piece in pieces:
+        count = piece.shape[0]
+        block = dot(piece[...], w[...]).astype(bf16)
+        q_all[row : row + count, :] = block[:, :PAIR]
+        k_t[:, row : row + count] = block[:, PAIR : 2 * PAIR].T
+        v_ones[row : row + count, :PAIR] = block[:, 2 * PAIR :]
+        row += count
+    v_ones[:, PAIR:] = jnp.ones_like(v_ones[:, PAIR:])
+
+
+def row_block(q_all, size, start=0):
+    return lambda i: q_all[pl.ds(pl.multiple_of(start + i * size, 128), size), :]
+
+
+def near_kernel(
+    place, own, peer, up, down, up_far, down_far, mine, twin,
+    q_all, k_t, v_ones, w, mixed, weight, scores_0, scores_1,
 ):
     step = pl.program_id(0)
-
-    def q_block(i):
-        return q_all[pl.ds(pl.multiple_of(i * BLOCK, BLOCK), BLOCK), :]
+    q_block = row_block(q_all, NEAR_BLOCK)
 
     @pl.when(step == 0)
     def _():
-        v_ones[:, PAIR:] = jnp.ones_like(v_ones[:, PAIR:])
-        done = early.shape[0]
-        q_all[:done, :] = early[:, :PAIR]
-        k_t[:, :done] = early[:, PAIR : 2 * PAIR].T
-        v_ones[:done, :PAIR] = early[:, 2 * PAIR :]
-        row = done
-        for piece in (up, down, up_far, down_far):
-            count = piece.shape[0]
-            block = dot(piece[...], w[...]).astype(bf16)
-            q_all[row : row + count, :] = block[:, :PAIR]
-            k_t[:, row : row + count] = block[:, PAIR : 2 * PAIR].T
-            v_ones[row : row + count, :PAIR] = block[:, 2 * PAIR :]
-            row += count
+        for k in range(1 << len(SPREAD)):
+            flip = sum(bit for p, bit in enumerate(SPREAD) if k >> p & 1)
+            for core, blocks in enumerate((mine, twin)):
+                start = pl.multiple_of((place[1] ^ (flip + core)) * 32, 32)
+                w[pl.ds(start, 32), :] = blocks[k * 32 : (k + 1) * 32, :]
+        project((own, peer, up, down, up_far, down_far), w, q_all, k_t, v_ones, 0)
         scores_0[...] = head_scores(q_block(0), k_t[...], 0)
 
-    mixed, _, _ = softmax_pair(step, q_block, k_t, v_ones, scores_0, scores_1)
-    mixed = mixed.astype(bf16)
-    for p in range(BLOCK // ROWS):
-        out[table[step * (BLOCK // ROWS) + p]] = mixed[p * ROWS : (p + 1) * ROWS]
-
-
-def encode_kernel(attn, tokens, w_out, gain, bias, w_cross, encoded, cross_kv):
+    mixed[...], weight[...] = softmax_pair(
+        step, NEAR // NEAR_BLOCK, q_block, k_t, v_ones, scores_0, scores_1
+    )
+
+
+def far_kernel(table, *refs):
+    pieces, rest = refs[:FAR_PIECES], refs[FAR_PIECES:]
+    w, q_near, k_near, v_near, mixed_near, weight_near, out = rest[:7]
+    q_far, k_far, v_far, k_t, v_ones, near_0, near_1, far_0, far_1 = rest[7:]
+    step = pl.program_id(0)
+    near_steps, far_steps = NEAR // NEAR_BLOCK, FAR // FAR_BLOCK
+    near_rows, far_rows = row_block(q_near, NEAR_BLOCK), row_block(q_far, FAR_BLOCK)
+
+    def store(mixed, first):
+        for c in range(mixed.shape[0] // 128):
+            g = first // 128 + c
+            start = pl.multiple_of(g % 2 * 128, 128)
+            out[table[g // 2], pl.ds(start, 128), :] = mixed[c * 128 : (c + 1) * 128].astype(bf16)
+
+    @pl.when(step == 0)
+    def _():
+        project(pieces, w, q_far, k_far, v_far, 0)
+        k_t[:, :NEAR] = k_near[...]
+        k_t[:, NEAR:] = k_far[...]
+        v_ones[:NEAR, :] = v_near[...]
+        v_ones[NEAR:, :] = v_far[...]
+        near_0[...] = head_scores(near_rows(0), k_far[...], 0)
+
+    @pl.when(step < near_steps)
+    def _():
+        mixed, weight = softmax_pair(step, near_steps, near_rows, k_far, v_far, near_0, near_1)
+        rows = pl.ds(pl.multiple_of(step * NEAR_BLOCK, 128), NEAR_BLOCK)
+        mixed, _ = merge_pair(mixed, weight, mixed_near[rows, :], weight_near[rows, :])
+        store(mixed, step * NEAR_BLOCK)
+
+    @pl.when(step == near_steps)
+    def _():
+        far_0[...] = head_scores(far_rows(0), k_t[...], 0)
+
+    @pl.when(step >= near_steps)
+    def _():
+        mixed, _ = softmax_pair(step - near_steps, far_steps, far_rows, k_t, v_ones, far_0, far_1)
+        store(mixed, NEAR + (step - near_steps) * FAR_BLOCK)
+
+
+def encode_kernel(
+    attn, tokens, w_out, gain, bias, w_cross_far, encoded, cross_kv, w_cross, arrived
+):
+    fetch = pltpu.make_async_copy(w_cross_far, w_cross, arrived)
+    fetch.start()
     joined = jnp.concatenate([attn[p] for p in range(SEQ)], axis=1)
     residual = tokens[...].astype(f32) + dot(joined, w_out[...])
     center = residual - jnp.mean(residual, -1, keepdims=True)
     spread = jnp.mean(center * center, -1, keepdims=True)
     state = (center * lax.rsqrt(spread + 1e-05) * gain[...] + bias[...]).astype(bf16)
     encoded[...] = state
+    fetch.wait()
     for g in range(SEQ // 2):
         for part in range(2):
             start = part * MODEL + 2 * g * PAIR
@@ -148,9 +195,7 @@
 
 def cross_kernel(place, queries, kv, keep, send, k_t, v_ones, scores_0, scores_1):
     step = pl.program_id(0)
-
-    def q_block(i):
-        return queries[pl.ds(pl.multiple_of(i * BLOCK, BLOCK), BLOCK), :]
+    q_block = row_block(queries, BLOCK)
 
     @pl.when(step == 0)
     def _():
@@ -159,8 +204,9 @@
         v_ones[:, PAIR:] = jnp.ones_like(v_ones[:, PAIR:])
         scores_0[...] = head_scores(q_block(0), k_t[...], 0)
 
-    mixed, total, peak = softmax_pair(step, q_block, k_t, v_ones, scores_0, scores_1)
-    weight = peak * score_scale + jnp.log(total)
+    mixed, weight = softmax_pair(
+        step, NQ // BLOCK, q_block, k_t, v_ones, scores_0, scores_1
+    )
     is_even = place[1] % 2 == 0
     for g in range(BLOCK // (2 * OWN)):
         even = slice(2 * g * OWN, (2 * g + 1) * OWN)
@@ -172,12 +218,7 @@
 
 
 def merge_kernel(keep, received, out):
-    here, there = keep[:, PAIR:], received[:, PAIR:]
-    top = jnp.maximum(here, there)
-    scale_here, scale_there = jnp.exp(here - top), jnp.exp(there - top)
-    total = scale_here + scale_there
-    mixed = (keep[:, :PAIR] * scale_here + received[:, :PAIR] * scale_there) / total
-    weight = top + jnp.log(total)
+    mixed, weight = merge_pair(keep[:, :PAIR], keep[:, PAIR:], received[:, :PAIR], received[:, PAIR:])
     high = weight.astype(bf16)
     rest = weight - high.astype(f32)
     middle = rest.astype(bf16)
@@ -228,58 +269,67 @@
         return pl.BlockSpec(shape, lambda *_: (0,) * len(shape))
 
     place = jnp.stack([seq_index, span_index]).astype(jnp.int32)
-    early_rows = 5 * ROWS
-    early, weight = pl.pallas_call(
-        project_kernel,
-        in_specs=[pl.BlockSpec(memory_space=pltpu.SMEM)] + [pl.BlockSpec(memory_space=pltpu.VMEM)] * 8,
-        out_shape=[
-            jax.ShapeDtypeStruct((early_rows, 3 * PAIR), bf16),
-            jax.ShapeDtypeStruct((MODEL, 3 * PAIR), bf16),
-        ],
-        compiler_params=params(),
+    length = SEQ * ROWS
+    shapes = [
+        jax.ShapeDtypeStruct((NEAR, PAIR), bf16),
+        jax.ShapeDtypeStruct((PAIR, NEAR), bf16),
+        jax.ShapeDtypeStruct((NEAR, 2 * PAIR), bf16),
+        jax.ShapeDtypeStruct((MODEL, 3 * PAIR), bf16),
+        jax.ShapeDtypeStruct((NEAR, PAIR), f32),
+        jax.ShapeDtypeStruct((NEAR, PAIR), f32),
+    ]
+    pieces = (tokens, peer, *near, mine, twin)
+    q_near, k_near, v_near, weight, mixed_near, weight_near = pl.pallas_call(
+        near_kernel,
+        grid=(NEAR // NEAR_BLOCK,),
+        in_specs=[pl.BlockSpec(memory_space=pltpu.SMEM)] + [whole(p.shape) for p in pieces],
+        out_specs=[whole(p.shape) for p in shapes[:4]]
+        + [pl.BlockSpec((NEAR_BLOCK, PAIR), lambda b: (b, 0))] * 2,
+        out_shape=shapes,
+        scratch_shapes=[pltpu.VMEM((NEAR_BLOCK, NEAR), f32)] * 2,
+        compiler_params=params(28),
         cost_estimate=pl.CostEstimate(
-            flops=2 * early_rows * MODEL * 3 * PAIR, bytes_accessed=4 << 20, transcendentals=0
-        ),
-    )(place, tokens, peer, *near, mine, twin)
+            flops=2 * NEAR * MODEL * 3 * PAIR, bytes_accessed=4 << 20, transcendentals=0
+        ),
+    )(place, *pieces)
 
     order = jnp.stack(
         [((y + dy) % 4) * 2 + (x_lo ^ flip) for dy, flip in
          ((0, 0), (0, 1), (3, 0), (1, 0), (2, 0), (3, 1), (1, 1), (2, 1))]
     ).astype(jnp.int32)
-    length = SEQ * ROWS
+    operands = (*far, weight, q_near, k_near, v_near, mixed_near, weight_near)
     attn = pl.pallas_call(
-        attend_kernel,
+        far_kernel,
         grid_spec=pltpu.PrefetchScalarGridSpec(
             num_scalar_prefetch=1,
-            grid=(length // BLOCK,),
-            in_specs=[
-                whole((early_rows, 3 * PAIR)),
-                whole((ROWS, MODEL)),
-                whole((ROWS, MODEL)),
-                whole((ROWS // 2, MODEL)),
-                whole((ROWS // 2, MODEL)),
-                whole((MODEL, 3 * PAIR)),
-            ],
+            grid=(NEAR // NEAR_BLOCK + FAR // FAR_BLOCK,),
+            in_specs=[whole(p.shape) for p in operands],
             out_specs=whole((SEQ, ROWS, PAIR)),
             scratch_shapes=[
-                pltpu.VMEM((length, PAIR), bf16),
+                pltpu.VMEM((FAR, PAIR), bf16),
+                pltpu.VMEM((PAIR, FAR), bf16),
+                pltpu.VMEM((FAR, 2 * PAIR), bf16),
                 pltpu.VMEM((PAIR, length), bf16),
                 pltpu.VMEM((length, 2 * PAIR), bf16),
-                pltpu.VMEM((BLOCK, length), f32),
-                pltpu.VMEM((BLOCK, length), f32),
+                pltpu.VMEM((NEAR_BLOCK, FAR), f32),
+                pltpu.VMEM((NEAR_BLOCK, FAR), f32),
+                pltpu.VMEM((FAR_BLOCK, length), f32),
+                pltpu.VMEM((FAR_BLOCK, length), f32),
             ],
         ),
         out_shape=jax.ShapeDtypeStruct((SEQ, ROWS, PAIR), bf16),
-        compiler_params=params(),
+        compiler_params=params(32),
         cost_estimate=pl.CostEstimate(
-            flops=8 * length * length * 2 * PAIR, bytes_accessed=4 << 20,
+            flops=6 * length * length * 2 * PAIR, bytes_accessed=4 << 20,
             transcendentals=2 * length * length,
         ),
-    )(order, early, *far, weight)
+    )(order, *operands)
     attn = lax.all_to_all(attn, "seq", split_axis=0, concat_axis=0, tiled=True)
 
     encoded, cross_kv = pl.pallas_call(
         encode_kernel,
+        in_specs=[pl.BlockSpec(memory_space=pltpu.VMEM)] * 5 + [pl.BlockSpec(memory_space=pl.ANY)],
+        scratch_shapes=[pltpu.VMEM((MODEL, 2 * MODEL), bf16), pltpu.SemaphoreType.DMA],
         out_shape=[
             jax.ShapeDtypeStruct((ROWS, MODEL), bf16),
             jax.ShapeDtypeStruct((SEQ, ROWS, 2 * PAIR), bf16),

time: 131 us -> 132 us (level)
  waiting for transfers between devices: 17.8 us -> 12.5 us
  blocking collectives: 53.6 us -> 58.9 us
    ppermute x17, waiting for transfers between devices: 17.8 us -> 12.5 us  [permute(): return lax.ppermute(x, axis, [(i, target(i)) for i in range(size)])]
    all_to_all x1, blocking collectives: 11.1 us -> 14.1 us  [per_device(): attn = lax.all_to_all(attn, 'seq', split_axis=0, concat_axis=0, tiled=True)]
    all_to_all x1, blocking collectives: 14.4 us -> 17.3 us  [per_device(): lax.all_to_all(cross_kv, 'seq', split_axis=0, concat_axis=0, tiled=True)]
  transfers between devices with their start and end apart: 17 -> 17, of which waited for: 8 -> 7; matrix products, arithmetic and copies ran while one was open for 1% -> 1% of each run, Pallas kernels for 2% -> 6%
where the time goes in v6:
time: 132 us
  blocking collectives  58.9 us (45%)
  starting transfers between devices  29.2 us (22%)
  Pallas kernels  28.4 us (22%)
  waiting for transfers between devices  12.5 us (9%)
  local copies, waits for them, and re-layouts  1.52 us (1%)
    ppermute x17, starting transfers between devices, permute(): return lax.ppermute(x, axis, [(i, target(i)) for i in range(size)])  29.2 us
    all_to_all x1, blocking collectives, per_device(): lax.all_to_all(merged.reshape(16, OWN, 2 * PAIR), 'span', split_axis=0, c...  18.7 us
    all_to_all x1, blocking collectives, per_device(): lax.all_to_all(cross_kv, 'seq', split_axis=0, concat_axis=0, tiled=True)  17.3 us
    all_to_all x1, blocking collectives, per_device(): attn = lax.all_to_all(attn, 'seq', split_axis=0, concat_axis=0, tiled=True)  14.1 us
    ppermute x17, waiting for transfers between devices, permute(): return lax.ppermute(x, axis, [(i, target(i)) for i in range(size)])  12.5 us
    pallas_call x1, Pallas kernels, per_device(): pl.pallas_call(far_kernel, grid_spec=pltpu.PrefetchScalarGridSpec(num_sca...  10.4 us
    all_to_all x1, blocking collectives, per_device(): heads = lax.all_to_all(mine, 'seq', split_axis=0, concat_axis=0, tiled=True)  8.78 us
    pallas_call x1, Pallas kernels, per_device(): pl.pallas_call(near_kernel, grid=(NEAR // NEAR_BLOCK,), in_specs=[pl.Bloc...  7.43 us
  transfers between devices with their start and end apart: 17, of which 7 were waited for; matrix products, arithmetic and copies ran while one was open for 1% of the time, Pallas kernels for 6%

profile of v6, /device:TPU:32, one launch (start us, length us, event | category | flops | bytes accessed | tf_op | source)
XLA Modules:
  0.0 131.5 jit_solution(5979938962904473742)
XLA Ops:
  0.6 1.6 %collective-permute-start = (bf16[256,1024]{1,0:T(8,128)(2,1)}, bf16[256,1024]{1,0:T(8,128)(2,1)S(1)}, u32[]{:S(2)}, u32[]{:S(2)}) collective-permute-start(bf16[256,1024]{1,0:T(8,128)(2,1)} %tokens.1), channel_id=1, source_target_pairs={{0,1},{1,0},{2,3},{3,2},{4,5},{5,4},{6,7},{7,6},{8,9},{9,8},{10,11... | collective-permute-start | bytes 1572872 | tf_op jit(solution)/shard_map/ppermute | solution.py:43
  2.2 1.6 %collective-permute-start.1 = (bf16[256,1024]{1,0:T(8,128)(2,1)}, bf16[256,1024]{1,0:T(8,128)(2,1)S(1)}, u32[]{:S(2)}, u32[]{:S(2)}) collective-permute-start(bf16[256,1024]{1,0:T(8,128)(2,1)} %tokens.1), channel_id=1, source_target_pairs={{0,2},{1,3},{2,4},{3,5},{4,6},{5,7},{6,0},{7,1},{8,10},{9,11},{10,... | collective-permute-start | bytes 1572872 | tf_op jit(solution)/shard_map/ppermute | solution.py:43
  3.8 1.7 %collective-permute-start.2 = (bf16[256,1024]{1,0:T(8,128)(2,1)}, bf16[256,1024]{1,0:T(8,128)(2,1)S(1)}, u32[]{:S(2)}, u32[]{:S(2)}) collective-permute-start(bf16[256,1024]{1,0:T(8,128)(2,1)} %tokens.1), channel_id=1, source_target_pairs={{0,6},{1,7},{2,0},{3,1},{4,2},{5,3},{6,4},{7,5},{8,14},{9,15},{10,... | collective-permute-start | bytes 1572872 | tf_op jit(solution)/shard_map/ppermute | solution.py:43
  5.5 0.7 constant_dynamic-slice_fusion.2
  6.2 6.4 %collective-permute-start.3 = (bf16[32,384]{1,0:T(8,128)(2,1)S(1)}, bf16[32,384]{1,0:T(8,128)(2,1)S(1)}, u32[]{:S(2)}, u32[]{:S(2)}) collective-permute-start(bf16[32,384]{1,0:T(8,128)(2,1)S(1)} %pad_maximum_fusion.2), channel_id=1, source_target_pairs={{0,64},{8,72},{16,80},{24,88},{32,96},{40,104},{48,112},{56,120},{... | collective-permute-start | bytes 73736 | tf_op jit(solution)/shard_map/ppermute | solution.py:43
  12.6 1.5 %collective-permute-start.4 = (bf16[32,384]{1,0:T(8,128)(2,1)S(1)}, bf16[32,384]{1,0:T(8,128)(2,1)S(1)}, u32[]{:S(2)}, u32[]{:S(2)}) collective-permute-start(bf16[32,384]{1,0:T(8,128)(2,1)S(1)} %pad_maximum_fusion.2), channel_id=1, source_target_pairs={{0,32},{8,40},{16,48},{24,56},{32,0},{40,8},{48,16},{56,24},{64,96... | collective-permute-start | bytes 73736 | tf_op jit(solution)/shard_map/ppermute | solution.py:43
  14.0 0.9 collective-permute-done.3
  14.9 4.5 %collective-permute-start.5 = (bf16[32,384]{1,0:T(8,128)(2,1)S(1)}, bf16[32,384]{1,0:T(8,128)(2,1)S(1)}, u32[]{:S(2)}, u32[]{:S(2)}) collective-permute-start(bf16[32,384]{1,0:T(8,128)(2,1)S(1)} %pad_maximum_fusion.2), channel_id=1, source_target_pairs={{0,96},{8,104},{16,112},{24,120},{32,64},{40,72},{48,80},{56,88},{... | collective-permute-start | bytes 73736 | tf_op jit(solution)/shard_map/ppermute | solution.py:43
  19.4 0.0 collective-permute-done.4
  19.4 1.8 %collective-permute-done.5 = bf16[32,384]{1,0:T(8,128)(2,1)S(1)} collective-permute-done((bf16[32,384]{1,0:T(8,128)(2,1)S(1)}, bf16[32,384]{1,0:T(8,128)(2,1)S(1)}, u32[]{:S(2)}, u32[]{:S(2)}) %collective-permute-start.5) | collective-permute-done | bytes 24608 | tf_op jit(solution)/shard_map/ppermute | solution.py:43
  21.3 0.0 collective-permute-done.1.up
  21.3 0.0 collective-permute-done.2.down
  21.3 1.1 collective-permute-start.6
  22.4 2.7 %collective-permute-start.7 = (bf16[128,384]{1,0:T(8,128)(2,1)S(1)}, bf16[128,384]{1,0:T(8,128)(2,1)S(1)}, u32[]{:S(2)}, u32[]{:S(2)}) collective-permute-start(bf16[128,384]{1,0:T(8,128)(2,1)S(1)} %pad_maximum_fusion.1), channel_id=1, source_target_pairs={{0,128},{8,136},{16,144},{24,152},{32,160},{40,168},{48,176},{56,1... | collective-permute-start | bytes 294920 | tf_op jit(solution)/shard_map/ppermute | solution.py:43
  25.1 1.3 collective-permute-start.8
  26.4 0.5 collective-permute-start.11
  26.9 2.9 %collective-permute-start.13 = (bf16[128,1024]{1,0:T(8,128)(2,1)S(1)}, bf16[128,1024]{1,0:T(8,128)(2,1)}, u32[]{:S(2)}, u32[]{:S(2)}) collective-permute-start(bf16[128,1024]{1,0:T(8,128)(2,1)S(1)} %slice.7), channel_id=1, source_target_pairs={{0,6},{1,7},{2,0},{3,1},{4,2},{5,3},{6,4},{7,5},{8,14},{9,15},{10,... | collective-permute-start | bytes 786440 | tf_op jit(solution)/shard_map/ppermute | solution.py:43
  29.8 0.0 collective-permute-done.6
  29.8 0.0 collective-permute-done.7
  29.8 2.3 %collective-permute-done.8 = bf16[128,384]{1,0:T(8,128)(2,1)S(1)} collective-permute-done((bf16[128,384]{1,0:T(8,128)(2,1)S(1)}, bf16[128,384]{1,0:T(8,128)(2,1)S(1)}, u32[]{:S(2)}, u32[]{:S(2)}) %collective-permute-start.8) | collective-permute-done | bytes 98336 | tf_op jit(solution)/shard_map/ppermute | solution.py:43
  32.2 1.9 %collective-permute-start.10 = (bf16[256,1024]{1,0:T(8,128)(2,1)S(1)}, bf16[256,1024]{1,0:T(8,128)(2,1)S(1)}, u32[]{:S(2)}, u32[]{:S(2)}) collective-permute-start(bf16[256,1024]{1,0:T(8,128)(2,1)S(1)} %collective-permute-done.peer), channel_id=1, source_target_pairs={{0,6},{1,7},{2,0},{3,1},{4,2},{5,3},{6,4},{7,5},{8,14},{9,15},{10,... | collective-permute-start | bytes 1572872 | tf_op jit(solution)/shard_map/ppermute | solution.py:43
  34.0 0.2 collective-permute-start.9
  34.3 0.4 collective-permute-done.11.up_far
  34.7 0.8 collective-permute-start.12
  35.5 0.9 collective-permute-done.13.down_far
  36.5 0.6 collective-permute-start.14
  37.0 0.1 stack.44.table
  37.1 0.1 pad_add_fusion.place
  37.2 0.0 collective-permute-done.15.twin
  37.2 7.4 %shard_map.86 = (bf16[1280,128]{1,0:T(8,128)(2,1)S(1)}, bf16[128,1280]{1,0:T(8,128)(2,1)S(1)}, bf16[1280,256]{1,0:T(8,128)(2,1)S(1)}, bf16[1024,384]{1,0:T(8,128...) custom-call(s32[2]{0:T(128)S(1)} %pad_add_fusion.place, bf16[256,1024]{1,0:T(8,128)(2,1)S(1)} %copy-done.1, ...), custom_call_target="tpu_custom_call" | custom-call | flops 1006632960 | bytes 4194304 | tf_op jit(solution)/shard_map/pallas_call | solution.py:282
  44.6 0.0 collective-permute-done.12.refs_2_
  44.7 4.3 %collective-permute-done.14.refs_3_ = bf16[128,1024]{1,0:T(8,128)(2,1)} collective-permute-done((bf16[128,1024]{1,0:T(8,128)(2,1)}, bf16[128,1024]{1,0:T(8,128)(2,1)}, u32[]{:S(2)}, u32[]{:S(2)}) %collective-permute-start.14) | collective-permute-done | bytes 262176 | tf_op jit(solution)/shard_map/ppermute | solution.py:43
  48.9 0.0 collective-permute-done.10.refs_1_
  48.9 0.0 copy-start.2
  48.9 0.0 copy-start.3
  49.0 10.4 %shard_map.87 = bf16[8,256,128]{2,1,0:T(8,128)(2,1)S(1)} custom-call(s32[8]{0:T(128)S(1)} %stack.44.table, bf16[256,1024]{1,0:T(8,128)(2,1)S(1)} %collective-permute-done.9.refs_0_, bf16[256,1024]{1,0:T(8,128)(2,1)S(1)} %collective-permute-done.10.refs_1_, bf16[128,1024]{1,0:T(8,128)(2,1)} %collective-permute-done.12.refs_2_, ...), custom_call_target="tpu_custom_call" | custom-call | flops 6442450944 | bytes 4194304 | tf_op jit(solution)/shard_map/pallas_call | solution.py:301
  59.3 14.1 %all_to_all.20.attn = bf16[8,256,128]{2,1,0:T(8,128)(2,1)S(1)} all-to-all(bf16[8,256,128]{2,1,0:T(8,128)(2,1)S(1)} %shard_map.87), channel_id=1, replica_groups=mesh['span'=32,'seq'=8] {'seq'}, dimensions={0} | all-to-all | bytes 1048576 | tf_op jit(solution)/shard_map/all_to_all | solution.py:327
  73.5 3.6 %shard_map.88 = (bf16[256,1024]{1,0:T(8,128)(2,1)}, bf16[8,256,256]{2,1,0:T(8,128)(2,1)S(1)}) custom-call(bf16[8,256,128]{2,1,0:T(8,128)(2,1)S(1)} %all_to_all.20.attn, bf16[256,1024]{1,0:T(8,128)(2,1)S(1)} %copy-done.1, bf16[1024,1024]{1,0:T(8,128)(2,1)S(1)} %copy-done, f32[1,1024]{1,0:T(1,128)S(1)} %bitcast.22, f32[1,1024]{1,0:T(1,128)S(1)} %bitcast.23, ...), custom_call_target="tpu_custom_call" | custom-call | flops 1610612736 | bytes 8388608 | tf_op jit(solution)/shard_map/pallas_call | solution.py:329
  77.0 0.0 copy-start.4
  77.0 17.3 %all_to_all.21 = bf16[8,256,256]{2,1,0:T(8,128)(2,1)S(1)} all-to-all(bf16[8,256,256]{2,1,0:T(8,128)(2,1)S(1)} %get-tuple-element.31), channel_id=1, replica_groups=mesh['span'=32,'seq'=8] {'seq'}, dimensions={0} | all-to-all | bytes 2097152 | tf_op jit(solution)/shard_map/all_to_all | solution.py:343
  94.4 6.4 %shard_map.89 = (f32[512,256]{1,0:T(8,128)S(1)}, f32[512,256]{1,0:T(8,128)S(1)}) custom-call(s32[2]{0:T(128)S(1)} %pad_add_fusion.place, bf16[1024,1024]{1,0:T(8,128)(2,1)S(1)} %copy-done.4, bf16[2048,256]{1,0:T(8,128)(2,1)S(1)} %bitcast.21), custom_call_target="tpu_custom_call" | custom-call | flops 4294967296 | bytes 2097152 | tf_op jit(solution)/shard_map/pallas_call | solution.py:347
  100.8 0.1 collective-permute-start.16
  100.9 1.9 %collective-permute-done.16.received = f32[512,256]{1,0:T(8,128)S(1)} collective-permute-done((f32[512,256]{1,0:T(8,128)S(1)}, f32[512,256]{1,0:T(8,128)S(1)}, u32[]{:S(2)}, u32[]{:S(2)}) %collective-permute-start.16) | collective-permute-done | bytes 524320 | tf_op jit(solution)/shard_map/ppermute | solution.py:43
  102.8 0.2 shard_map.90
  103.0 18.7 %all_to_all.22.parts = bf16[16,32,256]{2,1,0:T(8,128)(2,1)S(1)} all-to-all(bf16[16,32,256]{2,1,0:T(8,128)(2,1)S(1)} %bitcast.20), channel_id=1, replica_groups={{0,16,32,48,64,80,96,112,128,144,160,176,192,208,224,240},{8,24,40,56,7..., dimensions={0} | all-to-all | bytes 524288 | tf_op jit(solution)/shard_map/all_to_all | solution.py:381
  121.7 0.4 shard_map.91
  122.1 8.8 %all_to_all.23 = bf16[8,32,128]{2,1,0:T(8,128)(2,1)S(1)} all-to-all(bf16[8,32,128]{2,1,0:T(8,128)(2,1)S(1)} %shard_map.91), channel_id=1, replica_groups=mesh['span'=32,'seq'=8] {'seq'}, dimensions={0} | all-to-all | bytes 131072 | tf_op jit(solution)/shard_map/all_to_all | solution.py:394
  130.9 0.6 copy_bitcast_fusion
  (15 shorter events, 0.1 us)
Async XLA Ops:
  0.6 36.6 %copy-start.1 = (bf16[256,1024]{1,0:T(8,128)(2,1)S(1)}, bf16[256,1024]{1,0:T(8,128)(2,1)}, u32[]{:S(2)}) copy-start(bf16[256,1024]{1,0:T(8,128)(2,1)} %tokens.1) | copy-start | bytes 1572868
  0.6 20.6 %collective-permute-start = (bf16[256,1024]{1,0:T(8,128)(2,1)}, bf16[256,1024]{1,0:T(8,128)(2,1)S(1)}, u32[]{:S(2)}, u32[]{:S(2)}) collective-permute-start(bf16[256,1024]{1,0:T(8,128)(2,1)} %tokens.1), channel_id=1, source_target_pairs={{0,1},{1,0},{2,3},{3,2},{4,5},{5,4},{6,7},{7,6},{8,9},{9,8},{10,11... | collective-permute-start | bytes 1572872 | tf_op jit(solution)/shard_map/ppermute | solution.py:43
  2.2 19.0 %collective-permute-start.1 = (bf16[256,1024]{1,0:T(8,128)(2,1)}, bf16[256,1024]{1,0:T(8,128)(2,1)S(1)}, u32[]{:S(2)}, u32[]{:S(2)}) collective-permute-start(bf16[256,1024]{1,0:T(8,128)(2,1)} %tokens.1), channel_id=1, source_target_pairs={{0,2},{1,3},{2,4},{3,5},{4,6},{5,7},{6,0},{7,1},{8,10},{9,11},{10,... | collective-permute-start | bytes 1572872 | tf_op jit(solution)/shard_map/ppermute | solution.py:43
  3.8 17.5 %collective-permute-start.2 = (bf16[256,1024]{1,0:T(8,128)(2,1)}, bf16[256,1024]{1,0:T(8,128)(2,1)S(1)}, u32[]{:S(2)}, u32[]{:S(2)}) collective-permute-start(bf16[256,1024]{1,0:T(8,128)(2,1)} %tokens.1), channel_id=1, source_target_pairs={{0,6},{1,7},{2,0},{3,1},{4,2},{5,3},{6,4},{7,5},{8,14},{9,15},{10,... | collective-permute-start | bytes 1572872 | tf_op jit(solution)/shard_map/ppermute | solution.py:43
  6.2 8.7 %collective-permute-start.3 = (bf16[32,384]{1,0:T(8,128)(2,1)S(1)}, bf16[32,384]{1,0:T(8,128)(2,1)S(1)}, u32[]{:S(2)}, u32[]{:S(2)}) collective-permute-start(bf16[32,384]{1,0:T(8,128)(2,1)S(1)} %pad_maximum_fusion.2), channel_id=1, source_target_pairs={{0,64},{8,72},{16,80},{24,88},{32,96},{40,104},{48,112},{56,120},{... | collective-permute-start | bytes 73736 | tf_op jit(solution)/shard_map/ppermute | solution.py:43
  12.6 6.8 %collective-permute-start.4 = (bf16[32,384]{1,0:T(8,128)(2,1)S(1)}, bf16[32,384]{1,0:T(8,128)(2,1)S(1)}, u32[]{:S(2)}, u32[]{:S(2)}) collective-permute-start(bf16[32,384]{1,0:T(8,128)(2,1)S(1)} %pad_maximum_fusion.2), channel_id=1, source_target_pairs={{0,32},{8,40},{16,48},{24,56},{32,0},{40,8},{48,16},{56,24},{64,96... | collective-permute-start | bytes 73736 | tf_op jit(solution)/shard_map/ppermute | solution.py:43
  14.9 6.3 %collective-permute-start.5 = (bf16[32,384]{1,0:T(8,128)(2,1)S(1)}, bf16[32,384]{1,0:T(8,128)(2,1)S(1)}, u32[]{:S(2)}, u32[]{:S(2)}) collective-permute-start(bf16[32,384]{1,0:T(8,128)(2,1)S(1)} %pad_maximum_fusion.2), channel_id=1, source_target_pairs={{0,96},{8,104},{16,112},{24,120},{32,64},{40,72},{48,80},{56,88},{... | collective-permute-start | bytes 73736 | tf_op jit(solution)/shard_map/ppermute | solution.py:43
  21.3 8.5 %collective-permute-start.6 = (bf16[128,384]{1,0:T(8,128)(2,1)S(1)}, bf16[128,384]{1,0:T(8,128)(2,1)S(1)}, u32[]{:S(2)}, u32[]{:S(2)}) collective-permute-start(bf16[128,384]{1,0:T(8,128)(2,1)S(1)} %pad_maximum_fusion.1), channel_id=1, source_target_pairs={{0,16},{8,24},{16,0},{24,8},{32,48},{40,56},{48,32},{56,40},{64,80... | collective-permute-start | bytes 294920 | tf_op jit(solution)/shard_map/ppermute | solution.py:43
  22.4 7.4 %collective-permute-start.7 = (bf16[128,384]{1,0:T(8,128)(2,1)S(1)}, bf16[128,384]{1,0:T(8,128)(2,1)S(1)}, u32[]{:S(2)}, u32[]{:S(2)}) collective-permute-start(bf16[128,384]{1,0:T(8,128)(2,1)S(1)} %pad_maximum_fusion.1), channel_id=1, source_target_pairs={{0,128},{8,136},{16,144},{24,152},{32,160},{40,168},{48,176},{56,1... | collective-permute-start | bytes 294920 | tf_op jit(solution)/shard_map/ppermute | solution.py:43
  25.1 7.0 %collective-permute-start.8 = (bf16[128,384]{1,0:T(8,128)(2,1)S(1)}, bf16[128,384]{1,0:T(8,128)(2,1)S(1)}, u32[]{:S(2)}, u32[]{:S(2)}) collective-permute-start(bf16[128,384]{1,0:T(8,128)(2,1)S(1)} %pad_maximum_fusion.1), channel_id=1, source_target_pairs={{0,144},{8,152},{16,128},{24,136},{32,176},{40,184},{48,160},{56,1... | collective-permute-start | bytes 294920 | tf_op jit(solution)/shard_map/ppermute | solution.py:43
  26.4 8.3 %collective-permute-start.11 = (bf16[128,1024]{1,0:T(8,128)(2,1)S(1)}, bf16[128,1024]{1,0:T(8,128)(2,1)}, u32[]{:S(2)}, u32[]{:S(2)}) collective-permute-start(bf16[128,1024]{1,0:T(8,128)(2,1)S(1)} %slice.6), channel_id=1, source_target_pairs={{0,2},{1,3},{2,4},{3,5},{4,6},{5,7},{6,0},{7,1},{8,10},{9,11},{10,... | collective-permute-start | bytes 786440 | tf_op jit(solution)/shard_map/ppermute | solution.py:43
  26.9 9.5 %collective-permute-start.13 = (bf16[128,1024]{1,0:T(8,128)(2,1)S(1)}, bf16[128,1024]{1,0:T(8,128)(2,1)}, u32[]{:S(2)}, u32[]{:S(2)}) collective-permute-start(bf16[128,1024]{1,0:T(8,128)(2,1)S(1)} %slice.7), channel_id=1, source_target_pairs={{0,6},{1,7},{2,0},{3,1},{4,2},{5,3},{6,4},{7,5},{8,14},{9,15},{10,... | collective-permute-start | bytes 786440 | tf_op jit(solution)/shard_map/ppermute | solution.py:43
  32.2 16.8 %collective-permute-start.10 = (bf16[256,1024]{1,0:T(8,128)(2,1)S(1)}, bf16[256,1024]{1,0:T(8,128)(2,1)S(1)}, u32[]{:S(2)}, u32[]{:S(2)}) collective-permute-start(bf16[256,1024]{1,0:T(8,128)(2,1)S(1)} %collective-permute-done.peer), channel_id=1, source_target_pairs={{0,6},{1,7},{2,0},{3,1},{4,2},{5,3},{6,4},{7,5},{8,14},{9,15},{10,... | collective-permute-start | bytes 1572872 | tf_op jit(solution)/shard_map/ppermute | solution.py:43
  34.0 14.9 %collective-permute-start.9 = (bf16[256,1024]{1,0:T(8,128)(2,1)S(1)}, bf16[256,1024]{1,0:T(8,128)(2,1)S(1)}, u32[]{:S(2)}, u32[]{:S(2)}) collective-permute-start(bf16[256,1024]{1,0:T(8,128)(2,1)S(1)} %collective-permute-done.peer), channel_id=1, source_target_pairs={{0,2},{1,3},{2,4},{3,5},{4,6},{5,7},{6,0},{7,1},{8,10},{9,11},{10,... | collective-permute-start | bytes 1572872 | tf_op jit(solution)/shard_map/ppermute | solution.py:43
  34.3 2.9 %collective-permute-start.15 = (bf16[512,384]{1,0:T(8,128)(2,1)S(1)}, bf16[512,384]{1,0:T(8,128)(2,1)}, u32[]{:S(2)}, u32[]{:S(2)}) collective-permute-start(bf16[512,384]{1,0:T(8,128)(2,1)S(1)} %pad_maximum_fusion.mine), channel_id=1, source_target_pairs={{0,8},{8,0},{16,24},{24,16},{32,40},{40,32},{48,56},{56,48},{64,72... | collective-permute-start | bytes 1179656 | tf_op jit(solution)/shard_map/ppermute | solution.py:43
  34.7 10.0 %collective-permute-start.12 = (bf16[128,1024]{1,0:T(8,128)(2,1)}, bf16[128,1024]{1,0:T(8,128)(2,1)}, u32[]{:S(2)}, u32[]{:S(2)}) collective-permute-start(bf16[128,1024]{1,0:T(8,128)(2,1)} %collective-permute-done.11.up_far), channel_id=1, source_target_pairs={{0,1},{1,0},{2,3},{3,2},{4,5},{5,4},{6,7},{7,6},{8,9},{9,8},{10,11... | collective-permute-start | bytes 786440 | tf_op jit(solution)/shard_map/ppermute | solution.py:43
  36.5 12.4 %collective-permute-start.14 = (bf16[128,1024]{1,0:T(8,128)(2,1)}, bf16[128,1024]{1,0:T(8,128)(2,1)}, u32[]{:S(2)}, u32[]{:S(2)}) collective-permute-start(bf16[128,1024]{1,0:T(8,128)(2,1)} %collective-permute-done.13.down_far), channel_id=1, source_target_pairs={{0,1},{1,0},{2,3},{3,2},{4,5},{5,4},{6,7},{7,6},{8,9},{9,8},{10,11... | collective-permute-start | bytes 786440 | tf_op jit(solution)/shard_map/ppermute | solution.py:43
  48.9 24.5 %copy-start = (bf16[1024,1024]{1,0:T(8,128)(2,1)S(1)}, bf16[1024,1024]{1,0:T(8,128)(2,1)}, u32[]{:S(2)}) copy-start(bf16[1024,1024]{1,0:T(8,128)(2,1)} %w_out.1) | copy-start | bytes 6291460
  48.9 24.5 %copy-start.2 = (f32[1024]{0:T(1024)S(1)}, f32[1024]{0:T(1024)}, u32[]{:S(2)}) copy-start(f32[1024]{0:T(1024)} %param.11) | copy-start | bytes 12292
  48.9 24.5 %copy-start.3 = (f32[1024]{0:T(1024)S(1)}, f32[1024]{0:T(1024)}, u32[]{:S(2)}) copy-start(f32[1024]{0:T(1024)} %param.12) | copy-start | bytes 12292
  77.0 17.3 %copy-start.4 = (bf16[1024,1024]{1,0:T(8,128)(2,1)S(1)}, bf16[1024,1024]{1,0:T(8,128)(2,1)}, u32[]{:S(2)}) copy-start(bf16[1024,1024]{1,0:T(8,128)(2,1)} %queries.1) | copy-start | bytes 6291460
  100.8 2.0 %collective-permute-start.16 = (f32[512,256]{1,0:T(8,128)S(1)}, f32[512,256]{1,0:T(8,128)S(1)}, u32[]{:S(2)}, u32[]{:S(2)}) collective-permute-start(f32[512,256]{1,0:T(8,128)S(1)} %get-tuple-element.33), channel_id=1, source_target_pairs={{0,8},{8,0},{16,24},{24,16},{32,40},{40,32},{48,56},{56,48},{64,72... | collective-permute-start | bytes 1572872 | tf_op jit(solution)/shard_map/ppermute | solution.py:43

commit v7 on v6

--- a/solution.py
+++ b/solution.py
@@ -19,7 +19,7 @@
 NQ = 1024
 STAT_LANES = 16
 BLOCK = 512
-SPREAD = (8, 4, 2, 16)
+SPREAD = (2, 4, 8, 16)
 NEAR, FAR = 5 * ROWS, 3 * ROWS
 NEAR_BLOCK, FAR_BLOCK = 640, 384
 FAR_PIECES = 4
@@ -257,7 +257,8 @@
         ],
         axis=1,
     )
-    mine = spread(mine, SPREAD[:2])
+    for bit in SPREAD[:2]:
+        mine = jnp.concatenate([mine, permute(mine, "span", SPAN, lambda i, f=bit: i ^ f)])
     peer, up, down, mine = lax.optimization_barrier((peer, up, down, mine))
     near = (up, down, from_below(up[:half]), from_above(down[half:]))
     mine = spread(mine, SPREAD[2:])

time: 132 us -> 136 us (1.030)
  waiting for transfers between devices: 12.5 us -> 21.3 us
  blocking collectives: 58.9 us -> 56.4 us
  starting transfers between devices: 29.2 us -> 26.7 us
    ppermute x17 -> x16, waiting for transfers between devices: 12.5 us -> 21.3 us  [permute(): return lax.ppermute(x, axis, [(i, target(i)) for i in range(size)])]
    ppermute x17 -> x16, starting transfers between devices: 29.2 us -> 26.7 us  [permute(): return lax.ppermute(x, axis, [(i, target(i)) for i in range(size)])]
  transfers between devices with their start and end apart: 17 -> 16, of which waited for: 7 -> 6; matrix products, arithmetic and copies ran while one was open for 1% -> 1% of each run, Pallas kernels for 6% -> 5%
where the time goes in v7:
time: 136 us; the launch traced here: 135 us
  blocking collectives  56.4 us (41%)
  Pallas kernels  28.4 us (21%)
  starting transfers between devices  26.7 us (20%)
  waiting for transfers between devices  21.3 us (16%)
  local copies, waits for them, and re-layouts  1.52 us (1%)
    ppermute x16, starting transfers between devices, permute(): return lax.ppermute(x, axis, [(i, target(i)) for i in range(size)])  26.7 us
    ppermute x16, waiting for transfers between devices, permute(): return lax.ppermute(x, axis, [(i, target(i)) for i in range(size)])  21.3 us
    all_to_all x1, blocking collectives, per_device(): lax.all_to_all(merged.reshape(16, OWN, 2 * PAIR), 'span', split_axis=0, c...  17.5 us
    all_to_all x1, blocking collectives, per_device(): lax.all_to_all(cross_kv, 'seq', split_axis=0, concat_axis=0, tiled=True)  17.3 us
    all_to_all x1, blocking collectives, per_device(): attn = lax.all_to_all(attn, 'seq', split_axis=0, concat_axis=0, tiled=True)  12.8 us
    pallas_call x1, Pallas kernels, per_device(): pl.pallas_call(far_kernel, grid_spec=pltpu.PrefetchScalarGridSpec(num_sca...  10.4 us
    all_to_all x1, blocking collectives, per_device(): heads = lax.all_to_all(mine, 'seq', split_axis=0, concat_axis=0, tiled=True)  8.72 us
    pallas_call x1, Pallas kernels, per_device(): pl.pallas_call(near_kernel, grid=(NEAR // NEAR_BLOCK,), in_specs=[pl.Bloc...  7.43 us
  transfers between devices with their start and end apart: 16, of which 6 were waited for; matrix products, arithmetic and copies ran while one was open for 1% of the time, Pallas kernels for 5%

profile of v7, /device:TPU:32, one launch (start us, length us, event | category | flops | bytes accessed | tf_op | source)
XLA Modules:
  0.0 135.1 jit_solution(18358555995097945837)
XLA Ops:
  0.6 1.6 %collective-permute-start = (bf16[256,1024]{1,0:T(8,128)(2,1)}, bf16[256,1024]{1,0:T(8,128)(2,1)S(1)}, u32[]{:S(2)}, u32[]{:S(2)}) collective-permute-start(bf16[256,1024]{1,0:T(8,128)(2,1)} %tokens.1), channel_id=1, source_target_pairs={{0,1},{1,0},{2,3},{3,2},{4,5},{5,4},{6,7},{7,6},{8,9},{9,8},{10,11... | collective-permute-start | bytes 1572872 | tf_op jit(solution)/shard_map/ppermute | solution.py:43
  2.2 1.6 %collective-permute-start.1 = (bf16[256,1024]{1,0:T(8,128)(2,1)}, bf16[256,1024]{1,0:T(8,128)(2,1)S(1)}, u32[]{:S(2)}, u32[]{:S(2)}) collective-permute-start(bf16[256,1024]{1,0:T(8,128)(2,1)} %tokens.1), channel_id=1, source_target_pairs={{0,2},{1,3},{2,4},{3,5},{4,6},{5,7},{6,0},{7,1},{8,10},{9,11},{10,... | collective-permute-start | bytes 1572872 | tf_op jit(solution)/shard_map/ppermute | solution.py:43
  3.8 1.7 %collective-permute-start.2 = (bf16[256,1024]{1,0:T(8,128)(2,1)}, bf16[256,1024]{1,0:T(8,128)(2,1)S(1)}, u32[]{:S(2)}, u32[]{:S(2)}) collective-permute-start(bf16[256,1024]{1,0:T(8,128)(2,1)} %tokens.1), channel_id=1, source_target_pairs={{0,6},{1,7},{2,0},{3,1},{4,2},{5,3},{6,4},{7,5},{8,14},{9,15},{10,... | collective-permute-start | bytes 1572872 | tf_op jit(solution)/shard_map/ppermute | solution.py:43
  5.5 0.7 constant_dynamic-slice_fusion.2
  6.2 0.5 collective-permute-start.3
  6.7 3.4 %collective-permute-done.3 = bf16[32,384]{1,0:T(8,128)(2,1)S(1)} collective-permute-done((bf16[32,384]{1,0:T(8,128)(2,1)S(1)}, bf16[32,384]{1,0:T(8,128)(2,1)S(1)}, u32[]{:S(2)}, u32[]{:S(2)}) %collective-permute-start.3) | collective-permute-done | bytes 24608 | tf_op jit(solution)/shard_map/ppermute | solution.py:43
  10.1 3.3 %collective-permute-start.4 = (bf16[64,384]{1,0:T(8,128)(2,1)S(1)}, bf16[64,384]{1,0:T(8,128)(2,1)S(1)}, u32[]{:S(2)}, u32[]{:S(2)}) collective-permute-start(bf16[64,384]{1,0:T(8,128)(2,1)S(1)} %pad_maximum_fusion.2), channel_id=1, source_target_pairs={{0,32},{8,40},{16,48},{24,56},{32,0},{40,8},{48,16},{56,24},{64,96... | collective-permute-start | bytes 147464 | tf_op jit(solution)/shard_map/ppermute | solution.py:43
  13.4 2.1 %collective-permute-done.4 = bf16[64,384]{1,0:T(8,128)(2,1)S(1)} collective-permute-done((bf16[64,384]{1,0:T(8,128)(2,1)S(1)}, bf16[64,384]{1,0:T(8,128)(2,1)S(1)}, u32[]{:S(2)}, u32[]{:S(2)}) %collective-permute-start.4) | collective-permute-done | bytes 49184 | tf_op jit(solution)/shard_map/ppermute | solution.py:43
  15.5 0.0 collective-permute-done.peer
  15.5 1.6 %collective-permute-done.1.up = bf16[256,1024]{1,0:T(8,128)(2,1)S(1)} collective-permute-done((bf16[256,1024]{1,0:T(8,128)(2,1)}, bf16[256,1024]{1,0:T(8,128)(2,1)S(1)}, u32[]{:S(2)}, u32[]{:S(2)}) %collective-permute-start.1) | collective-permute-done | bytes 524320 | tf_op jit(solution)/shard_map/ppermute | solution.py:43
  17.1 0.0 collective-permute-done.2.down
  17.1 6.3 %collective-permute-start.5 = (bf16[128,384]{1,0:T(8,128)(2,1)S(1)}, bf16[128,384]{1,0:T(8,128)(2,1)S(1)}, u32[]{:S(2)}, u32[]{:S(2)}) collective-permute-start(bf16[128,384]{1,0:T(8,128)(2,1)S(1)} %pad_maximum_fusion.1), channel_id=1, source_target_pairs={{0,64},{8,72},{16,80},{24,88},{32,96},{40,104},{48,112},{56,120},{... | collective-permute-start | bytes 294920 | tf_op jit(solution)/shard_map/ppermute | solution.py:43
  23.4 2.7 %collective-permute-start.6 = (bf16[128,384]{1,0:T(8,128)(2,1)S(1)}, bf16[128,384]{1,0:T(8,128)(2,1)S(1)}, u32[]{:S(2)}, u32[]{:S(2)}) collective-permute-start(bf16[128,384]{1,0:T(8,128)(2,1)S(1)} %pad_maximum_fusion.1), channel_id=1, source_target_pairs={{0,128},{8,136},{16,144},{24,152},{32,160},{40,168},{48,176},{56,1... | collective-permute-start | bytes 294920 | tf_op jit(solution)/shard_map/ppermute | solution.py:43
  26.1 0.2 collective-permute-start.7
  26.4 1.6 %collective-permute-start.10 = (bf16[128,1024]{1,0:T(8,128)(2,1)S(1)}, bf16[128,1024]{1,0:T(8,128)(2,1)}, u32[]{:S(2)}, u32[]{:S(2)}) collective-permute-start(bf16[128,1024]{1,0:T(8,128)(2,1)S(1)} %slice.6), channel_id=1, source_target_pairs={{0,2},{1,3},{2,4},{3,5},{4,6},{5,7},{6,0},{7,1},{8,10},{9,11},{10,... | collective-permute-start | bytes 786440 | tf_op jit(solution)/shard_map/ppermute | solution.py:43
  28.1 1.7 %collective-permute-start.12 = (bf16[128,1024]{1,0:T(8,128)(2,1)S(1)}, bf16[128,1024]{1,0:T(8,128)(2,1)}, u32[]{:S(2)}, u32[]{:S(2)}) collective-permute-start(bf16[128,1024]{1,0:T(8,128)(2,1)S(1)} %slice.7), channel_id=1, source_target_pairs={{0,6},{1,7},{2,0},{3,1},{4,2},{5,3},{6,4},{7,5},{8,14},{9,15},{10,... | collective-permute-start | bytes 786440 | tf_op jit(solution)/shard_map/ppermute | solution.py:43
  29.8 0.0 collective-permute-done.5
  29.8 0.0 collective-permute-done.6
  29.8 7.3 %collective-permute-done.7 = bf16[128,384]{1,0:T(8,128)(2,1)S(1)} collective-permute-done((bf16[128,384]{1,0:T(8,128)(2,1)S(1)}, bf16[128,384]{1,0:T(8,128)(2,1)S(1)}, u32[]{:S(2)}, u32[]{:S(2)}) %collective-permute-start.7) | collective-permute-done | bytes 98336 | tf_op jit(solution)/shard_map/ppermute | solution.py:43
  37.1 1.6 %collective-permute-start.8 = (bf16[256,1024]{1,0:T(8,128)(2,1)S(1)}, bf16[256,1024]{1,0:T(8,128)(2,1)S(1)}, u32[]{:S(2)}, u32[]{:S(2)}) collective-permute-start(bf16[256,1024]{1,0:T(8,128)(2,1)S(1)} %collective-permute-done.peer), channel_id=1, source_target_pairs={{0,2},{1,3},{2,4},{3,5},{4,6},{5,7},{6,0},{7,1},{8,10},{9,11},{10,... | collective-permute-start | bytes 1572872 | tf_op jit(solution)/shard_map/ppermute | solution.py:43
  38.8 1.7 %collective-permute-start.9 = (bf16[256,1024]{1,0:T(8,128)(2,1)S(1)}, bf16[256,1024]{1,0:T(8,128)(2,1)S(1)}, u32[]{:S(2)}, u32[]{:S(2)}) collective-permute-start(bf16[256,1024]{1,0:T(8,128)(2,1)S(1)} %collective-permute-done.peer), channel_id=1, source_target_pairs={{0,6},{1,7},{2,0},{3,1},{4,2},{5,3},{6,4},{7,5},{8,14},{9,15},{10,... | collective-permute-start | bytes 1572872 | tf_op jit(solution)/shard_map/ppermute | solution.py:43
  40.4 0.0 collective-permute-start.14
  40.4 0.0 collective-permute-done.10.up_far
  40.4 0.2 collective-permute-start.11
  40.7 0.0 collective-permute-done.12.down_far
  40.7 1.8 %collective-permute-start.13 = (bf16[128,1024]{1,0:T(8,128)(2,1)}, bf16[128,1024]{1,0:T(8,128)(2,1)}, u32[]{:S(2)}, u32[]{:S(2)}) collective-permute-start(bf16[128,1024]{1,0:T(8,128)(2,1)} %collective-permute-done.12.down_far), channel_id=1, source_target_pairs={{0,1},{1,0},{2,3},{3,2},{4,5},{5,4},{6,7},{7,6},{8,9},{9,8},{10,11... | collective-permute-start | bytes 786440 | tf_op jit(solution)/shard_map/ppermute | solution.py:43
  42.5 0.1 stack.44.table
  42.6 0.1 pad_add_fusion.place
  42.6 0.0 collective-permute-done.14.twin
  42.6 7.4 %shard_map.86 = (bf16[1280,128]{1,0:T(8,128)(2,1)S(1)}, bf16[128,1280]{1,0:T(8,128)(2,1)S(1)}, bf16[1280,256]{1,0:T(8,128)(2,1)S(1)}, bf16[1024,384]{1,0:T(8,128...) custom-call(s32[2]{0:T(128)S(1)} %pad_add_fusion.place, bf16[256,1024]{1,0:T(8,128)(2,1)S(1)} %copy-done.1, ...), custom_call_target="tpu_custom_call" | custom-call | flops 1006632960 | bytes 4194304 | tf_op jit(solution)/shard_map/pallas_call | solution.py:283
  50.1 0.0 collective-permute-done.11.refs_2_
  50.1 5.0 %collective-permute-done.13.refs_3_ = bf16[128,1024]{1,0:T(8,128)(2,1)} collective-permute-done((bf16[128,1024]{1,0:T(8,128)(2,1)}, bf16[128,1024]{1,0:T(8,128)(2,1)}, u32[]{:S(2)}, u32[]{:S(2)}) %collective-permute-start.13) | collective-permute-done | bytes 262176 | tf_op jit(solution)/shard_map/ppermute | solution.py:43
  55.1 0.0 collective-permute-done.8.refs_0_
  55.1 0.0 copy-start.2
  55.1 0.0 copy-start.3
  55.1 10.4 %shard_map.87 = bf16[8,256,128]{2,1,0:T(8,128)(2,1)S(1)} custom-call(s32[8]{0:T(128)S(1)} %stack.44.table, bf16[256,1024]{1,0:T(8,128)(2,1)S(1)} %collective-permute-done.8.refs_0_, bf16[256,1024]{1,0:T(8,128)(2,1)S(1)} %collective-permute-done.9.refs_1_, bf16[128,1024]{1,0:T(8,128)(2,1)} %collective-permute-done.11.refs_2_, ...), custom_call_target="tpu_custom_call" | custom-call | flops 6442450944 | bytes 4194304 | tf_op jit(solution)/shard_map/pallas_call | solution.py:302
  65.5 12.8 %all_to_all.20.attn = bf16[8,256,128]{2,1,0:T(8,128)(2,1)S(1)} all-to-all(bf16[8,256,128]{2,1,0:T(8,128)(2,1)S(1)} %shard_map.87), channel_id=1, replica_groups=mesh['span'=32,'seq'=8] {'seq'}, dimensions={0} | all-to-all | bytes 1048576 | tf_op jit(solution)/shard_map/all_to_all | solution.py:328
  78.3 3.6 %shard_map.88 = (bf16[256,1024]{1,0:T(8,128)(2,1)}, bf16[8,256,256]{2,1,0:T(8,128)(2,1)S(1)}) custom-call(bf16[8,256,128]{2,1,0:T(8,128)(2,1)S(1)} %all_to_all.20.attn, bf16[256,1024]{1,0:T(8,128)(2,1)S(1)} %copy-done.1, bf16[1024,1024]{1,0:T(8,128)(2,1)S(1)} %copy-done, f32[1,1024]{1,0:T(1,128)S(1)} %bitcast.22, f32[1,1024]{1,0:T(1,128)S(1)} %bitcast.23, ...), custom_call_target="tpu_custom_call" | custom-call | flops 1610612736 | bytes 8388608 | tf_op jit(solution)/shard_map/pallas_call | solution.py:330
  81.9 0.0 copy-start.4
  81.9 17.3 %all_to_all.21 = bf16[8,256,256]{2,1,0:T(8,128)(2,1)S(1)} all-to-all(bf16[8,256,256]{2,1,0:T(8,128)(2,1)S(1)} %get-tuple-element.31), channel_id=1, replica_groups=mesh['span'=32,'seq'=8] {'seq'}, dimensions={0} | all-to-all | bytes 2097152 | tf_op jit(solution)/shard_map/all_to_all | solution.py:344
  99.2 6.4 %shard_map.89 = (f32[512,256]{1,0:T(8,128)S(1)}, f32[512,256]{1,0:T(8,128)S(1)}) custom-call(s32[2]{0:T(128)S(1)} %pad_add_fusion.place, bf16[1024,1024]{1,0:T(8,128)(2,1)S(1)} %copy-done.4, bf16[2048,256]{1,0:T(8,128)(2,1)S(1)} %bitcast.21), custom_call_target="tpu_custom_call" | custom-call | flops 4294967296 | bytes 2097152 | tf_op jit(solution)/shard_map/pallas_call | solution.py:348
  105.6 0.1 collective-permute-start.15
  105.7 1.9 %collective-permute-done.15.received = f32[512,256]{1,0:T(8,128)S(1)} collective-permute-done((f32[512,256]{1,0:T(8,128)S(1)}, f32[512,256]{1,0:T(8,128)S(1)}, u32[]{:S(2)}, u32[]{:S(2)}) %collective-permute-start.15) | collective-permute-done | bytes 524320 | tf_op jit(solution)/shard_map/ppermute | solution.py:43
  107.6 0.2 shard_map.90
  107.9 17.5 %all_to_all.22.parts = bf16[16,32,256]{2,1,0:T(8,128)(2,1)S(1)} all-to-all(bf16[16,32,256]{2,1,0:T(8,128)(2,1)S(1)} %bitcast.20), channel_id=1, replica_groups={{0,16,32,48,64,80,96,112,128,144,160,176,192,208,224,240},{8,24,40,56,7..., dimensions={0} | all-to-all | bytes 524288 | tf_op jit(solution)/shard_map/all_to_all | solution.py:382
  125.4 0.4 shard_map.91
  125.8 8.7 %all_to_all.23 = bf16[8,32,128]{2,1,0:T(8,128)(2,1)S(1)} all-to-all(bf16[8,32,128]{2,1,0:T(8,128)(2,1)S(1)} %shard_map.91), channel_id=1, replica_groups=mesh['span'=32,'seq'=8] {'seq'}, dimensions={0} | all-to-all | bytes 131072 | tf_op jit(solution)/shard_map/all_to_all | solution.py:395
  134.5 0.6 copy_bitcast_fusion
  (14 shorter events, 0.1 us)
Async XLA Ops:
  0.6 42.0 %copy-start.1 = (bf16[256,1024]{1,0:T(8,128)(2,1)S(1)}, bf16[256,1024]{1,0:T(8,128)(2,1)}, u32[]{:S(2)}) copy-start(bf16[256,1024]{1,0:T(8,128)(2,1)} %tokens.1) | copy-start | bytes 1572868
  0.6 14.8 %collective-permute-start = (bf16[256,1024]{1,0:T(8,128)(2,1)}, bf16[256,1024]{1,0:T(8,128)(2,1)S(1)}, u32[]{:S(2)}, u32[]{:S(2)}) collective-permute-start(bf16[256,1024]{1,0:T(8,128)(2,1)} %tokens.1), channel_id=1, source_target_pairs={{0,1},{1,0},{2,3},{3,2},{4,5},{5,4},{6,7},{7,6},{8,9},{9,8},{10,11... | collective-permute-start | bytes 1572872 | tf_op jit(solution)/shard_map/ppermute | solution.py:43
  2.2 14.9 %collective-permute-start.1 = (bf16[256,1024]{1,0:T(8,128)(2,1)}, bf16[256,1024]{1,0:T(8,128)(2,1)S(1)}, u32[]{:S(2)}, u32[]{:S(2)}) collective-permute-start(bf16[256,1024]{1,0:T(8,128)(2,1)} %tokens.1), channel_id=1, source_target_pairs={{0,2},{1,3},{2,4},{3,5},{4,6},{5,7},{6,0},{7,1},{8,10},{9,11},{10,... | collective-permute-start | bytes 1572872 | tf_op jit(solution)/shard_map/ppermute | solution.py:43
  3.8 13.3 %collective-permute-start.2 = (bf16[256,1024]{1,0:T(8,128)(2,1)}, bf16[256,1024]{1,0:T(8,128)(2,1)S(1)}, u32[]{:S(2)}, u32[]{:S(2)}) collective-permute-start(bf16[256,1024]{1,0:T(8,128)(2,1)} %tokens.1), channel_id=1, source_target_pairs={{0,6},{1,7},{2,0},{3,1},{4,2},{5,3},{6,4},{7,5},{8,14},{9,15},{10,... | collective-permute-start | bytes 1572872 | tf_op jit(solution)/shard_map/ppermute | solution.py:43
  6.2 3.9 %collective-permute-start.3 = (bf16[32,384]{1,0:T(8,128)(2,1)S(1)}, bf16[32,384]{1,0:T(8,128)(2,1)S(1)}, u32[]{:S(2)}, u32[]{:S(2)}) collective-permute-start(bf16[32,384]{1,0:T(8,128)(2,1)S(1)} %pad_maximum_fusion.3), channel_id=1, source_target_pairs={{0,16},{8,24},{16,0},{24,8},{32,48},{40,56},{48,32},{56,40},{64,80... | collective-permute-start | bytes 73736 | tf_op jit(solution)/shard_map/ppermute | solution.py:43
  10.1 5.3 %collective-permute-start.4 = (bf16[64,384]{1,0:T(8,128)(2,1)S(1)}, bf16[64,384]{1,0:T(8,128)(2,1)S(1)}, u32[]{:S(2)}, u32[]{:S(2)}) collective-permute-start(bf16[64,384]{1,0:T(8,128)(2,1)S(1)} %pad_maximum_fusion.2), channel_id=1, source_target_pairs={{0,32},{8,40},{16,48},{24,56},{32,0},{40,8},{48,16},{56,24},{64,96... | collective-permute-start | bytes 147464 | tf_op jit(solution)/shard_map/ppermute | solution.py:43
  17.1 12.7 %collective-permute-start.5 = (bf16[128,384]{1,0:T(8,128)(2,1)S(1)}, bf16[128,384]{1,0:T(8,128)(2,1)S(1)}, u32[]{:S(2)}, u32[]{:S(2)}) collective-permute-start(bf16[128,384]{1,0:T(8,128)(2,1)S(1)} %pad_maximum_fusion.1), channel_id=1, source_target_pairs={{0,64},{8,72},{16,80},{24,88},{32,96},{40,104},{48,112},{56,120},{... | collective-permute-start | bytes 294920 | tf_op jit(solution)/shard_map/ppermute | solution.py:43
  23.4 6.4 %collective-permute-start.6 = (bf16[128,384]{1,0:T(8,128)(2,1)S(1)}, bf16[128,384]{1,0:T(8,128)(2,1)S(1)}, u32[]{:S(2)}, u32[]{:S(2)}) collective-permute-start(bf16[128,384]{1,0:T(8,128)(2,1)S(1)} %pad_maximum_fusion.1), channel_id=1, source_target_pairs={{0,128},{8,136},{16,144},{24,152},{32,160},{40,168},{48,176},{56,1... | collective-permute-start | bytes 294920 | tf_op jit(solution)/shard_map/ppermute | solution.py:43
  26.1 10.9 %collective-permute-start.7 = (bf16[128,384]{1,0:T(8,128)(2,1)S(1)}, bf16[128,384]{1,0:T(8,128)(2,1)S(1)}, u32[]{:S(2)}, u32[]{:S(2)}) collective-permute-start(bf16[128,384]{1,0:T(8,128)(2,1)S(1)} %pad_maximum_fusion.1), channel_id=1, source_target_pairs={{0,192},{8,200},{16,208},{24,216},{32,224},{40,232},{48,240},{56,2... | collective-permute-start | bytes 294920 | tf_op jit(solution)/shard_map/ppermute | solution.py:43
  26.4 14.0 %collective-permute-start.10 = (bf16[128,1024]{1,0:T(8,128)(2,1)S(1)}, bf16[128,1024]{1,0:T(8,128)(2,1)}, u32[]{:S(2)}, u32[]{:S(2)}) collective-permute-start(bf16[128,1024]{1,0:T(8,128)(2,1)S(1)} %slice.6), channel_id=1, source_target_pairs={{0,2},{1,3},{2,4},{3,5},{4,6},{5,7},{6,0},{7,1},{8,10},{9,11},{10,... | collective-permute-start | bytes 786440 | tf_op jit(solution)/shard_map/ppermute | solution.py:43
  28.1 12.6 %collective-permute-start.12 = (bf16[128,1024]{1,0:T(8,128)(2,1)S(1)}, bf16[128,1024]{1,0:T(8,128)(2,1)}, u32[]{:S(2)}, u32[]{:S(2)}) collective-permute-start(bf16[128,1024]{1,0:T(8,128)(2,1)S(1)} %slice.7), channel_id=1, source_target_pairs={{0,6},{1,7},{2,0},{3,1},{4,2},{5,3},{6,4},{7,5},{8,14},{9,15},{10,... | collective-permute-start | bytes 786440 | tf_op jit(solution)/shard_map/ppermute | solution.py:43
  37.1 18.0 %collective-permute-start.8 = (bf16[256,1024]{1,0:T(8,128)(2,1)S(1)}, bf16[256,1024]{1,0:T(8,128)(2,1)S(1)}, u32[]{:S(2)}, u32[]{:S(2)}) collective-permute-start(bf16[256,1024]{1,0:T(8,128)(2,1)S(1)} %collective-permute-done.peer), channel_id=1, source_target_pairs={{0,2},{1,3},{2,4},{3,5},{4,6},{5,7},{6,0},{7,1},{8,10},{9,11},{10,... | collective-permute-start | bytes 1572872 | tf_op jit(solution)/shard_map/ppermute | solution.py:43
  38.8 16.3 %collective-permute-start.9 = (bf16[256,1024]{1,0:T(8,128)(2,1)S(1)}, bf16[256,1024]{1,0:T(8,128)(2,1)S(1)}, u32[]{:S(2)}, u32[]{:S(2)}) collective-permute-start(bf16[256,1024]{1,0:T(8,128)(2,1)S(1)} %collective-permute-done.peer), channel_id=1, source_target_pairs={{0,6},{1,7},{2,0},{3,1},{4,2},{5,3},{6,4},{7,5},{8,14},{9,15},{10,... | collective-permute-start | bytes 1572872 | tf_op jit(solution)/shard_map/ppermute | solution.py:43
  40.4 2.2 %collective-permute-start.14 = (bf16[512,384]{1,0:T(8,128)(2,1)S(1)}, bf16[512,384]{1,0:T(8,128)(2,1)}, u32[]{:S(2)}, u32[]{:S(2)}) collective-permute-start(bf16[512,384]{1,0:T(8,128)(2,1)S(1)} %pad_maximum_fusion.mine), channel_id=1, source_target_pairs={{0,8},{8,0},{16,24},{24,16},{32,40},{40,32},{48,56},{56,48},{64,72... | collective-permute-start | bytes 1179656 | tf_op jit(solution)/shard_map/ppermute | solution.py:43
  40.4 9.6 %collective-permute-start.11 = (bf16[128,1024]{1,0:T(8,128)(2,1)}, bf16[128,1024]{1,0:T(8,128)(2,1)}, u32[]{:S(2)}, u32[]{:S(2)}) collective-permute-start(bf16[128,1024]{1,0:T(8,128)(2,1)} %collective-permute-done.10.up_far), channel_id=1, source_target_pairs={{0,1},{1,0},{2,3},{3,2},{4,5},{5,4},{6,7},{7,6},{8,9},{9,8},{10,11... | collective-permute-start | bytes 786440 | tf_op jit(solution)/shard_map/ppermute | solution.py:43
  40.7 14.4 %collective-permute-start.13 = (bf16[128,1024]{1,0:T(8,128)(2,1)}, bf16[128,1024]{1,0:T(8,128)(2,1)}, u32[]{:S(2)}, u32[]{:S(2)}) collective-permute-start(bf16[128,1024]{1,0:T(8,128)(2,1)} %collective-permute-done.12.down_far), channel_id=1, source_target_pairs={{0,1},{1,0},{2,3},{3,2},{4,5},{5,4},{6,7},{7,6},{8,9},{9,8},{10,11... | collective-permute-start | bytes 786440 | tf_op jit(solution)/shard_map/ppermute | solution.py:43
  55.1 23.2 %copy-start = (bf16[1024,1024]{1,0:T(8,128)(2,1)S(1)}, bf16[1024,1024]{1,0:T(8,128)(2,1)}, u32[]{:S(2)}) copy-start(bf16[1024,1024]{1,0:T(8,128)(2,1)} %w_out.1) | copy-start | bytes 6291460
  55.1 23.2 %copy-start.2 = (f32[1024]{0:T(1024)S(1)}, f32[1024]{0:T(1024)}, u32[]{:S(2)}) copy-start(f32[1024]{0:T(1024)} %param.11) | copy-start | bytes 12292
  55.1 23.2 %copy-start.3 = (f32[1024]{0:T(1024)S(1)}, f32[1024]{0:T(1024)}, u32[]{:S(2)}) copy-start(f32[1024]{0:T(1024)} %param.12) | copy-start | bytes 12292
  81.9 17.3 %copy-start.4 = (bf16[1024,1024]{1,0:T(8,128)(2,1)S(1)}, bf16[1024,1024]{1,0:T(8,128)(2,1)}, u32[]{:S(2)}) copy-start(bf16[1024,1024]{1,0:T(8,128)(2,1)} %queries.1) | copy-start | bytes 6291460
  105.6 2.0 %collective-permute-start.15 = (f32[512,256]{1,0:T(8,128)S(1)}, f32[512,256]{1,0:T(8,128)S(1)}, u32[]{:S(2)}, u32[]{:S(2)}) collective-permute-start(f32[512,256]{1,0:T(8,128)S(1)} %get-tuple-element.33), channel_id=1, source_target_pairs={{0,8},{8,0},{16,24},{24,16},{32,40},{40,32},{48,56},{56,48},{64,72... | collective-permute-start | bytes 1572872 | tf_op jit(solution)/shard_map/ppermute | solution.py:43

commit v8 on v7

--- a/solution.py
+++ b/solution.py
@@ -19,7 +19,7 @@
 NQ = 1024
 STAT_LANES = 16
 BLOCK = 512
-SPREAD = (2, 4, 8, 16)
+SPREAD = (4, 8, 2, 16)
 NEAR, FAR = 5 * ROWS, 3 * ROWS
 NEAR_BLOCK, FAR_BLOCK = 640, 384
 FAR_PIECES = 4

time: 136 us -> 131 us (0.963)
  waiting for transfers between devices: 21.3 us -> 13.2 us
  blocking collectives: 56.4 us -> 58.1 us
    ppermute x16, waiting for transfers between devices: 21.3 us -> 13.2 us  [permute(): return lax.ppermute(x, axis, [(i, target(i)) for i in range(size)])]
    all_to_all x1, blocking collectives: 17.5 us -> 19.8 us  [per_device(): lax.all_to_all(merged.reshape(16, OWN, 2 * PAIR), 'span', split_axis=0, c...]
  transfers between devices with their start and end apart: 16 -> 16, of which waited for: 6 -> 6; matrix products, arithmetic and copies ran while one was open for 1% -> 1% of each run, Pallas kernels for 5% -> 6%
where the time goes in v8:
time: 131 us; the launch traced here: 130 us
  blocking collectives  58.1 us (44%)
  Pallas kernels  28.4 us (22%)
  starting transfers between devices  28 us (21%)
  waiting for transfers between devices  13.2 us (10%)
  local copies, waits for them, and re-layouts  1.52 us (1%)
    ppermute x16, starting transfers between devices, permute(): return lax.ppermute(x, axis, [(i, target(i)) for i in range(size)])  28 us
    all_to_all x1, blocking collectives, per_device(): lax.all_to_all(merged.reshape(16, OWN, 2 * PAIR), 'span', split_axis=0, c...  19.8 us
    all_to_all x1, blocking collectives, per_device(): lax.all_to_all(cross_kv, 'seq', split_axis=0, concat_axis=0, tiled=True)  17.2 us
    ppermute x16, waiting for transfers between devices, permute(): return lax.ppermute(x, axis, [(i, target(i)) for i in range(size)])  13.2 us
    all_to_all x1, blocking collectives, per_device(): attn = lax.all_to_all(attn, 'seq', split_axis=0, concat_axis=0, tiled=True)  12.2 us
    pallas_call x1, Pallas kernels, per_device(): pl.pallas_call(far_kernel, grid_spec=pltpu.PrefetchScalarGridSpec(num_sca...  10.4 us
    all_to_all x1, blocking collectives, per_device(): heads = lax.all_to_all(mine, 'seq', split_axis=0, concat_axis=0, tiled=True)  8.87 us
    pallas_call x1, Pallas kernels, per_device(): pl.pallas_call(near_kernel, grid=(NEAR // NEAR_BLOCK,), in_specs=[pl.Bloc...  7.43 us
  transfers between devices with their start and end apart: 16, of which 6 were waited for; matrix products, arithmetic and copies ran while one was open for 1% of the time, Pallas kernels for 6%

profile of v8, /device:TPU:32, one launch (start us, length us, event | category | flops | bytes accessed | tf_op | source)
XLA Modules:
  0.0 130.1 jit_solution(6314044453261407162)
XLA Ops:
  0.6 1.6 %collective-permute-start = (bf16[256,1024]{1,0:T(8,128)(2,1)}, bf16[256,1024]{1,0:T(8,128)(2,1)S(1)}, u32[]{:S(2)}, u32[]{:S(2)}) collective-permute-start(bf16[256,1024]{1,0:T(8,128)(2,1)} %tokens.1), channel_id=1, source_target_pairs={{0,1},{1,0},{2,3},{3,2},{4,5},{5,4},{6,7},{7,6},{8,9},{9,8},{10,11... | collective-permute-start | bytes 1572872 | tf_op jit(solution)/shard_map/ppermute | solution.py:43
  2.2 1.6 %collective-permute-start.1 = (bf16[256,1024]{1,0:T(8,128)(2,1)}, bf16[256,1024]{1,0:T(8,128)(2,1)S(1)}, u32[]{:S(2)}, u32[]{:S(2)}) collective-permute-start(bf16[256,1024]{1,0:T(8,128)(2,1)} %tokens.1), channel_id=1, source_target_pairs={{0,2},{1,3},{2,4},{3,5},{4,6},{5,7},{6,0},{7,1},{8,10},{9,11},{10,... | collective-permute-start | bytes 1572872 | tf_op jit(solution)/shard_map/ppermute | solution.py:43
  3.8 1.7 %collective-permute-start.2 = (bf16[256,1024]{1,0:T(8,128)(2,1)}, bf16[256,1024]{1,0:T(8,128)(2,1)S(1)}, u32[]{:S(2)}, u32[]{:S(2)}) collective-permute-start(bf16[256,1024]{1,0:T(8,128)(2,1)} %tokens.1), channel_id=1, source_target_pairs={{0,6},{1,7},{2,0},{3,1},{4,2},{5,3},{6,4},{7,5},{8,14},{9,15},{10,... | collective-permute-start | bytes 1572872 | tf_op jit(solution)/shard_map/ppermute | solution.py:43
  5.5 0.7 constant_dynamic-slice_fusion.2
  6.2 3.3 %collective-permute-start.3 = (bf16[32,384]{1,0:T(8,128)(2,1)S(1)}, bf16[32,384]{1,0:T(8,128)(2,1)S(1)}, u32[]{:S(2)}, u32[]{:S(2)}) collective-permute-start(bf16[32,384]{1,0:T(8,128)(2,1)S(1)} %pad_maximum_fusion.3), channel_id=1, source_target_pairs={{0,32},{8,40},{16,48},{24,56},{32,0},{40,8},{48,16},{56,24},{64,96... | collective-permute-start | bytes 73736 | tf_op jit(solution)/shard_map/ppermute | solution.py:43
  9.5 1.8 %collective-permute-done.3 = bf16[32,384]{1,0:T(8,128)(2,1)S(1)} collective-permute-done((bf16[32,384]{1,0:T(8,128)(2,1)S(1)}, bf16[32,384]{1,0:T(8,128)(2,1)S(1)}, u32[]{:S(2)}, u32[]{:S(2)}) %collective-permute-start.3) | collective-permute-done | bytes 24608 | tf_op jit(solution)/shard_map/ppermute | solution.py:43
  11.4 5.9 %collective-permute-start.4 = (bf16[64,384]{1,0:T(8,128)(2,1)S(1)}, bf16[64,384]{1,0:T(8,128)(2,1)S(1)}, u32[]{:S(2)}, u32[]{:S(2)}) collective-permute-start(bf16[64,384]{1,0:T(8,128)(2,1)S(1)} %pad_maximum_fusion.2), channel_id=1, source_target_pairs={{0,64},{8,72},{16,80},{24,88},{32,96},{40,104},{48,112},{56,120},{... | collective-permute-start | bytes 147464 | tf_op jit(solution)/shard_map/ppermute | solution.py:43
  17.3 2.2 %collective-permute-done.4 = bf16[64,384]{1,0:T(8,128)(2,1)S(1)} collective-permute-done((bf16[64,384]{1,0:T(8,128)(2,1)S(1)}, bf16[64,384]{1,0:T(8,128)(2,1)S(1)}, u32[]{:S(2)}, u32[]{:S(2)}) %collective-permute-start.4) | collective-permute-done | bytes 49184 | tf_op jit(solution)/shard_map/ppermute | solution.py:43
  19.5 0.0 collective-permute-done.peer
  19.5 0.0 collective-permute-done.1.up
  19.5 0.0 collective-permute-done.2.down
  19.5 1.1 collective-permute-start.5
  20.6 2.7 %collective-permute-start.6 = (bf16[128,384]{1,0:T(8,128)(2,1)S(1)}, bf16[128,384]{1,0:T(8,128)(2,1)S(1)}, u32[]{:S(2)}, u32[]{:S(2)}) collective-permute-start(bf16[128,384]{1,0:T(8,128)(2,1)S(1)} %pad_maximum_fusion.1), channel_id=1, source_target_pairs={{0,128},{8,136},{16,144},{24,152},{32,160},{40,168},{48,176},{56,1... | collective-permute-start | bytes 294920 | tf_op jit(solution)/shard_map/ppermute | solution.py:43
  23.3 1.3 collective-permute-start.7
  24.6 0.3 collective-permute-start.10
  25.0 3.1 %collective-permute-start.12 = (bf16[128,1024]{1,0:T(8,128)(2,1)S(1)}, bf16[128,1024]{1,0:T(8,128)(2,1)}, u32[]{:S(2)}, u32[]{:S(2)}) collective-permute-start(bf16[128,1024]{1,0:T(8,128)(2,1)S(1)} %slice.7), channel_id=1, source_target_pairs={{0,6},{1,7},{2,0},{3,1},{4,2},{5,3},{6,4},{7,5},{8,14},{9,15},{10,... | collective-permute-start | bytes 786440 | tf_op jit(solution)/shard_map/ppermute | solution.py:43
  28.0 0.0 collective-permute-done.5
  28.0 0.0 collective-permute-done.6
  28.0 2.3 %collective-permute-done.7 = bf16[128,384]{1,0:T(8,128)(2,1)S(1)} collective-permute-done((bf16[128,384]{1,0:T(8,128)(2,1)S(1)}, bf16[128,384]{1,0:T(8,128)(2,1)S(1)}, u32[]{:S(2)}, u32[]{:S(2)}) %collective-permute-start.7) | collective-permute-done | bytes 98336 | tf_op jit(solution)/shard_map/ppermute | solution.py:43
  30.4 0.5 collective-permute-start.8
  30.9 2.8 %collective-permute-start.9 = (bf16[256,1024]{1,0:T(8,128)(2,1)S(1)}, bf16[256,1024]{1,0:T(8,128)(2,1)S(1)}, u32[]{:S(2)}, u32[]{:S(2)}) collective-permute-start(bf16[256,1024]{1,0:T(8,128)(2,1)S(1)} %collective-permute-done.peer), channel_id=1, source_target_pairs={{0,6},{1,7},{2,0},{3,1},{4,2},{5,3},{6,4},{7,5},{8,14},{9,15},{10,... | collective-permute-start | bytes 1572872 | tf_op jit(solution)/shard_map/ppermute | solution.py:43
  33.7 0.0 collective-permute-start.14
  33.7 0.4 collective-permute-done.10.up_far
  34.1 0.9 collective-permute-start.11
  35.0 0.0 collective-permute-done.12.down_far
  35.0 1.2 collective-permute-start.13
  36.2 0.1 stack.44.table
  36.3 0.1 pad_add_fusion.place
  36.3 0.0 collective-permute-done.14.twin
  36.3 7.4 %shard_map.86 = (bf16[1280,128]{1,0:T(8,128)(2,1)S(1)}, bf16[128,1280]{1,0:T(8,128)(2,1)S(1)}, bf16[1280,256]{1,0:T(8,128)(2,1)S(1)}, bf16[1024,384]{1,0:T(8,128...) custom-call(s32[2]{0:T(128)S(1)} %pad_add_fusion.place, bf16[256,1024]{1,0:T(8,128)(2,1)S(1)} %copy-done.1, ...), custom_call_target="tpu_custom_call" | custom-call | flops 1006632960 | bytes 4194304 | tf_op jit(solution)/shard_map/pallas_call | solution.py:283
  43.8 0.0 collective-permute-done.11.refs_2_
  43.8 4.6 %collective-permute-done.13.refs_3_ = bf16[128,1024]{1,0:T(8,128)(2,1)} collective-permute-done((bf16[128,1024]{1,0:T(8,128)(2,1)}, bf16[128,1024]{1,0:T(8,128)(2,1)}, u32[]{:S(2)}, u32[]{:S(2)}) %collective-permute-start.13) | collective-permute-done | bytes 262176 | tf_op jit(solution)/shard_map/ppermute | solution.py:43
  48.4 0.0 collective-permute-done.9.refs_1_
  48.4 0.0 copy-start.2
  48.4 0.0 copy-start.3
  48.4 10.4 %shard_map.87 = bf16[8,256,128]{2,1,0:T(8,128)(2,1)S(1)} custom-call(s32[8]{0:T(128)S(1)} %stack.44.table, bf16[256,1024]{1,0:T(8,128)(2,1)S(1)} %collective-permute-done.8.refs_0_, bf16[256,1024]{1,0:T(8,128)(2,1)S(1)} %collective-permute-done.9.refs_1_, bf16[128,1024]{1,0:T(8,128)(2,1)} %collective-permute-done.11.refs_2_, ...), custom_call_target="tpu_custom_call" | custom-call | flops 6442450944 | bytes 4194304 | tf_op jit(solution)/shard_map/pallas_call | solution.py:302
  58.8 12.2 %all_to_all.20.attn = bf16[8,256,128]{2,1,0:T(8,128)(2,1)S(1)} all-to-all(bf16[8,256,128]{2,1,0:T(8,128)(2,1)S(1)} %shard_map.87), channel_id=1, replica_groups=mesh['span'=32,'seq'=8] {'seq'}, dimensions={0} | all-to-all | bytes 1048576 | tf_op jit(solution)/shard_map/all_to_all | solution.py:328
  71.0 3.6 %shard_map.88 = (bf16[256,1024]{1,0:T(8,128)(2,1)}, bf16[8,256,256]{2,1,0:T(8,128)(2,1)S(1)}) custom-call(bf16[8,256,128]{2,1,0:T(8,128)(2,1)S(1)} %all_to_all.20.attn, bf16[256,1024]{1,0:T(8,128)(2,1)S(1)} %copy-done.1, bf16[1024,1024]{1,0:T(8,128)(2,1)S(1)} %copy-done, f32[1,1024]{1,0:T(1,128)S(1)} %bitcast.22, f32[1,1024]{1,0:T(1,128)S(1)} %bitcast.23, ...), custom_call_target="tpu_custom_call" | custom-call | flops 1610612736 | bytes 8388608 | tf_op jit(solution)/shard_map/pallas_call | solution.py:330
  74.6 0.0 copy-start.4
  74.6 17.2 %all_to_all.21 = bf16[8,256,256]{2,1,0:T(8,128)(2,1)S(1)} all-to-all(bf16[8,256,256]{2,1,0:T(8,128)(2,1)S(1)} %get-tuple-element.31), channel_id=1, replica_groups=mesh['span'=32,'seq'=8] {'seq'}, dimensions={0} | all-to-all | bytes 2097152 | tf_op jit(solution)/shard_map/all_to_all | solution.py:344
  91.8 6.4 %shard_map.89 = (f32[512,256]{1,0:T(8,128)S(1)}, f32[512,256]{1,0:T(8,128)S(1)}) custom-call(s32[2]{0:T(128)S(1)} %pad_add_fusion.place, bf16[1024,1024]{1,0:T(8,128)(2,1)S(1)} %copy-done.4, bf16[2048,256]{1,0:T(8,128)(2,1)S(1)} %bitcast.21), custom_call_target="tpu_custom_call" | custom-call | flops 4294967296 | bytes 2097152 | tf_op jit(solution)/shard_map/pallas_call | solution.py:348
  98.2 0.1 collective-permute-start.15
  98.3 1.9 %collective-permute-done.15.received = f32[512,256]{1,0:T(8,128)S(1)} collective-permute-done((f32[512,256]{1,0:T(8,128)S(1)}, f32[512,256]{1,0:T(8,128)S(1)}, u32[]{:S(2)}, u32[]{:S(2)}) %collective-permute-start.15) | collective-permute-done | bytes 524320 | tf_op jit(solution)/shard_map/ppermute | solution.py:43
  100.2 0.2 shard_map.90
  100.4 19.8 %all_to_all.22.parts = bf16[16,32,256]{2,1,0:T(8,128)(2,1)S(1)} all-to-all(bf16[16,32,256]{2,1,0:T(8,128)(2,1)S(1)} %bitcast.20), channel_id=1, replica_groups={{0,16,32,48,64,80,96,112,128,144,160,176,192,208,224,240},{8,24,40,56,7..., dimensions={0} | all-to-all | bytes 524288 | tf_op jit(solution)/shard_map/all_to_all | solution.py:382
  120.2 0.4 shard_map.91
  120.6 8.9 %all_to_all.23 = bf16[8,32,128]{2,1,0:T(8,128)(2,1)S(1)} all-to-all(bf16[8,32,128]{2,1,0:T(8,128)(2,1)S(1)} %shard_map.91), channel_id=1, replica_groups=mesh['span'=32,'seq'=8] {'seq'}, dimensions={0} | all-to-all | bytes 131072 | tf_op jit(solution)/shard_map/all_to_all | solution.py:395
  129.5 0.6 copy_bitcast_fusion
  (14 shorter events, 0.1 us)
Async XLA Ops:
  0.6 35.7 %copy-start.1 = (bf16[256,1024]{1,0:T(8,128)(2,1)S(1)}, bf16[256,1024]{1,0:T(8,128)(2,1)}, u32[]{:S(2)}) copy-start(bf16[256,1024]{1,0:T(8,128)(2,1)} %tokens.1) | copy-start | bytes 1572868
  0.6 18.8 %collective-permute-start = (bf16[256,1024]{1,0:T(8,128)(2,1)}, bf16[256,1024]{1,0:T(8,128)(2,1)S(1)}, u32[]{:S(2)}, u32[]{:S(2)}) collective-permute-start(bf16[256,1024]{1,0:T(8,128)(2,1)} %tokens.1), channel_id=1, source_target_pairs={{0,1},{1,0},{2,3},{3,2},{4,5},{5,4},{6,7},{7,6},{8,9},{9,8},{10,11... | collective-permute-start | bytes 1572872 | tf_op jit(solution)/shard_map/ppermute | solution.py:43
  2.2 17.3 %collective-permute-start.1 = (bf16[256,1024]{1,0:T(8,128)(2,1)}, bf16[256,1024]{1,0:T(8,128)(2,1)S(1)}, u32[]{:S(2)}, u32[]{:S(2)}) collective-permute-start(bf16[256,1024]{1,0:T(8,128)(2,1)} %tokens.1), channel_id=1, source_target_pairs={{0,2},{1,3},{2,4},{3,5},{4,6},{5,7},{6,0},{7,1},{8,10},{9,11},{10,... | collective-permute-start | bytes 1572872 | tf_op jit(solution)/shard_map/ppermute | solution.py:43
  3.8 15.7 %collective-permute-start.2 = (bf16[256,1024]{1,0:T(8,128)(2,1)}, bf16[256,1024]{1,0:T(8,128)(2,1)S(1)}, u32[]{:S(2)}, u32[]{:S(2)}) collective-permute-start(bf16[256,1024]{1,0:T(8,128)(2,1)} %tokens.1), channel_id=1, source_target_pairs={{0,6},{1,7},{2,0},{3,1},{4,2},{5,3},{6,4},{7,5},{8,14},{9,15},{10,... | collective-permute-start | bytes 1572872 | tf_op jit(solution)/shard_map/ppermute | solution.py:43
  6.2 5.2 %collective-permute-start.3 = (bf16[32,384]{1,0:T(8,128)(2,1)S(1)}, bf16[32,384]{1,0:T(8,128)(2,1)S(1)}, u32[]{:S(2)}, u32[]{:S(2)}) collective-permute-start(bf16[32,384]{1,0:T(8,128)(2,1)S(1)} %pad_maximum_fusion.3), channel_id=1, source_target_pairs={{0,32},{8,40},{16,48},{24,56},{32,0},{40,8},{48,16},{56,24},{64,96... | collective-permute-start | bytes 73736 | tf_op jit(solution)/shard_map/ppermute | solution.py:43
  11.4 8.1 %collective-permute-start.4 = (bf16[64,384]{1,0:T(8,128)(2,1)S(1)}, bf16[64,384]{1,0:T(8,128)(2,1)S(1)}, u32[]{:S(2)}, u32[]{:S(2)}) collective-permute-start(bf16[64,384]{1,0:T(8,128)(2,1)S(1)} %pad_maximum_fusion.2), channel_id=1, source_target_pairs={{0,64},{8,72},{16,80},{24,88},{32,96},{40,104},{48,112},{56,120},{... | collective-permute-start | bytes 147464 | tf_op jit(solution)/shard_map/ppermute | solution.py:43
  19.5 8.5 %collective-permute-start.5 = (bf16[128,384]{1,0:T(8,128)(2,1)S(1)}, bf16[128,384]{1,0:T(8,128)(2,1)S(1)}, u32[]{:S(2)}, u32[]{:S(2)}) collective-permute-start(bf16[128,384]{1,0:T(8,128)(2,1)S(1)} %pad_maximum_fusion.1), channel_id=1, source_target_pairs={{0,16},{8,24},{16,0},{24,8},{32,48},{40,56},{48,32},{56,40},{64,80... | collective-permute-start | bytes 294920 | tf_op jit(solution)/shard_map/ppermute | solution.py:43
  20.6 7.4 %collective-permute-start.6 = (bf16[128,384]{1,0:T(8,128)(2,1)S(1)}, bf16[128,384]{1,0:T(8,128)(2,1)S(1)}, u32[]{:S(2)}, u32[]{:S(2)}) collective-permute-start(bf16[128,384]{1,0:T(8,128)(2,1)S(1)} %pad_maximum_fusion.1), channel_id=1, source_target_pairs={{0,128},{8,136},{16,144},{24,152},{32,160},{40,168},{48,176},{56,1... | collective-permute-start | bytes 294920 | tf_op jit(solution)/shard_map/ppermute | solution.py:43
  23.3 7.0 %collective-permute-start.7 = (bf16[128,384]{1,0:T(8,128)(2,1)S(1)}, bf16[128,384]{1,0:T(8,128)(2,1)S(1)}, u32[]{:S(2)}, u32[]{:S(2)}) collective-permute-start(bf16[128,384]{1,0:T(8,128)(2,1)S(1)} %pad_maximum_fusion.1), channel_id=1, source_target_pairs={{0,144},{8,152},{16,128},{24,136},{32,176},{40,184},{48,160},{56,1... | collective-permute-start | bytes 294920 | tf_op jit(solution)/shard_map/ppermute | solution.py:43
  24.6 9.5 %collective-permute-start.10 = (bf16[128,1024]{1,0:T(8,128)(2,1)S(1)}, bf16[128,1024]{1,0:T(8,128)(2,1)}, u32[]{:S(2)}, u32[]{:S(2)}) collective-permute-start(bf16[128,1024]{1,0:T(8,128)(2,1)S(1)} %slice.6), channel_id=1, source_target_pairs={{0,2},{1,3},{2,4},{3,5},{4,6},{5,7},{6,0},{7,1},{8,10},{9,11},{10,... | collective-permute-start | bytes 786440 | tf_op jit(solution)/shard_map/ppermute | solution.py:43
  25.0 10.0 %collective-permute-start.12 = (bf16[128,1024]{1,0:T(8,128)(2,1)S(1)}, bf16[128,1024]{1,0:T(8,128)(2,1)}, u32[]{:S(2)}, u32[]{:S(2)}) collective-permute-start(bf16[128,1024]{1,0:T(8,128)(2,1)S(1)} %slice.7), channel_id=1, source_target_pairs={{0,6},{1,7},{2,0},{3,1},{4,2},{5,3},{6,4},{7,5},{8,14},{9,15},{10,... | collective-permute-start | bytes 786440 | tf_op jit(solution)/shard_map/ppermute | solution.py:43
  30.4 18.0 %collective-permute-start.8 = (bf16[256,1024]{1,0:T(8,128)(2,1)S(1)}, bf16[256,1024]{1,0:T(8,128)(2,1)S(1)}, u32[]{:S(2)}, u32[]{:S(2)}) collective-permute-start(bf16[256,1024]{1,0:T(8,128)(2,1)S(1)} %collective-permute-done.peer), channel_id=1, source_target_pairs={{0,2},{1,3},{2,4},{3,5},{4,6},{5,7},{6,0},{7,1},{8,10},{9,11},{10,... | collective-permute-start | bytes 1572872 | tf_op jit(solution)/shard_map/ppermute | solution.py:43
  30.9 17.5 %collective-permute-start.9 = (bf16[256,1024]{1,0:T(8,128)(2,1)S(1)}, bf16[256,1024]{1,0:T(8,128)(2,1)S(1)}, u32[]{:S(2)}, u32[]{:S(2)}) collective-permute-start(bf16[256,1024]{1,0:T(8,128)(2,1)S(1)} %collective-permute-done.peer), channel_id=1, source_target_pairs={{0,6},{1,7},{2,0},{3,1},{4,2},{5,3},{6,4},{7,5},{8,14},{9,15},{10,... | collective-permute-start | bytes 1572872 | tf_op jit(solution)/shard_map/ppermute | solution.py:43
  33.7 2.6 %collective-permute-start.14 = (bf16[512,384]{1,0:T(8,128)(2,1)S(1)}, bf16[512,384]{1,0:T(8,128)(2,1)}, u32[]{:S(2)}, u32[]{:S(2)}) collective-permute-start(bf16[512,384]{1,0:T(8,128)(2,1)S(1)} %pad_maximum_fusion.mine), channel_id=1, source_target_pairs={{0,8},{8,0},{16,24},{24,16},{32,40},{40,32},{48,56},{56,48},{64,72... | collective-permute-start | bytes 1179656 | tf_op jit(solution)/shard_map/ppermute | solution.py:43
  34.1 9.7 %collective-permute-start.11 = (bf16[128,1024]{1,0:T(8,128)(2,1)}, bf16[128,1024]{1,0:T(8,128)(2,1)}, u32[]{:S(2)}, u32[]{:S(2)}) collective-permute-start(bf16[128,1024]{1,0:T(8,128)(2,1)} %collective-permute-done.10.up_far), channel_id=1, source_target_pairs={{0,1},{1,0},{2,3},{3,2},{4,5},{5,4},{6,7},{7,6},{8,9},{9,8},{10,11... | collective-permute-start | bytes 786440 | tf_op jit(solution)/shard_map/ppermute | solution.py:43
  35.0 13.4 %collective-permute-start.13 = (bf16[128,1024]{1,0:T(8,128)(2,1)}, bf16[128,1024]{1,0:T(8,128)(2,1)}, u32[]{:S(2)}, u32[]{:S(2)}) collective-permute-start(bf16[128,1024]{1,0:T(8,128)(2,1)} %collective-permute-done.12.down_far), channel_id=1, source_target_pairs={{0,1},{1,0},{2,3},{3,2},{4,5},{5,4},{6,7},{7,6},{8,9},{9,8},{10,11... | collective-permute-start | bytes 786440 | tf_op jit(solution)/shard_map/ppermute | solution.py:43
  48.4 22.6 %copy-start = (bf16[1024,1024]{1,0:T(8,128)(2,1)S(1)}, bf16[1024,1024]{1,0:T(8,128)(2,1)}, u32[]{:S(2)}) copy-start(bf16[1024,1024]{1,0:T(8,128)(2,1)} %w_out.1) | copy-start | bytes 6291460
  48.4 22.6 %copy-start.2 = (f32[1024]{0:T(1024)S(1)}, f32[1024]{0:T(1024)}, u32[]{:S(2)}) copy-start(f32[1024]{0:T(1024)} %param.11) | copy-start | bytes 12292
  48.4 22.6 %copy-start.3 = (f32[1024]{0:T(1024)S(1)}, f32[1024]{0:T(1024)}, u32[]{:S(2)}) copy-start(f32[1024]{0:T(1024)} %param.12) | copy-start | bytes 12292
  74.6 17.2 %copy-start.4 = (bf16[1024,1024]{1,0:T(8,128)(2,1)S(1)}, bf16[1024,1024]{1,0:T(8,128)(2,1)}, u32[]{:S(2)}) copy-start(bf16[1024,1024]{1,0:T(8,128)(2,1)} %queries.1) | copy-start | bytes 6291460
  98.2 2.0 %collective-permute-start.15 = (f32[512,256]{1,0:T(8,128)S(1)}, f32[512,256]{1,0:T(8,128)S(1)}, u32[]{:S(2)}, u32[]{:S(2)}) collective-permute-start(f32[512,256]{1,0:T(8,128)S(1)} %get-tuple-element.33), channel_id=1, source_target_pairs={{0,8},{8,0},{16,24},{24,16},{32,40},{40,32},{48,56},{56,48},{64,72... | collective-permute-start | bytes 1572872 | tf_op jit(solution)/shard_map/ppermute | solution.py:43

commit v9 on v8

--- a/solution.py
+++ b/solution.py
@@ -262,7 +262,7 @@
     peer, up, down, mine = lax.optimization_barrier((peer, up, down, mine))
     near = (up, down, from_below(up[:half]), from_above(down[half:]))
     mine = spread(mine, SPREAD[2:])
-    peer, mine = lax.optimization_barrier((peer, mine))
+
     far = (from_below(peer), from_above(peer), across(near[2]), across(near[3]))
     twin = permute(mine, "span", SPAN, lambda i: i ^ 1)
 

time: 131 us -> 133 us (1.015)
  waiting for transfers between devices: 13.2 us -> 15.6 us
    all_to_all x1, blocking collectives: 17.2 us -> 14.2 us  [per_device(): lax.all_to_all(cross_kv, 'seq', split_axis=0, concat_axis=0, tiled=True)]
    ppermute x16, waiting for transfers between devices: 13.2 us -> 15.6 us  [permute(): return lax.ppermute(x, axis, [(i, target(i)) for i in range(size)])]
    all_to_all x1, blocking collectives: 19.8 us -> 22.1 us  [per_device(): lax.all_to_all(merged.reshape(16, OWN, 2 * PAIR), 'span', split_axis=0, c...]
    all_to_all x1, blocking collectives: 12.2 us -> 13.6 us  [per_device(): attn = lax.all_to_all(attn, 'seq', split_axis=0, concat_axis=0, tiled=True)]
  transfers between devices with their start and end apart: 16 -> 16, of which waited for: 6 -> 5; matrix products, arithmetic and copies ran while one was open for 1% -> 1% of each run, Pallas kernels for 6% -> 6%
where the time goes in v9:
time: 133 us
  blocking collectives  58.5 us (44%)
  Pallas kernels  28.4 us (21%)
  starting transfers between devices  27.7 us (21%)
  waiting for transfers between devices  15.6 us (12%)
  local copies, waits for them, and re-layouts  1.59 us (1%)
    ppermute x16, starting transfers between devices, permute(): return lax.ppermute(x, axis, [(i, target(i)) for i in range(size)])  27.7 us
    all_to_all x1, blocking collectives, per_device(): lax.all_to_all(merged.reshape(16, OWN, 2 * PAIR), 'span', split_axis=0, c...  22.1 us
    ppermute x16, waiting for transfers between devices, permute(): return lax.ppermute(x, axis, [(i, target(i)) for i in range(size)])  15.6 us
    all_to_all x1, blocking collectives, per_device(): lax.all_to_all(cross_kv, 'seq', split_axis=0, concat_axis=0, tiled=True)  14.2 us
    all_to_all x1, blocking collectives, per_device(): attn = lax.all_to_all(attn, 'seq', split_axis=0, concat_axis=0, tiled=True)  13.6 us
    pallas_call x1, Pallas kernels, per_device(): pl.pallas_call(far_kernel, grid_spec=pltpu.PrefetchScalarGridSpec(num_sca...  10.4 us
    all_to_all x1, blocking collectives, per_device(): heads = lax.all_to_all(mine, 'seq', split_axis=0, concat_axis=0, tiled=True)  8.72 us
    pallas_call x1, Pallas kernels, per_device(): pl.pallas_call(near_kernel, grid=(NEAR // NEAR_BLOCK,), in_specs=[pl.Bloc...  7.43 us
  transfers between devices with their start and end apart: 16, of which 5 were waited for; matrix products, arithmetic and copies ran while one was open for 1% of the time, Pallas kernels for 6%

profile of v9, /device:TPU:32, one launch (start us, length us, event | category | flops | bytes accessed | tf_op | source)
XLA Modules:
  0.0 132.8 jit_solution(1127626694655972544)
XLA Ops:
  0.6 1.6 %collective-permute-start = (bf16[256,1024]{1,0:T(8,128)(2,1)}, bf16[256,1024]{1,0:T(8,128)(2,1)S(1)}, u32[]{:S(2)}, u32[]{:S(2)}) collective-permute-start(bf16[256,1024]{1,0:T(8,128)(2,1)} %tokens.1), channel_id=1, source_target_pairs={{0,1},{1,0},{2,3},{3,2},{4,5},{5,4},{6,7},{7,6},{8,9},{9,8},{10,11... | collective-permute-start | bytes 1572872 | tf_op jit(solution)/shard_map/ppermute | solution.py:43
  2.2 1.6 %collective-permute-start.1 = (bf16[256,1024]{1,0:T(8,128)(2,1)}, bf16[256,1024]{1,0:T(8,128)(2,1)S(1)}, u32[]{:S(2)}, u32[]{:S(2)}) collective-permute-start(bf16[256,1024]{1,0:T(8,128)(2,1)} %tokens.1), channel_id=1, source_target_pairs={{0,2},{1,3},{2,4},{3,5},{4,6},{5,7},{6,0},{7,1},{8,10},{9,11},{10,... | collective-permute-start | bytes 1572872 | tf_op jit(solution)/shard_map/ppermute | solution.py:43
  3.8 1.7 %collective-permute-start.2 = (bf16[256,1024]{1,0:T(8,128)(2,1)}, bf16[256,1024]{1,0:T(8,128)(2,1)S(1)}, u32[]{:S(2)}, u32[]{:S(2)}) collective-permute-start(bf16[256,1024]{1,0:T(8,128)(2,1)} %tokens.1), channel_id=1, source_target_pairs={{0,6},{1,7},{2,0},{3,1},{4,2},{5,3},{6,4},{7,5},{8,14},{9,15},{10,... | collective-permute-start | bytes 1572872 | tf_op jit(solution)/shard_map/ppermute | solution.py:43
  5.5 0.7 constant_dynamic-slice_fusion.2
  6.2 3.3 %collective-permute-start.3 = (bf16[32,384]{1,0:T(8,128)(2,1)S(1)}, bf16[32,384]{1,0:T(8,128)(2,1)S(1)}, u32[]{:S(2)}, u32[]{:S(2)}) collective-permute-start(bf16[32,384]{1,0:T(8,128)(2,1)S(1)} %pad_maximum_fusion.2), channel_id=1, source_target_pairs={{0,32},{8,40},{16,48},{24,56},{32,0},{40,8},{48,16},{56,24},{64,96... | collective-permute-start | bytes 73736 | tf_op jit(solution)/shard_map/ppermute | solution.py:43
  9.5 1.8 %collective-permute-done.3 = bf16[32,384]{1,0:T(8,128)(2,1)S(1)} collective-permute-done((bf16[32,384]{1,0:T(8,128)(2,1)S(1)}, bf16[32,384]{1,0:T(8,128)(2,1)S(1)}, u32[]{:S(2)}, u32[]{:S(2)}) %collective-permute-start.3) | collective-permute-done | bytes 24608 | tf_op jit(solution)/shard_map/ppermute | solution.py:43
  11.4 5.9 %collective-permute-start.4 = (bf16[64,384]{1,0:T(8,128)(2,1)S(1)}, bf16[64,384]{1,0:T(8,128)(2,1)S(1)}, u32[]{:S(2)}, u32[]{:S(2)}) collective-permute-start(bf16[64,384]{1,0:T(8,128)(2,1)S(1)} %pad_maximum_fusion.1), channel_id=1, source_target_pairs={{0,64},{8,72},{16,80},{24,88},{32,96},{40,104},{48,112},{56,120},{... | collective-permute-start | bytes 147464 | tf_op jit(solution)/shard_map/ppermute | solution.py:43
  17.3 2.2 %collective-permute-done.4 = bf16[64,384]{1,0:T(8,128)(2,1)S(1)} collective-permute-done((bf16[64,384]{1,0:T(8,128)(2,1)S(1)}, bf16[64,384]{1,0:T(8,128)(2,1)S(1)}, u32[]{:S(2)}, u32[]{:S(2)}) %collective-permute-start.4) | collective-permute-done | bytes 49184 | tf_op jit(solution)/shard_map/ppermute | solution.py:43
  19.5 0.0 collective-permute-done.peer
  19.5 0.0 collective-permute-done.2.down
  19.5 1.1 collective-permute-start.11
  20.6 2.7 %collective-permute-start.12 = (bf16[128,384]{1,0:T(8,128)(2,1)S(1)}, bf16[128,384]{1,0:T(8,128)(2,1)S(1)}, u32[]{:S(2)}, u32[]{:S(2)}) collective-permute-start(bf16[128,384]{1,0:T(8,128)(2,1)S(1)} %pad_maximum_fusion), channel_id=1, source_target_pairs={{0,128},{8,136},{16,144},{24,152},{32,160},{40,168},{48,176},{56,1... | collective-permute-start | bytes 294920 | tf_op jit(solution)/shard_map/ppermute | solution.py:43
  23.3 1.3 collective-permute-start.13
  24.6 0.3 collective-permute-start.5
  24.9 3.0 %collective-permute-start.6 = (bf16[256,1024]{1,0:T(8,128)(2,1)S(1)}, bf16[256,1024]{1,0:T(8,128)(2,1)S(1)}, u32[]{:S(2)}, u32[]{:S(2)}) collective-permute-start(bf16[256,1024]{1,0:T(8,128)(2,1)S(1)} %collective-permute-done.peer), channel_id=1, source_target_pairs={{0,6},{1,7},{2,0},{3,1},{4,2},{5,3},{6,4},{7,5},{8,14},{9,15},{10,... | collective-permute-start | bytes 1572872 | tf_op jit(solution)/shard_map/ppermute | solution.py:43
  27.9 0.0 collective-permute-done.11
  27.9 0.1 collective-permute-start.7
  28.0 0.0 collective-permute-done.12
  28.0 3.3 %collective-permute-start.9 = (bf16[128,1024]{1,0:T(8,128)(2,1)S(1)}, bf16[128,1024]{1,0:T(8,128)(2,1)}, u32[]{:S(2)}, u32[]{:S(2)}) collective-permute-start(bf16[128,1024]{1,0:T(8,128)(2,1)S(1)} %slice.7), channel_id=1, source_target_pairs={{0,6},{1,7},{2,0},{3,1},{4,2},{5,3},{6,4},{7,5},{8,14},{9,15},{10,... | collective-permute-start | bytes 786440 | tf_op jit(solution)/shard_map/ppermute | solution.py:43
  31.4 0.0 collective-permute-done.13
  31.4 0.1 collective-permute-start.14
  31.5 9.4 %collective-permute-done.9.down_far = bf16[128,1024]{1,0:T(8,128)(2,1)} collective-permute-done((bf16[128,1024]{1,0:T(8,128)(2,1)S(1)}, bf16[128,1024]{1,0:T(8,128)(2,1)}, u32[]{:S(2)}, u32[]{:S(2)}) %collective-permute-start.9) | collective-permute-done | bytes 262176 | tf_op jit(solution)/shard_map/ppermute | solution.py:43
  40.9 0.5 collective-permute-start.10
  41.4 0.3 collective-permute-done.7.up_far
  41.7 1.2 collective-permute-start.8
  42.9 0.1 stack.44.table
  43.0 0.1 pad_add_fusion.place
  43.1 0.0 collective-permute-done.14.twin
  43.1 7.4 %shard_map.86 = (bf16[1280,128]{1,0:T(8,128)(2,1)S(1)}, bf16[128,1280]{1,0:T(8,128)(2,1)S(1)}, bf16[1280,256]{1,0:T(8,128)(2,1)S(1)}, bf16[1024,384]{1,0:T(8,128...) custom-call(s32[2]{0:T(128)S(1)} %pad_add_fusion.place, bf16[256,1024]{1,0:T(8,128)(2,1)S(1)} %copy-done.1, ...), custom_call_target="tpu_custom_call" | custom-call | flops 1006632960 | bytes 4194304 | tf_op jit(solution)/shard_map/pallas_call | solution.py:283
  50.5 0.0 collective-permute-done.10.refs_3_
  50.6 0.0 collective-permute-done.8.refs_2_
  50.6 0.0 collective-permute-done.6.refs_1_
  50.6 0.0 copy-start
  50.6 0.0 copy-start.2
  50.6 0.0 copy-start.3
  50.6 10.4 %shard_map.87 = bf16[8,256,128]{2,1,0:T(8,128)(2,1)S(1)} custom-call(s32[8]{0:T(128)S(1)} %stack.44.table, bf16[256,1024]{1,0:T(8,128)(2,1)S(1)} %collective-permute-done.5.refs_0_, bf16[256,1024]{1,0:T(8,128)(2,1)S(1)} %collective-permute-done.6.refs_1_, bf16[128,1024]{1,0:T(8,128)(2,1)} %collective-permute-done.8.refs_2_, ...), custom_call_target="tpu_custom_call" | custom-call | flops 6442450944 | bytes 4194304 | tf_op jit(solution)/shard_map/pallas_call | solution.py:302
  61.0 13.6 %all_to_all.20.attn = bf16[8,256,128]{2,1,0:T(8,128)(2,1)S(1)} all-to-all(bf16[8,256,128]{2,1,0:T(8,128)(2,1)S(1)} %shard_map.87), channel_id=1, replica_groups=mesh['span'=32,'seq'=8] {'seq'}, dimensions={0} | all-to-all | bytes 1048576 | tf_op jit(solution)/shard_map/all_to_all | solution.py:328
  74.6 3.6 %shard_map.88 = (bf16[256,1024]{1,0:T(8,128)(2,1)}, bf16[8,256,256]{2,1,0:T(8,128)(2,1)S(1)}) custom-call(bf16[8,256,128]{2,1,0:T(8,128)(2,1)S(1)} %all_to_all.20.attn, bf16[256,1024]{1,0:T(8,128)(2,1)S(1)} %copy-done.1, bf16[1024,1024]{1,0:T(8,128)(2,1)S(1)} %copy-done, f32[1,1024]{1,0:T(1,128)S(1)} %bitcast.22, f32[1,1024]{1,0:T(1,128)S(1)} %bitcast.23, ...), custom_call_target="tpu_custom_call" | custom-call | flops 1610612736 | bytes 8388608 | tf_op jit(solution)/shard_map/pallas_call | solution.py:330
  78.1 0.0 copy-start.4
  78.1 14.2 %all_to_all.21 = bf16[8,256,256]{2,1,0:T(8,128)(2,1)S(1)} all-to-all(bf16[8,256,256]{2,1,0:T(8,128)(2,1)S(1)} %get-tuple-element.27), channel_id=1, replica_groups=mesh['span'=32,'seq'=8] {'seq'}, dimensions={0} | all-to-all | bytes 2097152 | tf_op jit(solution)/shard_map/all_to_all | solution.py:344
  92.3 6.4 %shard_map.89 = (f32[512,256]{1,0:T(8,128)S(1)}, f32[512,256]{1,0:T(8,128)S(1)}) custom-call(s32[2]{0:T(128)S(1)} %pad_add_fusion.place, bf16[1024,1024]{1,0:T(8,128)(2,1)S(1)} %copy-done.4, bf16[2048,256]{1,0:T(8,128)(2,1)S(1)} %bitcast.21), custom_call_target="tpu_custom_call" | custom-call | flops 4294967296 | bytes 2097152 | tf_op jit(solution)/shard_map/pallas_call | solution.py:348
  98.7 0.1 collective-permute-start.15
  98.8 1.9 %collective-permute-done.15.received = f32[512,256]{1,0:T(8,128)S(1)} collective-permute-done((f32[512,256]{1,0:T(8,128)S(1)}, f32[512,256]{1,0:T(8,128)S(1)}, u32[]{:S(2)}, u32[]{:S(2)}) %collective-permute-start.15) | collective-permute-done | bytes 524320 | tf_op jit(solution)/shard_map/ppermute | solution.py:43
  100.7 0.2 shard_map.90
  100.9 22.1 %all_to_all.22.parts = bf16[16,32,256]{2,1,0:T(8,128)(2,1)S(1)} all-to-all(bf16[16,32,256]{2,1,0:T(8,128)(2,1)S(1)} %bitcast.20), channel_id=1, replica_groups={{0,16,32,48,64,80,96,112,128,144,160,176,192,208,224,240},{8,24,40,56,7..., dimensions={0} | all-to-all | bytes 524288 | tf_op jit(solution)/shard_map/all_to_all | solution.py:382
  123.0 0.4 shard_map.91
  123.4 8.7 %all_to_all.23 = bf16[8,32,128]{2,1,0:T(8,128)(2,1)S(1)} all-to-all(bf16[8,32,128]{2,1,0:T(8,128)(2,1)S(1)} %shard_map.91), channel_id=1, replica_groups=mesh['span'=32,'seq'=8] {'seq'}, dimensions={0} | all-to-all | bytes 131072 | tf_op jit(solution)/shard_map/all_to_all | solution.py:395
  132.1 0.6 copy_bitcast_fusion
  (17 shorter events, 0.1 us)
Async XLA Ops:
  0.6 42.5 %copy-start.1 = (bf16[256,1024]{1,0:T(8,128)(2,1)S(1)}, bf16[256,1024]{1,0:T(8,128)(2,1)}, u32[]{:S(2)}) copy-start(bf16[256,1024]{1,0:T(8,128)(2,1)} %tokens.1) | copy-start | bytes 1572868
  0.6 18.8 %collective-permute-start = (bf16[256,1024]{1,0:T(8,128)(2,1)}, bf16[256,1024]{1,0:T(8,128)(2,1)S(1)}, u32[]{:S(2)}, u32[]{:S(2)}) collective-permute-start(bf16[256,1024]{1,0:T(8,128)(2,1)} %tokens.1), channel_id=1, source_target_pairs={{0,1},{1,0},{2,3},{3,2},{4,5},{5,4},{6,7},{7,6},{8,9},{9,8},{10,11... | collective-permute-start | bytes 1572872 | tf_op jit(solution)/shard_map/ppermute | solution.py:43
  2.2 17.3 %collective-permute-start.1 = (bf16[256,1024]{1,0:T(8,128)(2,1)}, bf16[256,1024]{1,0:T(8,128)(2,1)S(1)}, u32[]{:S(2)}, u32[]{:S(2)}) collective-permute-start(bf16[256,1024]{1,0:T(8,128)(2,1)} %tokens.1), channel_id=1, source_target_pairs={{0,2},{1,3},{2,4},{3,5},{4,6},{5,7},{6,0},{7,1},{8,10},{9,11},{10,... | collective-permute-start | bytes 1572872 | tf_op jit(solution)/shard_map/ppermute | solution.py:43
  3.8 15.7 %collective-permute-start.2 = (bf16[256,1024]{1,0:T(8,128)(2,1)}, bf16[256,1024]{1,0:T(8,128)(2,1)S(1)}, u32[]{:S(2)}, u32[]{:S(2)}) collective-permute-start(bf16[256,1024]{1,0:T(8,128)(2,1)} %tokens.1), channel_id=1, source_target_pairs={{0,6},{1,7},{2,0},{3,1},{4,2},{5,3},{6,4},{7,5},{8,14},{9,15},{10,... | collective-permute-start | bytes 1572872 | tf_op jit(solution)/shard_map/ppermute | solution.py:43
  6.2 5.2 %collective-permute-start.3 = (bf16[32,384]{1,0:T(8,128)(2,1)S(1)}, bf16[32,384]{1,0:T(8,128)(2,1)S(1)}, u32[]{:S(2)}, u32[]{:S(2)}) collective-permute-start(bf16[32,384]{1,0:T(8,128)(2,1)S(1)} %pad_maximum_fusion.2), channel_id=1, source_target_pairs={{0,32},{8,40},{16,48},{24,56},{32,0},{40,8},{48,16},{56,24},{64,96... | collective-permute-start | bytes 73736 | tf_op jit(solution)/shard_map/ppermute | solution.py:43
  11.4 8.1 %collective-permute-start.4 = (bf16[64,384]{1,0:T(8,128)(2,1)S(1)}, bf16[64,384]{1,0:T(8,128)(2,1)S(1)}, u32[]{:S(2)}, u32[]{:S(2)}) collective-permute-start(bf16[64,384]{1,0:T(8,128)(2,1)S(1)} %pad_maximum_fusion.1), channel_id=1, source_target_pairs={{0,64},{8,72},{16,80},{24,88},{32,96},{40,104},{48,112},{56,120},{... | collective-permute-start | bytes 147464 | tf_op jit(solution)/shard_map/ppermute | solution.py:43
  19.5 8.4 %collective-permute-start.11 = (bf16[128,384]{1,0:T(8,128)(2,1)S(1)}, bf16[128,384]{1,0:T(8,128)(2,1)S(1)}, u32[]{:S(2)}, u32[]{:S(2)}) collective-permute-start(bf16[128,384]{1,0:T(8,128)(2,1)S(1)} %pad_maximum_fusion), channel_id=1, source_target_pairs={{0,16},{8,24},{16,0},{24,8},{32,48},{40,56},{48,32},{56,40},{64,80... | collective-permute-start | bytes 294920 | tf_op jit(solution)/shard_map/ppermute | solution.py:43
  20.6 7.4 %collective-permute-start.12 = (bf16[128,384]{1,0:T(8,128)(2,1)S(1)}, bf16[128,384]{1,0:T(8,128)(2,1)S(1)}, u32[]{:S(2)}, u32[]{:S(2)}) collective-permute-start(bf16[128,384]{1,0:T(8,128)(2,1)S(1)} %pad_maximum_fusion), channel_id=1, source_target_pairs={{0,128},{8,136},{16,144},{24,152},{32,160},{40,168},{48,176},{56,1... | collective-permute-start | bytes 294920 | tf_op jit(solution)/shard_map/ppermute | solution.py:43
  23.3 8.0 %collective-permute-start.13 = (bf16[128,384]{1,0:T(8,128)(2,1)S(1)}, bf16[128,384]{1,0:T(8,128)(2,1)S(1)}, u32[]{:S(2)}, u32[]{:S(2)}) collective-permute-start(bf16[128,384]{1,0:T(8,128)(2,1)S(1)} %pad_maximum_fusion), channel_id=1, source_target_pairs={{0,144},{8,152},{16,128},{24,136},{32,176},{40,184},{48,160},{56,1... | collective-permute-start | bytes 294920 | tf_op jit(solution)/shard_map/ppermute | solution.py:43
  24.6 26.0 %collective-permute-start.5 = (bf16[256,1024]{1,0:T(8,128)(2,1)S(1)}, bf16[256,1024]{1,0:T(8,128)(2,1)S(1)}, u32[]{:S(2)}, u32[]{:S(2)}) collective-permute-start(bf16[256,1024]{1,0:T(8,128)(2,1)S(1)} %collective-permute-done.peer), channel_id=1, source_target_pairs={{0,2},{1,3},{2,4},{3,5},{4,6},{5,7},{6,0},{7,1},{8,10},{9,11},{10,... | collective-permute-start | bytes 1572872 | tf_op jit(solution)/shard_map/ppermute | solution.py:43
  24.9 25.7 %collective-permute-start.6 = (bf16[256,1024]{1,0:T(8,128)(2,1)S(1)}, bf16[256,1024]{1,0:T(8,128)(2,1)S(1)}, u32[]{:S(2)}, u32[]{:S(2)}) collective-permute-start(bf16[256,1024]{1,0:T(8,128)(2,1)S(1)} %collective-permute-done.peer), channel_id=1, source_target_pairs={{0,6},{1,7},{2,0},{3,1},{4,2},{5,3},{6,4},{7,5},{8,14},{9,15},{10,... | collective-permute-start | bytes 1572872 | tf_op jit(solution)/shard_map/ppermute | solution.py:43
  27.9 13.8 %collective-permute-start.7 = (bf16[128,1024]{1,0:T(8,128)(2,1)S(1)}, bf16[128,1024]{1,0:T(8,128)(2,1)}, u32[]{:S(2)}, u32[]{:S(2)}) collective-permute-start(bf16[128,1024]{1,0:T(8,128)(2,1)S(1)} %slice.6), channel_id=1, source_target_pairs={{0,2},{1,3},{2,4},{3,5},{4,6},{5,7},{6,0},{7,1},{8,10},{9,11},{10,... | collective-permute-start | bytes 786440 | tf_op jit(solution)/shard_map/ppermute | solution.py:43
  28.0 12.9 %collective-permute-start.9 = (bf16[128,1024]{1,0:T(8,128)(2,1)S(1)}, bf16[128,1024]{1,0:T(8,128)(2,1)}, u32[]{:S(2)}, u32[]{:S(2)}) collective-permute-start(bf16[128,1024]{1,0:T(8,128)(2,1)S(1)} %slice.7), channel_id=1, source_target_pairs={{0,6},{1,7},{2,0},{3,1},{4,2},{5,3},{6,4},{7,5},{8,14},{9,15},{10,... | collective-permute-start | bytes 786440 | tf_op jit(solution)/shard_map/ppermute | solution.py:43
  31.4 11.7 %collective-permute-start.14 = (bf16[512,384]{1,0:T(8,128)(2,1)S(1)}, bf16[512,384]{1,0:T(8,128)(2,1)}, u32[]{:S(2)}, u32[]{:S(2)}) collective-permute-start(bf16[512,384]{1,0:T(8,128)(2,1)S(1)} %constant_dynamic-update-slice_fusion.mine), channel_id=1, source_target_pairs={{0,8},{8,0},{16,24},{24,16},{32,40},{40,32},{48,56},{56,48},{64,72... | collective-permute-start | bytes 1179656 | tf_op jit(solution)/shard_map/ppermute | solution.py:43
  40.9 9.6 %collective-permute-start.10 = (bf16[128,1024]{1,0:T(8,128)(2,1)}, bf16[128,1024]{1,0:T(8,128)(2,1)}, u32[]{:S(2)}, u32[]{:S(2)}) collective-permute-start(bf16[128,1024]{1,0:T(8,128)(2,1)} %collective-permute-done.9.down_far), channel_id=1, source_target_pairs={{0,1},{1,0},{2,3},{3,2},{4,5},{5,4},{6,7},{7,6},{8,9},{9,8},{10,11... | collective-permute-start | bytes 786440 | tf_op jit(solution)/shard_map/ppermute | solution.py:43
  41.7 8.8 %collective-permute-start.8 = (bf16[128,1024]{1,0:T(8,128)(2,1)}, bf16[128,1024]{1,0:T(8,128)(2,1)}, u32[]{:S(2)}, u32[]{:S(2)}) collective-permute-start(bf16[128,1024]{1,0:T(8,128)(2,1)} %collective-permute-done.7.up_far), channel_id=1, source_target_pairs={{0,1},{1,0},{2,3},{3,2},{4,5},{5,4},{6,7},{7,6},{8,9},{9,8},{10,11... | collective-permute-start | bytes 786440 | tf_op jit(solution)/shard_map/ppermute | solution.py:43
  50.6 24.0 %copy-start = (bf16[1024,1024]{1,0:T(8,128)(2,1)S(1)}, bf16[1024,1024]{1,0:T(8,128)(2,1)}, u32[]{:S(2)}) copy-start(bf16[1024,1024]{1,0:T(8,128)(2,1)} %w_out.1) | copy-start | bytes 6291460
  50.6 24.0 %copy-start.2 = (f32[1024]{0:T(1024)S(1)}, f32[1024]{0:T(1024)}, u32[]{:S(2)}) copy-start(f32[1024]{0:T(1024)} %param.11) | copy-start | bytes 12292
  50.6 23.9 %copy-start.3 = (f32[1024]{0:T(1024)S(1)}, f32[1024]{0:T(1024)}, u32[]{:S(2)}) copy-start(f32[1024]{0:T(1024)} %param.12) | copy-start | bytes 12292
  78.1 14.2 %copy-start.4 = (bf16[1024,1024]{1,0:T(8,128)(2,1)S(1)}, bf16[1024,1024]{1,0:T(8,128)(2,1)}, u32[]{:S(2)}) copy-start(bf16[1024,1024]{1,0:T(8,128)(2,1)} %queries.1) | copy-start | bytes 6291460
  98.7 2.0 %collective-permute-start.15 = (f32[512,256]{1,0:T(8,128)S(1)}, f32[512,256]{1,0:T(8,128)S(1)}, u32[]{:S(2)}, u32[]{:S(2)}) collective-permute-start(f32[512,256]{1,0:T(8,128)S(1)} %get-tuple-element.29), channel_id=1, source_target_pairs={{0,8},{8,0},{16,24},{24,16},{32,40},{40,32},{48,56},{56,48},{64,72... | collective-permute-start | bytes 1572872 | tf_op jit(solution)/shard_map/ppermute | solution.py:43

commit v10 on v8

--- a/solution.py
+++ b/solution.py
@@ -19,7 +19,7 @@
 NQ = 1024
 STAT_LANES = 16
 BLOCK = 512
-SPREAD = (4, 8, 2, 16)
+SPREAD = (8, 4, 2, 16)
 NEAR, FAR = 5 * ROWS, 3 * ROWS
 NEAR_BLOCK, FAR_BLOCK = 640, 384
 FAR_PIECES = 4

time: 131 us -> 130 us (level)
  transfers between devices with their start and end apart: 16 -> 16, of which waited for: 6 -> 5; matrix products, arithmetic and copies ran while one was open for 1% -> 1% of each run, Pallas kernels for 6% -> 6%
where the time goes in v10:
time: 130 us
  blocking collectives  57.7 us (44%)
  Pallas kernels  28.4 us (22%)
  starting transfers between devices  28 us (22%)
  waiting for transfers between devices  13.2 us (10%)
  local copies, waits for them, and re-layouts  1.52 us (1%)
    ppermute x16, starting transfers between devices, permute(): return lax.ppermute(x, axis, [(i, target(i)) for i in range(size)])  28 us
    all_to_all x1, blocking collectives, per_device(): lax.all_to_all(merged.reshape(16, OWN, 2 * PAIR), 'span', split_axis=0, c...  18.8 us
    all_to_all x1, blocking collectives, per_device(): lax.all_to_all(cross_kv, 'seq', split_axis=0, concat_axis=0, tiled=True)  17.4 us
    ppermute x16, waiting for transfers between devices, permute(): return lax.ppermute(x, axis, [(i, target(i)) for i in range(size)])  13.2 us
    all_to_all x1, blocking collectives, per_device(): attn = lax.all_to_all(attn, 'seq', split_axis=0, concat_axis=0, tiled=True)  12.7 us
    pallas_call x1, Pallas kernels, per_device(): pl.pallas_call(far_kernel, grid_spec=pltpu.PrefetchScalarGridSpec(num_sca...  10.4 us
    all_to_all x1, blocking collectives, per_device(): heads = lax.all_to_all(mine, 'seq', split_axis=0, concat_axis=0, tiled=True)  8.78 us
    pallas_call x1, Pallas kernels, per_device(): pl.pallas_call(near_kernel, grid=(NEAR // NEAR_BLOCK,), in_specs=[pl.Bloc...  7.43 us
  transfers between devices with their start and end apart: 16, of which 5 were waited for; matrix products, arithmetic and copies ran while one was open for 1% of the time, Pallas kernels for 6%

profile of v10, /device:TPU:32, one launch (start us, length us, event | category | flops | bytes accessed | tf_op | source)
XLA Modules:
  0.0 129.7 jit_solution(15344287208372505840)
XLA Ops:
  0.6 1.6 %collective-permute-start = (bf16[256,1024]{1,0:T(8,128)(2,1)}, bf16[256,1024]{1,0:T(8,128)(2,1)S(1)}, u32[]{:S(2)}, u32[]{:S(2)}) collective-permute-start(bf16[256,1024]{1,0:T(8,128)(2,1)} %tokens.1), channel_id=1, source_target_pairs={{0,1},{1,0},{2,3},{3,2},{4,5},{5,4},{6,7},{7,6},{8,9},{9,8},{10,11... | collective-permute-start | bytes 1572872 | tf_op jit(solution)/shard_map/ppermute | solution.py:43
  2.2 1.6 %collective-permute-start.1 = (bf16[256,1024]{1,0:T(8,128)(2,1)}, bf16[256,1024]{1,0:T(8,128)(2,1)S(1)}, u32[]{:S(2)}, u32[]{:S(2)}) collective-permute-start(bf16[256,1024]{1,0:T(8,128)(2,1)} %tokens.1), channel_id=1, source_target_pairs={{0,2},{1,3},{2,4},{3,5},{4,6},{5,7},{6,0},{7,1},{8,10},{9,11},{10,... | collective-permute-start | bytes 1572872 | tf_op jit(solution)/shard_map/ppermute | solution.py:43
  3.8 1.7 %collective-permute-start.2 = (bf16[256,1024]{1,0:T(8,128)(2,1)}, bf16[256,1024]{1,0:T(8,128)(2,1)S(1)}, u32[]{:S(2)}, u32[]{:S(2)}) collective-permute-start(bf16[256,1024]{1,0:T(8,128)(2,1)} %tokens.1), channel_id=1, source_target_pairs={{0,6},{1,7},{2,0},{3,1},{4,2},{5,3},{6,4},{7,5},{8,14},{9,15},{10,... | collective-permute-start | bytes 1572872 | tf_op jit(solution)/shard_map/ppermute | solution.py:43
  5.5 0.7 constant_dynamic-slice_fusion.2
  6.2 6.4 %collective-permute-start.3 = (bf16[32,384]{1,0:T(8,128)(2,1)S(1)}, bf16[32,384]{1,0:T(8,128)(2,1)S(1)}, u32[]{:S(2)}, u32[]{:S(2)}) collective-permute-start(bf16[32,384]{1,0:T(8,128)(2,1)S(1)} %pad_maximum_fusion.3), channel_id=1, source_target_pairs={{0,64},{8,72},{16,80},{24,88},{32,96},{40,104},{48,112},{56,120},{... | collective-permute-start | bytes 73736 | tf_op jit(solution)/shard_map/ppermute | solution.py:43
  12.6 1.8 %collective-permute-done.3 = bf16[32,384]{1,0:T(8,128)(2,1)S(1)} collective-permute-done((bf16[32,384]{1,0:T(8,128)(2,1)S(1)}, bf16[32,384]{1,0:T(8,128)(2,1)S(1)}, u32[]{:S(2)}, u32[]{:S(2)}) %collective-permute-start.3) | collective-permute-done | bytes 24608 | tf_op jit(solution)/shard_map/ppermute | solution.py:43
  14.4 2.9 %collective-permute-start.4 = (bf16[64,384]{1,0:T(8,128)(2,1)S(1)}, bf16[64,384]{1,0:T(8,128)(2,1)S(1)}, u32[]{:S(2)}, u32[]{:S(2)}) collective-permute-start(bf16[64,384]{1,0:T(8,128)(2,1)S(1)} %pad_maximum_fusion.2), channel_id=1, source_target_pairs={{0,32},{8,40},{16,48},{24,56},{32,0},{40,8},{48,16},{56,24},{64,96... | collective-permute-start | bytes 147464 | tf_op jit(solution)/shard_map/ppermute | solution.py:43
  17.3 2.2 %collective-permute-done.4 = bf16[64,384]{1,0:T(8,128)(2,1)S(1)} collective-permute-done((bf16[64,384]{1,0:T(8,128)(2,1)S(1)}, bf16[64,384]{1,0:T(8,128)(2,1)S(1)}, u32[]{:S(2)}, u32[]{:S(2)}) %collective-permute-start.4) | collective-permute-done | bytes 49184 | tf_op jit(solution)/shard_map/ppermute | solution.py:43
  19.5 0.0 collective-permute-done.peer
  19.5 0.0 collective-permute-done.1.up
  19.5 0.0 collective-permute-done.2.down
  19.5 1.0 collective-permute-start.5
  20.5 2.7 %collective-permute-start.6 = (bf16[128,384]{1,0:T(8,128)(2,1)S(1)}, bf16[128,384]{1,0:T(8,128)(2,1)S(1)}, u32[]{:S(2)}, u32[]{:S(2)}) collective-permute-start(bf16[128,384]{1,0:T(8,128)(2,1)S(1)} %pad_maximum_fusion.1), channel_id=1, source_target_pairs={{0,128},{8,136},{16,144},{24,152},{32,160},{40,168},{48,176},{56,1... | collective-permute-start | bytes 294920 | tf_op jit(solution)/shard_map/ppermute | solution.py:43
  23.3 1.3 %collective-permute-start.7 = (bf16[128,384]{1,0:T(8,128)(2,1)S(1)}, bf16[128,384]{1,0:T(8,128)(2,1)S(1)}, u32[]{:S(2)}, u32[]{:S(2)}) collective-permute-start(bf16[128,384]{1,0:T(8,128)(2,1)S(1)} %pad_maximum_fusion.1), channel_id=1, source_target_pairs={{0,144},{8,152},{16,128},{24,136},{32,176},{40,184},{48,160},{56,1... | collective-permute-start | bytes 294920 | tf_op jit(solution)/shard_map/ppermute | solution.py:43
  24.6 0.4 collective-permute-start.10
  25.0 3.0 %collective-permute-start.12 = (bf16[128,1024]{1,0:T(8,128)(2,1)S(1)}, bf16[128,1024]{1,0:T(8,128)(2,1)}, u32[]{:S(2)}, u32[]{:S(2)}) collective-permute-start(bf16[128,1024]{1,0:T(8,128)(2,1)S(1)} %slice.7), channel_id=1, source_target_pairs={{0,6},{1,7},{2,0},{3,1},{4,2},{5,3},{6,4},{7,5},{8,14},{9,15},{10,... | collective-permute-start | bytes 786440 | tf_op jit(solution)/shard_map/ppermute | solution.py:43
  28.0 0.0 collective-permute-done.5
  28.0 2.3 %collective-permute-done.7 = bf16[128,384]{1,0:T(8,128)(2,1)S(1)} collective-permute-done((bf16[128,384]{1,0:T(8,128)(2,1)S(1)}, bf16[128,384]{1,0:T(8,128)(2,1)S(1)}, u32[]{:S(2)}, u32[]{:S(2)}) %collective-permute-start.7) | collective-permute-done | bytes 98336 | tf_op jit(solution)/shard_map/ppermute | solution.py:43
  30.3 0.4 collective-permute-start.8
  30.8 2.9 %collective-permute-start.9 = (bf16[256,1024]{1,0:T(8,128)(2,1)S(1)}, bf16[256,1024]{1,0:T(8,128)(2,1)S(1)}, u32[]{:S(2)}, u32[]{:S(2)}) collective-permute-start(bf16[256,1024]{1,0:T(8,128)(2,1)S(1)} %collective-permute-done.peer), channel_id=1, source_target_pairs={{0,6},{1,7},{2,0},{3,1},{4,2},{5,3},{6,4},{7,5},{8,14},{9,15},{10,... | collective-permute-start | bytes 1572872 | tf_op jit(solution)/shard_map/ppermute | solution.py:43
  33.6 0.0 collective-permute-start.14
  33.6 0.0 collective-permute-done.10.up_far
  33.6 0.6 collective-permute-start.11
  34.2 0.0 collective-permute-done.12.down_far
  34.2 1.5 %collective-permute-start.13 = (bf16[128,1024]{1,0:T(8,128)(2,1)}, bf16[128,1024]{1,0:T(8,128)(2,1)}, u32[]{:S(2)}, u32[]{:S(2)}) collective-permute-start(bf16[128,1024]{1,0:T(8,128)(2,1)} %collective-permute-done.12.down_far), channel_id=1, source_target_pairs={{0,1},{1,0},{2,3},{3,2},{4,5},{5,4},{6,7},{7,6},{8,9},{9,8},{10,11... | collective-permute-start | bytes 786440 | tf_op jit(solution)/shard_map/ppermute | solution.py:43
  35.7 0.1 stack.44.table
  35.8 0.1 pad_add_fusion.place
  35.8 0.0 collective-permute-done.14.twin
  35.8 7.4 %shard_map.86 = (bf16[1280,128]{1,0:T(8,128)(2,1)S(1)}, bf16[128,1280]{1,0:T(8,128)(2,1)S(1)}, bf16[1280,256]{1,0:T(8,128)(2,1)S(1)}, bf16[1024,384]{1,0:T(8,128...) custom-call(s32[2]{0:T(128)S(1)} %pad_add_fusion.place, bf16[256,1024]{1,0:T(8,128)(2,1)S(1)} %copy-done.1, ...), custom_call_target="tpu_custom_call" | custom-call | flops 1006632960 | bytes 4194304 | tf_op jit(solution)/shard_map/pallas_call | solution.py:283
  43.3 0.0 collective-permute-done.11.refs_2_
  43.3 5.0 %collective-permute-done.13.refs_3_ = bf16[128,1024]{1,0:T(8,128)(2,1)} collective-permute-done((bf16[128,1024]{1,0:T(8,128)(2,1)}, bf16[128,1024]{1,0:T(8,128)(2,1)}, u32[]{:S(2)}, u32[]{:S(2)}) %collective-permute-start.13) | collective-permute-done | bytes 262176 | tf_op jit(solution)/shard_map/ppermute | solution.py:43
  48.3 0.0 collective-permute-done.8.refs_0_
  48.3 0.0 collective-permute-done.9.refs_1_
  48.3 0.0 copy-start.2
  48.3 0.0 copy-start.3
  48.3 10.4 %shard_map.87 = bf16[8,256,128]{2,1,0:T(8,128)(2,1)S(1)} custom-call(s32[8]{0:T(128)S(1)} %stack.44.table, bf16[256,1024]{1,0:T(8,128)(2,1)S(1)} %collective-permute-done.8.refs_0_, bf16[256,1024]{1,0:T(8,128)(2,1)S(1)} %collective-permute-done.9.refs_1_, bf16[128,1024]{1,0:T(8,128)(2,1)} %collective-permute-done.11.refs_2_, ...), custom_call_target="tpu_custom_call" | custom-call | flops 6442450944 | bytes 4194304 | tf_op jit(solution)/shard_map/pallas_call | solution.py:302
  58.7 12.7 %all_to_all.20.attn = bf16[8,256,128]{2,1,0:T(8,128)(2,1)S(1)} all-to-all(bf16[8,256,128]{2,1,0:T(8,128)(2,1)S(1)} %shard_map.87), channel_id=1, replica_groups=mesh['span'=32,'seq'=8] {'seq'}, dimensions={0} | all-to-all | bytes 1048576 | tf_op jit(solution)/shard_map/all_to_all | solution.py:328
  71.4 3.6 %shard_map.88 = (bf16[256,1024]{1,0:T(8,128)(2,1)}, bf16[8,256,256]{2,1,0:T(8,128)(2,1)S(1)}) custom-call(bf16[8,256,128]{2,1,0:T(8,128)(2,1)S(1)} %all_to_all.20.attn, bf16[256,1024]{1,0:T(8,128)(2,1)S(1)} %copy-done.1, bf16[1024,1024]{1,0:T(8,128)(2,1)S(1)} %copy-done, f32[1,1024]{1,0:T(1,128)S(1)} %bitcast.22, f32[1,1024]{1,0:T(1,128)S(1)} %bitcast.23, ...), custom_call_target="tpu_custom_call" | custom-call | flops 1610612736 | bytes 8388608 | tf_op jit(solution)/shard_map/pallas_call | solution.py:330
  75.0 0.0 copy-start.4
  75.0 17.4 %all_to_all.21 = bf16[8,256,256]{2,1,0:T(8,128)(2,1)S(1)} all-to-all(bf16[8,256,256]{2,1,0:T(8,128)(2,1)S(1)} %get-tuple-element.31), channel_id=1, replica_groups=mesh['span'=32,'seq'=8] {'seq'}, dimensions={0} | all-to-all | bytes 2097152 | tf_op jit(solution)/shard_map/all_to_all | solution.py:344
  92.4 6.4 %shard_map.89 = (f32[512,256]{1,0:T(8,128)S(1)}, f32[512,256]{1,0:T(8,128)S(1)}) custom-call(s32[2]{0:T(128)S(1)} %pad_add_fusion.place, bf16[1024,1024]{1,0:T(8,128)(2,1)S(1)} %copy-done.4, bf16[2048,256]{1,0:T(8,128)(2,1)S(1)} %bitcast.21), custom_call_target="tpu_custom_call" | custom-call | flops 4294967296 | bytes 2097152 | tf_op jit(solution)/shard_map/pallas_call | solution.py:348
  98.8 0.1 collective-permute-start.15
  98.9 1.9 %collective-permute-done.15.received = f32[512,256]{1,0:T(8,128)S(1)} collective-permute-done((f32[512,256]{1,0:T(8,128)S(1)}, f32[512,256]{1,0:T(8,128)S(1)}, u32[]{:S(2)}, u32[]{:S(2)}) %collective-permute-start.15) | collective-permute-done | bytes 524320 | tf_op jit(solution)/shard_map/ppermute | solution.py:43
  100.8 0.2 shard_map.90
  101.0 18.8 %all_to_all.22.parts = bf16[16,32,256]{2,1,0:T(8,128)(2,1)S(1)} all-to-all(bf16[16,32,256]{2,1,0:T(8,128)(2,1)S(1)} %bitcast.20), channel_id=1, replica_groups={{0,16,32,48,64,80,96,112,128,144,160,176,192,208,224,240},{8,24,40,56,7..., dimensions={0} | all-to-all | bytes 524288 | tf_op jit(solution)/shard_map/all_to_all | solution.py:382
  119.8 0.4 shard_map.91
  120.3 8.8 %all_to_all.23 = bf16[8,32,128]{2,1,0:T(8,128)(2,1)S(1)} all-to-all(bf16[8,32,128]{2,1,0:T(8,128)(2,1)S(1)} %shard_map.91), channel_id=1, replica_groups=mesh['span'=32,'seq'=8] {'seq'}, dimensions={0} | all-to-all | bytes 131072 | tf_op jit(solution)/shard_map/all_to_all | solution.py:395
  129.0 0.6 copy_bitcast_fusion
  (14 shorter events, 0.1 us)
Async XLA Ops:
  0.6 35.2 %copy-start.1 = (bf16[256,1024]{1,0:T(8,128)(2,1)S(1)}, bf16[256,1024]{1,0:T(8,128)(2,1)}, u32[]{:S(2)}) copy-start(bf16[256,1024]{1,0:T(8,128)(2,1)} %tokens.1) | copy-start | bytes 1572868
  0.6 18.8 %collective-permute-start = (bf16[256,1024]{1,0:T(8,128)(2,1)}, bf16[256,1024]{1,0:T(8,128)(2,1)S(1)}, u32[]{:S(2)}, u32[]{:S(2)}) collective-permute-start(bf16[256,1024]{1,0:T(8,128)(2,1)} %tokens.1), channel_id=1, source_target_pairs={{0,1},{1,0},{2,3},{3,2},{4,5},{5,4},{6,7},{7,6},{8,9},{9,8},{10,11... | collective-permute-start | bytes 1572872 | tf_op jit(solution)/shard_map/ppermute | solution.py:43
  2.2 17.3 %collective-permute-start.1 = (bf16[256,1024]{1,0:T(8,128)(2,1)}, bf16[256,1024]{1,0:T(8,128)(2,1)S(1)}, u32[]{:S(2)}, u32[]{:S(2)}) collective-permute-start(bf16[256,1024]{1,0:T(8,128)(2,1)} %tokens.1), channel_id=1, source_target_pairs={{0,2},{1,3},{2,4},{3,5},{4,6},{5,7},{6,0},{7,1},{8,10},{9,11},{10,... | collective-permute-start | bytes 1572872 | tf_op jit(solution)/shard_map/ppermute | solution.py:43
  3.8 15.7 %collective-permute-start.2 = (bf16[256,1024]{1,0:T(8,128)(2,1)}, bf16[256,1024]{1,0:T(8,128)(2,1)S(1)}, u32[]{:S(2)}, u32[]{:S(2)}) collective-permute-start(bf16[256,1024]{1,0:T(8,128)(2,1)} %tokens.1), channel_id=1, source_target_pairs={{0,6},{1,7},{2,0},{3,1},{4,2},{5,3},{6,4},{7,5},{8,14},{9,15},{10,... | collective-permute-start | bytes 1572872 | tf_op jit(solution)/shard_map/ppermute | solution.py:43
  6.2 8.2 %collective-permute-start.3 = (bf16[32,384]{1,0:T(8,128)(2,1)S(1)}, bf16[32,384]{1,0:T(8,128)(2,1)S(1)}, u32[]{:S(2)}, u32[]{:S(2)}) collective-permute-start(bf16[32,384]{1,0:T(8,128)(2,1)S(1)} %pad_maximum_fusion.3), channel_id=1, source_target_pairs={{0,64},{8,72},{16,80},{24,88},{32,96},{40,104},{48,112},{56,120},{... | collective-permute-start | bytes 73736 | tf_op jit(solution)/shard_map/ppermute | solution.py:43
  14.4 5.1 %collective-permute-start.4 = (bf16[64,384]{1,0:T(8,128)(2,1)S(1)}, bf16[64,384]{1,0:T(8,128)(2,1)S(1)}, u32[]{:S(2)}, u32[]{:S(2)}) collective-permute-start(bf16[64,384]{1,0:T(8,128)(2,1)S(1)} %pad_maximum_fusion.2), channel_id=1, source_target_pairs={{0,32},{8,40},{16,48},{24,56},{32,0},{40,8},{48,16},{56,24},{64,96... | collective-permute-start | bytes 147464 | tf_op jit(solution)/shard_map/ppermute | solution.py:43
  19.5 8.5 %collective-permute-start.5 = (bf16[128,384]{1,0:T(8,128)(2,1)S(1)}, bf16[128,384]{1,0:T(8,128)(2,1)S(1)}, u32[]{:S(2)}, u32[]{:S(2)}) collective-permute-start(bf16[128,384]{1,0:T(8,128)(2,1)S(1)} %pad_maximum_fusion.1), channel_id=1, source_target_pairs={{0,16},{8,24},{16,0},{24,8},{32,48},{40,56},{48,32},{56,40},{64,80... | collective-permute-start | bytes 294920 | tf_op jit(solution)/shard_map/ppermute | solution.py:43
  20.5 7.5 %collective-permute-start.6 = (bf16[128,384]{1,0:T(8,128)(2,1)S(1)}, bf16[128,384]{1,0:T(8,128)(2,1)S(1)}, u32[]{:S(2)}, u32[]{:S(2)}) collective-permute-start(bf16[128,384]{1,0:T(8,128)(2,1)S(1)} %pad_maximum_fusion.1), channel_id=1, source_target_pairs={{0,128},{8,136},{16,144},{24,152},{32,160},{40,168},{48,176},{56,1... | collective-permute-start | bytes 294920 | tf_op jit(solution)/shard_map/ppermute | solution.py:43
  23.3 7.0 %collective-permute-start.7 = (bf16[128,384]{1,0:T(8,128)(2,1)S(1)}, bf16[128,384]{1,0:T(8,128)(2,1)S(1)}, u32[]{:S(2)}, u32[]{:S(2)}) collective-permute-start(bf16[128,384]{1,0:T(8,128)(2,1)S(1)} %pad_maximum_fusion.1), channel_id=1, source_target_pairs={{0,144},{8,152},{16,128},{24,136},{32,176},{40,184},{48,160},{56,1... | collective-permute-start | bytes 294920 | tf_op jit(solution)/shard_map/ppermute | solution.py:43
  24.6 9.0 %collective-permute-start.10 = (bf16[128,1024]{1,0:T(8,128)(2,1)S(1)}, bf16[128,1024]{1,0:T(8,128)(2,1)}, u32[]{:S(2)}, u32[]{:S(2)}) collective-permute-start(bf16[128,1024]{1,0:T(8,128)(2,1)S(1)} %slice.6), channel_id=1, source_target_pairs={{0,2},{1,3},{2,4},{3,5},{4,6},{5,7},{6,0},{7,1},{8,10},{9,11},{10,... | collective-permute-start | bytes 786440 | tf_op jit(solution)/shard_map/ppermute | solution.py:43
  25.0 9.2 %collective-permute-start.12 = (bf16[128,1024]{1,0:T(8,128)(2,1)S(1)}, bf16[128,1024]{1,0:T(8,128)(2,1)}, u32[]{:S(2)}, u32[]{:S(2)}) collective-permute-start(bf16[128,1024]{1,0:T(8,128)(2,1)S(1)} %slice.7), channel_id=1, source_target_pairs={{0,6},{1,7},{2,0},{3,1},{4,2},{5,3},{6,4},{7,5},{8,14},{9,15},{10,... | collective-permute-start | bytes 786440 | tf_op jit(solution)/shard_map/ppermute | solution.py:43
  30.3 18.0 %collective-permute-start.8 = (bf16[256,1024]{1,0:T(8,128)(2,1)S(1)}, bf16[256,1024]{1,0:T(8,128)(2,1)S(1)}, u32[]{:S(2)}, u32[]{:S(2)}) collective-permute-start(bf16[256,1024]{1,0:T(8,128)(2,1)S(1)} %collective-permute-done.peer), channel_id=1, source_target_pairs={{0,2},{1,3},{2,4},{3,5},{4,6},{5,7},{6,0},{7,1},{8,10},{9,11},{10,... | collective-permute-start | bytes 1572872 | tf_op jit(solution)/shard_map/ppermute | solution.py:43
  30.8 17.5 %collective-permute-start.9 = (bf16[256,1024]{1,0:T(8,128)(2,1)S(1)}, bf16[256,1024]{1,0:T(8,128)(2,1)S(1)}, u32[]{:S(2)}, u32[]{:S(2)}) collective-permute-start(bf16[256,1024]{1,0:T(8,128)(2,1)S(1)} %collective-permute-done.peer), channel_id=1, source_target_pairs={{0,6},{1,7},{2,0},{3,1},{4,2},{5,3},{6,4},{7,5},{8,14},{9,15},{10,... | collective-permute-start | bytes 1572872 | tf_op jit(solution)/shard_map/ppermute | solution.py:43
  33.6 2.2 %collective-permute-start.14 = (bf16[512,384]{1,0:T(8,128)(2,1)S(1)}, bf16[512,384]{1,0:T(8,128)(2,1)}, u32[]{:S(2)}, u32[]{:S(2)}) collective-permute-start(bf16[512,384]{1,0:T(8,128)(2,1)S(1)} %pad_maximum_fusion.mine), channel_id=1, source_target_pairs={{0,8},{8,0},{16,24},{24,16},{32,40},{40,32},{48,56},{56,48},{64,72... | collective-permute-start | bytes 1179656 | tf_op jit(solution)/shard_map/ppermute | solution.py:43
  33.6 9.6 %collective-permute-start.11 = (bf16[128,1024]{1,0:T(8,128)(2,1)}, bf16[128,1024]{1,0:T(8,128)(2,1)}, u32[]{:S(2)}, u32[]{:S(2)}) collective-permute-start(bf16[128,1024]{1,0:T(8,128)(2,1)} %collective-permute-done.10.up_far), channel_id=1, source_target_pairs={{0,1},{1,0},{2,3},{3,2},{4,5},{5,4},{6,7},{7,6},{8,9},{9,8},{10,11... | collective-permute-start | bytes 786440 | tf_op jit(solution)/shard_map/ppermute | solution.py:43
  34.2 14.1 %collective-permute-start.13 = (bf16[128,1024]{1,0:T(8,128)(2,1)}, bf16[128,1024]{1,0:T(8,128)(2,1)}, u32[]{:S(2)}, u32[]{:S(2)}) collective-permute-start(bf16[128,1024]{1,0:T(8,128)(2,1)} %collective-permute-done.12.down_far), channel_id=1, source_target_pairs={{0,1},{1,0},{2,3},{3,2},{4,5},{5,4},{6,7},{7,6},{8,9},{9,8},{10,11... | collective-permute-start | bytes 786440 | tf_op jit(solution)/shard_map/ppermute | solution.py:43
  48.3 23.1 %copy-start = (bf16[1024,1024]{1,0:T(8,128)(2,1)S(1)}, bf16[1024,1024]{1,0:T(8,128)(2,1)}, u32[]{:S(2)}) copy-start(bf16[1024,1024]{1,0:T(8,128)(2,1)} %w_out.1) | copy-start | bytes 6291460
  48.3 23.1 %copy-start.2 = (f32[1024]{0:T(1024)S(1)}, f32[1024]{0:T(1024)}, u32[]{:S(2)}) copy-start(f32[1024]{0:T(1024)} %param.11) | copy-start | bytes 12292
  48.3 23.1 %copy-start.3 = (f32[1024]{0:T(1024)S(1)}, f32[1024]{0:T(1024)}, u32[]{:S(2)}) copy-start(f32[1024]{0:T(1024)} %param.12) | copy-start | bytes 12292
  75.0 17.4 %copy-start.4 = (bf16[1024,1024]{1,0:T(8,128)(2,1)S(1)}, bf16[1024,1024]{1,0:T(8,128)(2,1)}, u32[]{:S(2)}) copy-start(bf16[1024,1024]{1,0:T(8,128)(2,1)} %queries.1) | copy-start | bytes 6291460
  98.8 2.0 %collective-permute-start.15 = (f32[512,256]{1,0:T(8,128)S(1)}, f32[512,256]{1,0:T(8,128)S(1)}, u32[]{:S(2)}, u32[]{:S(2)}) collective-permute-start(f32[512,256]{1,0:T(8,128)S(1)} %get-tuple-element.33), channel_id=1, source_target_pairs={{0,8},{8,0},{16,24},{24,16},{32,40},{40,32},{48,56},{56,48},{64,72... | collective-permute-start | bytes 1572872 | tf_op jit(solution)/shard_map/ppermute | solution.py:43
